TPU v7x, 32 devices: a whole 2x2x4 slice. The times are simulated.
32 devices in a mesh: dp: 4 (over y, x), vocab: 4 (over z), mp: 2 (over core).
Axes of the slice: x: 2, y: 2, z: 4, core: 2. Of those that a mesh axis runs over, the one named last changes fastest.
Arguments:
- hidden: bfloat16 [512, 3584], P('dp', 'mp'), may hold values from -20 to 20
- head_weight: bfloat16 [3584, 152064], P('mp', ('dp', 'vocab')), may hold values from -1 to 1
- teacher_logits: bfloat16 [512, 152064], P('mp', ('dp', 'vocab')), may hold values from -20 to 330
- response_start: int32 [2], replicated, may hold values from 0 to 128
Outputs:
- token_kl: float32 [512], P('mp')
- grad_hidden: float32 [512, 3584], P('dp', 'mp')
- grad_head: bfloat16 [3584, 152064], P('mp', ('dp', 'vocab'))
All inputs are finite; a program needn't handle non-finite values.
Results may differ from a plain program's by a relative error of at most 0.01.
Values may be sent and summed in bfloat16 or wider, within the bound.
No kernel may reach another device: no remote copies, remote signals or barrier semaphores. Data moves between devices by JAX's collectives and lax.ppermute only.
A program may use at most 128 MiB of HBM per device.

v0:
```python
import functools

import jax
import jax.numpy as jnp
from jax import lax
from jax.experimental import pallas as pl
from jax.experimental.pallas import tpu as pltpu
from jax.sharding import PartitionSpec as P

LEN = 256
F32 = jnp.float32
BF16 = jnp.bfloat16
MIB = 1 << 20
WEIGHT = 1 / 16
TILE = 528
COLUMNS = 256


def divide(total, parts, unit):
    return parts if total % (unit * parts) == 0 else 1


def tile_of(rows, want):
    for size in range(min(want, rows) // 16 * 16, 0, -16):
        if rows % size == 0:
            return size
    return rows


def params(mib):
    return pltpu.CompilerParams(
        dimension_semantics=("arbitrary",), vmem_limit_bytes=mib * MIB
    )


def cost(flops, moved, exps=0):
    return pl.CostEstimate(
        flops=int(flops * WEIGHT),
        bytes_accessed=int(moved * WEIGHT),
        transcendentals=int(exps * WEIGHT),
    )


def whole(shape):
    return pl.BlockSpec(shape, lambda i: (0,) * len(shape))


def fold(op, x, sub):
    if sub == 1:
        return (jnp.max if op is jnp.maximum else jnp.sum)(x, axis=0, keepdims=True)
    x = x.reshape(x.shape[0] // sub, sub, x.shape[1])
    while x.shape[0] > 1:
        half = x.shape[0] // 2
        rest = x[2 * half :]
        x = op(x[:half], x[half : 2 * half])
        if rest.shape[0]:
            x = jnp.concatenate([x, rest], axis=0)
    return x[0]


def spread(op, x, row, sub):
    if sub == 1:
        return op(x, row)
    rows, width = x.shape
    return op(x.reshape(rows // sub, sub, width), row[None]).reshape(rows, width)


def add_totals(parts, teacher_refs, state_ref, sub):
    student = parts[0][...]
    for part in parts[1:]:
        student = student + part[...]
    target = jnp.concatenate([ref[...] for ref in teacher_refs], axis=1).astype(F32)
    old = [state_ref[sub * r : sub * (r + 1)] for r in range(5)]
    top_s = jnp.maximum(old[0], fold(jnp.maximum, student, sub))
    top_t = jnp.maximum(old[1], fold(jnp.maximum, target, sub))
    exp_s = jnp.exp(spread(jnp.subtract, student, top_s, sub))
    exp_t = jnp.exp(spread(jnp.subtract, target, top_t, sub))
    scale_s = jnp.exp(old[0] - top_s)
    scale_t = jnp.exp(old[1] - top_t)
    new = [
        top_s,
        top_t,
        old[2] * scale_s + fold(jnp.add, exp_s, sub),
        old[3] * scale_t + fold(jnp.add, exp_t, sub),
        old[4] * scale_t + fold(jnp.add, exp_t * (target - student), sub),
    ]
    for r, value in enumerate(new):
        state_ref[sub * r : sub * (r + 1)] = value


def merge_classes(state_ref, sub):
    rows = [state_ref[sub * r : sub * (r + 1)] for r in range(5)]
    top_s = jnp.max(rows[0], axis=0, keepdims=True)
    top_t = jnp.max(rows[1], axis=0, keepdims=True)
    scale_s = jnp.exp(rows[0] - top_s)
    scale_t = jnp.exp(rows[1] - top_t)
    return [
        top_s,
        top_t,
        jnp.sum(rows[2] * scale_s, axis=0, keepdims=True),
        jnp.sum(rows[3] * scale_t, axis=0, keepdims=True),
        jnp.sum(rows[4] * scale_t, axis=0, keepdims=True),
    ]


def start_totals(sub, width):
    return jnp.concatenate(
        [jnp.full((2 * sub, width), -jnp.inf, F32), jnp.zeros((3 * sub, width), F32)]
    )


def totals_body(count, waves, sub, last, *refs):
    parts, teacher_refs = refs[:count], refs[count : count + waves]
    before_ref, out_ref, state_ref = refs[count + waves :]
    step = pl.program_id(0)

    @pl.when(step == 0)
    def _():
        state_ref[...] = before_ref[...]

    add_totals(parts, teacher_refs, state_ref, sub)

    @pl.when(step == pl.num_programs(0) - 1)
    def _():
        if last:
            out_ref[...] = jnp.zeros(out_ref.shape, F32)
            for r, value in enumerate(merge_classes(state_ref, sub)):
                out_ref[r : r + 1] = value
        else:
            out_ref[...] = state_ref[...]


def totals_chunk(parts, teachers, first, before, last):
    rows, width = parts[0].shape
    total = teachers[0].shape[0]
    sub = before.shape[0] // 5
    tile = tile_of(rows, TILE)
    out = (8 if last else 5 * sub, width)
    return pl.pallas_call(
        functools.partial(totals_body, len(parts), len(teachers), sub, last),
        grid=(rows // tile,),
        in_specs=chunk_specs([*parts, *teachers], tile, first, total) + [whole(before.shape)],
        out_specs=whole(out),
        out_shape=jax.ShapeDtypeStruct(out, F32),
        scratch_shapes=[pltpu.VMEM((5 * sub, width), F32)],
        compiler_params=params(12),
        cost_estimate=cost(
            12 * rows * width, (4 * len(parts) + 2) * rows * width, 2 * rows * width
        ),
        name="totals_chunk",
    )(*parts, *teachers, before)


def student_body(owners, places, *refs):
    refs = list(refs)
    if places is not None:
        own_ref = refs.pop(0)
        piece_refs = [refs.pop(0) for _ in places]
        turned_ref, ordered_ref = refs.pop(), refs.pop()

        for own in range(owners):

            @pl.when((pl.program_id(0) == 0) & (own_ref[0] == own))
            def _():
                for (a, at), ref in zip(places, piece_refs):
                    start = (own ^ a) * (ordered_ref.shape[0] // owners) + at
                    ordered_ref[start : start + ref.shape[0]] = ref[...]

        @pl.when(pl.program_id(0) == 0)
        def _():
            turned_ref[...] = ordered_ref[...].T

    else:
        turned_ref = refs.pop(0)
    head_ref, *out_refs = refs
    width = out_refs[0].shape[1]
    full = jnp.dot(head_ref[...], turned_ref[...], preferred_element_type=F32)
    for k, out_ref in enumerate(out_refs):
        out_ref[...] = full[:, k * width : (k + 1) * width]


def student_chunk(states, head_t, first, rows, owners, tokens):
    depth = head_t.shape[1]
    width = tokens // owners
    tile = tile_of(rows, TILE)
    base = first // tile
    outs = [pl.BlockSpec((tile, width), lambda i: (i, 0))] * owners
    shapes = [jax.ShapeDtypeStruct((rows, width), F32)] * owners
    places = None
    if isinstance(states, tuple):
        places = tuple((a, at) for _, a, at in states[1])
        args = [states[0]] + [x for x, _, _ in states[1]]
        specs = [pl.BlockSpec(memory_space=pltpu.SMEM)] + [whole(x.shape) for x in args[1:]]
        outs = outs + [whole((tokens, depth)), whole((depth, tokens))]
        shapes = shapes + [
            jax.ShapeDtypeStruct((tokens, depth), BF16),
            jax.ShapeDtypeStruct((depth, tokens), BF16),
        ]
    else:
        args, specs = [states], [whole((depth, tokens))]
    return pl.pallas_call(
        functools.partial(student_body, owners, places),
        grid=(rows // tile,),
        in_specs=specs + [pl.BlockSpec((tile, depth), lambda i: (i + base, 0))],
        out_specs=outs,
        out_shape=shapes,
        compiler_params=params(28),
        cost_estimate=cost(
            2 * rows * tokens * depth, 2 * rows * depth + 2 * tokens * depth + 4 * rows * tokens
        ),
        name="student_chunk",
    )(*args, head_t)


def merge(refs, shifts, width):
    rows = []
    for ref, shift in zip(refs, shifts):
        x = ref[...]
        if shift:
            cut = [x[:, at : at + width] for at in range(0, x.shape[1], width)]
            x = jnp.concatenate([cut[w ^ shift] for w in range(len(cut))], axis=1)
        rows.append(x)
    top_s = functools.reduce(jnp.maximum, [x[0:1] for x in rows])
    top_t = functools.reduce(jnp.maximum, [x[1:2] for x in rows])
    terms = []
    for x in rows:
        scale_s = jnp.exp(x[0:1] - top_s)
        scale_t = jnp.exp(x[1:2] - top_t)
        terms.append([x[2:3] * scale_s, x[3:4] * scale_t, x[4:5] * scale_t])
    while len(terms) > 1:
        terms = [
            [a + b for a, b in zip(left, right)] for left, right in zip(terms[::2], terms[1::2])
        ]
    return [top_s, top_t] + terms[0]


def merge_body(shifts, width, *refs):
    *in_refs, out_ref = refs
    out_ref[...] = jnp.zeros(out_ref.shape, F32)
    for row, value in enumerate(merge(in_refs, shifts, width)):
        out_ref[row : row + 1] = value


def finish_body(shifts, width, *refs):
    *in_refs, mask_ref, coef_ref, kl_ref = refs
    top_s, top_t, sum_s, sum_t, cross = merge(in_refs, shifts, width)
    mask = mask_ref[...]
    coef_ref[...] = jnp.zeros(coef_ref.shape, F32)
    coef_ref[0:1] = top_s
    coef_ref[1:2] = top_t
    coef_ref[2:3] = mask / sum_s
    coef_ref[3:4] = mask / sum_t
    kl_ref[...] = mask * (cross / sum_t - top_t - jnp.log(sum_t) + top_s + jnp.log(sum_s))


def merge_call(values, shifts, width, mask=None):
    shape = values[0].shape
    out = jax.ShapeDtypeStruct(shape, F32)
    small = pltpu.CompilerParams(vmem_limit_bytes=2 * MIB)
    guess = cost(1 << 20, 1 << 16)
    if mask is None:
        return pl.pallas_call(
            functools.partial(merge_body, shifts, width),
            out_shape=out,
            compiler_params=small,
            cost_estimate=guess,
            name="merge_totals",
        )(*values)
    kl = jax.ShapeDtypeStruct((1, shape[1]), F32)
    return pl.pallas_call(
        functools.partial(finish_body, shifts, width),
        out_shape=(out, kl),
        compiler_params=small,
        cost_estimate=guess,
        name="finish_totals",
    )(*values, mask)


def grads_body(count, *refs):
    parts, teacher_refs = refs[:count], refs[count:-2]
    coef_ref, out_ref = refs[-2:]
    width = out_ref.shape[1] // len(teacher_refs)
    for w, teacher_ref in enumerate(teacher_refs):
        lanes = slice(w * width, (w + 1) * width)
        coef = coef_ref[:, lanes]
        student = parts[0][:, lanes]
        for part in parts[1:]:
            student = student + part[:, lanes]
        target = teacher_ref[...].astype(F32)
        out_ref[:, lanes] = (
            jnp.exp(student - coef[0:1]) * coef[2:3] - jnp.exp(target - coef[1:2]) * coef[3:4]
        ).astype(BF16)


def grads_chunk(parts, teachers, coef, first):
    rows, width = parts[0].shape
    tile = tile_of(rows, 2 * TILE)
    return pl.pallas_call(
        functools.partial(grads_body, len(parts)),
        grid=(rows // tile,),
        in_specs=chunk_specs([*parts, *teachers], tile, first, teachers[0].shape[0])
        + [whole(coef.shape)],
        out_specs=pl.BlockSpec((tile, width), lambda i: (i, 0)),
        out_shape=jax.ShapeDtypeStruct((rows, width), BF16),
        compiler_params=params(20),
        cost_estimate=cost(
            8 * rows * width, (4 * len(parts) + 4) * rows * width, 2 * rows * width
        ),
        name="logit_grads_chunk",
    )(*parts, *teachers, coef)


def chunk_specs(arrays, tile, first, total):
    return [
        pl.BlockSpec(
            (tile, x.shape[1]),
            functools.partial(lambda base, i: (i + base, 0), first // tile if x.shape[0] == total else 0),
        )
        for x in arrays
    ]


def hidden_body(count, owners, has_acc, emit, last, *refs):
    grads_refs, head_ref, *rest = (refs[:count], *refs[count:])
    before_ref = rest.pop(0) if has_acc else None
    if emit:
        turned_ref = rest.pop(0)

        @pl.when(pl.program_id(0) == 0)
        def _():
            for k, ref in enumerate(grads_refs):
                width = ref.shape[1]
                turned_ref[k * width : (k + 1) * width] = ref[...].T

    else:
        turned_ref = grads_refs[0]
    total = jnp.dot(turned_ref[...], head_ref[...], preferred_element_type=F32)
    if has_acc:
        total = total + before_ref[...]
    if not last:
        rest[0][...] = total
        return
    shard = total.shape[0] // (owners * len(rest))
    for k in range(owners):
        for w, out_ref in enumerate(rest):
            at = (k * len(rest) + w) * shard
            out_ref[k * shard : (k + 1) * shard] = total[at : at + shard].astype(BF16)


def hidden_chunk(grads, head_t, first, rows, owners, waves, tile, tiles, emit, before, last):
    width = COLUMNS if head_t.shape[1] % COLUMNS == 0 else 128
    base = first // rows
    tokens = sum(g.shape[1] for g in grads) if emit else grads[0].shape[0]
    block = pl.BlockSpec((tokens, width), lambda i: (0, i))
    size = tiles * width
    pieces = waves if last else 1
    out_specs = [pl.BlockSpec((tokens // pieces, width), lambda i: (0, i))] * pieces
    out_shape = [jax.ShapeDtypeStruct((tokens // pieces, size), BF16 if last else F32)] * pieces
    if emit:
        out_specs = [whole((tokens, rows))] + out_specs
        out_shape = [jax.ShapeDtypeStruct((tokens, rows), BF16)] + out_shape
    has_acc = before is not None
    return pl.pallas_call(
        functools.partial(hidden_body, len(grads), owners, has_acc, emit, last),
        grid=(tiles,),
        in_specs=[whole(g.shape) for g in grads]
        + [pl.BlockSpec((rows, width), lambda i: (base, i + tile))]
        + [block] * has_acc,
        out_specs=out_specs,
        out_shape=out_shape,
        compiler_params=params(32),
        cost_estimate=cost(2 * rows * tokens * size, 2 * rows * (size + tokens)),
        name="grad_hidden_chunk",
    )(*grads, head_t, *([before] if has_acc else []))


def head_body(count, hidden_ref, *refs):
    grads = jnp.concatenate([ref[...] for ref in refs[:count]], axis=1)
    out_ref, flag_ref = refs[-2:]

    @pl.when(pl.program_id(0) == 0)
    def _():
        flag_ref[...] = jnp.zeros(flag_ref.shape, F32)

    for at in range(0, out_ref.shape[1], COLUMNS):
        lanes = slice(at, min(at + COLUMNS, out_ref.shape[1]))
        out_ref[:, lanes] = jnp.dot(
            grads, hidden_ref[:, lanes], preferred_element_type=F32
        ).astype(BF16)


def head_chunk(hidden, grads, first, total, before):
    rows = grads[0].shape[0]
    tokens, depth = hidden.shape
    tile = tile_of(rows, TILE)
    base = first // tile
    specs = [whole(hidden.shape)] + chunk_specs(grads, tile, first, total)
    extra, aliases = [], {}
    if before is not None:
        specs.append(pl.BlockSpec(memory_space=pl.ANY))
        extra, aliases = [before], {1 + len(grads): 0}
    return pl.pallas_call(
        functools.partial(head_body, len(grads)),
        grid=(rows // tile,),
        in_specs=specs,
        out_specs=[pl.BlockSpec((tile, depth), lambda i: (i + base, 0)), whole((8, 128))],
        out_shape=[
            jax.ShapeDtypeStruct((total, depth), BF16),
            jax.ShapeDtypeStruct((8, 128), F32),
        ],
        input_output_aliases=aliases,
        compiler_params=params(24),
        cost_estimate=cost(
            2 * rows * tokens * depth, 2 * rows * depth + 2 * tokens * depth + 2 * rows * tokens
        ),
        name="grad_head_chunk",
    )(hidden, *grads, *extra)


def swap(x, axis, k):
    n = lax.axis_size(axis)
    return lax.ppermute(x, axis, [(i, i ^ k) for i in range(n)])


def merge_over(totals, axis, waves, mask=None):
    n = lax.axis_size(axis)
    width = totals.shape[1] // waves
    step = 1
    while step < n:
        span = min(4, n // step)
        values = [totals] + [swap(totals, axis, k * step) for k in range(1, span)]
        shifts = tuple(k * step % waves if axis == "dp" else 0 for k in range(span))
        step *= span
        totals = merge_call(values, shifts, width, mask if step == n else None)
    return totals


def rows_at(x, index, size):
    return lax.dynamic_slice_in_dim(x, index * size, size)


class Reduction:
    def __init__(self, partial, shard, own):
        self.partial, self.shard, self.own = partial, shard, own
        self.owners = lax.axis_size("mp")
        self.waves = lax.axis_size("dp") // self.owners

    def over_inner(self, flag):
        total = self.partial[0].astype(F32)
        for w in range(1, self.waves):
            total += tie(swap(self.partial[w], "dp", w), flag).astype(F32)
        self.total = total
        return total

    def over_outer(self, flag):
        total = rows_at(self.total, self.own, self.shard)
        for a in range(1, self.owners):
            sent = rows_at(self.total, self.own ^ a, self.shard).astype(BF16)
            total += tie(swap(sent, "dp", a * self.waves), flag).astype(F32)
        self.total = total
        return total

    def scatter_vocab(self, flag):
        n = lax.axis_size("vocab")
        if n > 4 or self.shard % (8 * n):
            self.block = lax.psum(self.total, "vocab")
            return self.block
        mine, size = lax.axis_index("vocab"), self.shard // n
        block = rows_at(self.total, mine, size)
        for c in range(1, n):
            sent = rows_at(self.total, mine ^ c, size).astype(BF16)
            block += tie(swap(sent, "vocab", c), flag).astype(F32)
        self.block = block.astype(BF16)
        return self.block

    def gather_vocab(self, flag):
        if self.block.shape[0] == self.shard:
            return self.block
        n = lax.axis_size("vocab")
        mine, size = lax.axis_index("vocab"), self.shard // n
        result = jnp.zeros(self.total.shape, F32)
        for c in range(n):
            piece = tie(swap(self.block, "vocab", c), flag) if c else self.block
            result = lax.dynamic_update_slice_in_dim(
                result, piece.astype(F32), (mine ^ c) * size, 0
            )
        return result


def tie(x, *after):
    return lax.optimization_barrier((x, *after))[0]


def per_device(hidden, head_weight, teacher_logits, response_start):
    n_dp, n_mp = lax.axis_size("dp"), lax.axis_size("mp")
    waves = n_dp // n_mp
    shard, depth = hidden.shape
    own_rows, columns = teacher_logits.shape
    mp = lax.axis_index("mp")
    dp = lax.axis_index("dp")
    outer, inner = dp // waves, dp % waves
    own = outer ^ mp
    head_t = head_weight.T
    teacher_t = teacher_logits.T

    def in_wave(x, w):
        return lax.dynamic_slice_in_dim(x, (inner ^ w) * shard, shard, axis=1)

    positions = mp * own_rows + jnp.concatenate(
        [(inner ^ w) * shard + jnp.arange(shard, dtype=jnp.int32) for w in range(waves)]
    )
    sequence = positions // LEN
    seq_ids = jnp.arange(response_start.shape[0], dtype=jnp.int32)
    starts = jnp.sum(
        jnp.where(sequence[:, None] == seq_ids[None, :], response_start[None, :], 0), axis=1
    )
    mask = (positions % LEN >= starts).astype(F32)[None, :]
    teachers = [in_wave(teacher_t, w) for w in range(waves)]

    near = {k: swap(hidden, "dp", k) for k in range(1, n_dp) if k < waves or k % waves == 0}
    pieces = [(tie(hidden, *teachers), 0, 0)]
    for k in range(1, n_dp):
        a, w = k // waves, k % waves
        if k in near:
            pieces.append((near[k], a, w * shard))
        else:
            half = shard // 2
            pieces.append((swap(near[a * waves][:half], "dp", w), a, w * shard))
            pieces.append((swap(near[w][half:], "dp", a * waves), a, w * shard + half))

    chunks = divide(columns, 3, 16)
    rows = columns // chunks
    firsts = [c * rows for c in range(chunks)]
    sub = 8 if columns % 8 == 0 else 1

    def exchanged(outs):
        return [outs[0]] + [swap(outs[k], "mp", k) for k in range(1, n_mp)]

    parts = []
    states = (own.astype(jnp.int32).reshape(1), pieces)
    for first in firsts:
        outs = student_chunk(states, head_t, first, rows, n_mp, n_dp * shard)
        if len(outs) > n_mp:
            ordered, states = outs[n_mp:]
        parts.append(exchanged(outs[:n_mp]))
    totals = start_totals(sub, own_rows)
    for c, first in enumerate(firsts):
        totals = totals_chunk(parts[c], teachers, first, totals, c == chunks - 1)
    totals = merge_over(totals, "dp", waves)
    coef, kl = merge_over(totals, "vocab", waves, mask)
    token_kl = jnp.zeros((1, own_rows), F32)
    for w in range(waves):
        token_kl = lax.dynamic_update_slice_in_dim(
            token_kl, kl[:, w * shard : (w + 1) * shard], (inner ^ w) * shard, 1
        )

    all_grads = []
    for c, first in enumerate(firsts):
        all_grads.append(exchanged([grads_chunk(parts[c], teachers, coef, first)] * n_mp))

    tiles = depth // (COLUMNS if depth % COLUMNS == 0 else 128)
    split = (tiles + 1) // 2
    reductions = []
    turned = [None] * chunks
    for at, count in ((0, split), (split, tiles - split)):
        acc = None
        for c, first in enumerate(firsts):
            inputs = all_grads[c] if at == 0 else [turned[c]]
            outs = hidden_chunk(
                inputs, head_t, first, rows, n_mp, waves, at, count, at == 0, acc, c == chunks - 1
            )
            if at == 0:
                turned[c], *outs = outs
            acc = outs[0]
        turned[0] = tie(turned[0], *outs)
        reductions.append(Reduction(outs, shard, own))
    results = [reductions[0].over_inner(reductions[-1].partial[0])]
    plan = [
        lambda flag: [reductions[0].over_outer(flag)]
        + [r.over_inner(flag) for r in reductions[1:]],
        lambda flag: [reductions[0].scatter_vocab(flag)]
        + [r.over_outer(flag) for r in reductions[1:]],
        lambda flag: [reductions[0].gather_vocab(flag)]
        + [r.scatter_vocab(flag) for r in reductions[1:]],
    ]
    grad_head = None
    for c, first in enumerate(firsts):
        grad_head, flag = head_chunk(
            tie(ordered, *results), all_grads[c], first, columns, grad_head
        )
        if plan:
            results = plan.pop(0)(flag)
    while plan:
        results = plan.pop(0)(flag)
    grad_hidden = jnp.concatenate(
        [results[0]] + [r.gather_vocab(flag) for r in reductions[1:]], axis=1
    )
    return (token_kl.reshape(own_rows), grad_hidden, grad_head.T)


def solution(mesh):
    return jax.shard_map(
        per_device,
        mesh=mesh,
        in_specs=(P("dp", "mp"), P("mp", ("dp", "vocab")), P("mp", ("dp", "vocab")), P()),
        out_specs=(P("mp"), P("dp", "mp"), P("mp", ("dp", "vocab"))),
        check_vma=False,
    )
```

profile of v0, /device:TPU:0, one launch (start us, length us, event | category | flops | bytes accessed | tf_op | source)
XLA Modules:
  0.0 208.7 jit_solution(9764784190394222651)
XLA Ops:
  5.2 9.2 %collective-permute-done.1.refs_3_ = bf16[128,1792]{1,0:T(8,128)(2,1)S(1)} collective-permute-done((bf16[128,1792]{1,0:T(8,128)(2,1)}, bf16[128,1792]{1,0:T(8,128)(2,1)S(1)}, u32[]{:S(2)}, u32[]{:S(2)}) %collective-permute-start.1) | collective-permute-done | bytes 458784 | tf_op jit(solution)/shard_map/ppermute | solution.py:422
  19.0 3.6 %dynamic-slice_bitcast_fusion = (bf16[9504,128]{1,0:T(8,128)(2,1)S(1)}, bf16[9504,128]{1,0:T(8,128)(2,1)}) fusion(bf16[256,9504]{0,1:T(8,128)(2,1)} %param.6, s32[]{:T(128)S(6)} %select_n.80, s32[]{:T(128)S(6)} %select_n.79), kind=kLoop, calls=%fused_computation | loop fusion | bytes 9732104 | tf_op jit(solution)/shard_map/dynamic_slice | solution.py:507
  25.0 11.3 %student_chunk.3 = (f32[3168,256]{1,0:T(8,128)S(1)}, f32[3168,256]{1,0:T(8,128)}, bf16[512,1792]{1,0:T(8,128)(2,1)S(1)}, bf16[1792,512]{1,0:T(8,128)(2,1)S(1)}) custom-call(s32[1]{0:T(128)} %bitcast.refs_0_, bf16[128,1792]{1,0:T(8,128)(2,1)S(1)} %copy-done.27, bf16[128,1792]{1,0:T(8,128)(2,1)S(1)} %collective-permute-done.refs_2_, ...), custom_call_target="tpu_custom_call" | custom-call | flops 363331584 | bytes 1229824 | tf_op jit(solution)/shard_map/student_chunk/pallas_call | solution.py:201
  38.0 11.3 %student_chunk.5 = (f32[3168,256]{1,0:T(8,128)S(1)}, f32[3168,256]{1,0:T(8,128)}) custom-call(bf16[1792,512]{1,0:T(8,128)(2,1)S(1)} %get-tuple-element.50.refs_0_, bf16[9504,1792]{1,0:T(8,128)(2,1)} %bitcast.17), custom_call_target="tpu_custom_call" | custom-call | flops 363331584 | bytes 1229824 | tf_op jit(solution)/shard_map/student_chunk/pallas_call | solution.py:201
  51.0 10.6 %student_chunk.4 = (f32[3168,256]{1,0:T(8,128)S(1)}, f32[3168,256]{1,0:T(8,128)}) custom-call(bf16[1792,512]{1,0:T(8,128)(2,1)S(1)} %get-tuple-element.50.refs_0_, bf16[9504,1792]{1,0:T(8,128)(2,1)} %bitcast.18), custom_call_target="tpu_custom_call" | custom-call | flops 363331584 | bytes 1229824 | tf_op jit(solution)/shard_map/student_chunk/pallas_call | solution.py:201
  67.5 5.4 %totals_chunk.3.refs_4_ = f32[40,256]{1,0:T(8,128)S(1)} custom-call(f32[3168,256]{1,0:T(8,128)S(1)} %copy-done.11, f32[3168,256]{1,0:T(8,128)} %collective-permute-done.6.refs_1_, bf16[9504,128]{1,0:T(8,128)(2,1)S(1)} %copy-done, bf16[9504,128]{1,0:T(8,128)(2,1)S(1)} %get-tuple-element.99.refs_3_, f32[40,256]{1,0:T(8,128)S(1)} %copy-done.28), custom_call_target="tpu_custom_call" | custom-call | flops 608256 | bytes 506880 | tf_op jit(solution)/shard_map/totals_chunk/pallas_call | solution.py:139
  73.0 5.0 %totals_chunk.4.refs_4_ = f32[40,256]{1,0:T(8,128)S(1)} custom-call(f32[3168,256]{1,0:T(8,128)S(1)} %copy-done.16, f32[3168,256]{1,0:T(8,128)} %collective-permute-done.5.refs_1_, bf16[9504,128]{1,0:T(8,128)(2,1)S(1)} %copy-done.1, bf16[9504,128]{1,0:T(8,128)(2,1)S(1)} %get-tuple-element.99.refs_3_, f32[40,256]{1,0:T(8,128)S(1)} %totals_chunk.3.refs_4_), custom_call_target="tpu_custom_call" | custom-call | flops 608256 | bytes 506880 | tf_op jit(solution)/shard_map/totals_chunk/pallas_call | solution.py:139
  78.0 5.1 %totals_chunk.5.refs_0_ = f32[8,256]{1,0:T(8,128)S(1)} custom-call(f32[3168,256]{1,0:T(8,128)S(1)} %copy-done.14, f32[3168,256]{1,0:T(8,128)} %collective-permute-done.4.refs_1_, bf16[9504,128]{1,0:T(8,128)(2,1)S(1)} %copy-done.1, bf16[9504,128]{1,0:T(8,128)(2,1)S(1)} %get-tuple-element.99.refs_3_, f32[40,256]{1,0:T(8,128)S(1)} %totals_chunk.4.refs_4_), custom_call_target="tpu_custom_call" | custom-call | flops 608256 | bytes 506880 | tf_op jit(solution)/shard_map/totals_chunk/pallas_call | solution.py:139
  96.0 3.5 %collective-permute-done.12.refs_3_ = f32[8,256]{1,0:T(8,128)S(1)} collective-permute-done((f32[8,256]{1,0:T(8,128)S(1)}, f32[8,256]{1,0:T(8,128)S(1)}, u32[]{:S(2)}, u32[]{:S(2)}) %collective-permute-start.12) | collective-permute-done | bytes 8224 | tf_op jit(solution)/shard_map/ppermute | solution.py:422
  99.5 3.4 %logit_grads_chunk.5.refs_0_ = bf16[3168,256]{1,0:T(8,128)(2,1)S(1)} custom-call(f32[3168,256]{1,0:T(8,128)S(1)} %copy-done.12, f32[3168,256]{1,0:T(8,128)} %collective-permute-done.6.refs_1_, bf16[9504,128]{1,0:T(8,128)(2,1)S(1)} %copy-done.1, bf16[9504,128]{1,0:T(8,128)(2,1)S(1)} %get-tuple-element.99.refs_3_, f32[8,256]{1,0:T(8,128)S(1)} %get-tuple-element.58.refs_4_), custom_call_target="tpu_custom_call" | custom-call | flops 405504 | bytes 608256 | tf_op jit(solution)/shard_map/logit_grads_chunk/pallas_call | solution.py:298
  103.0 3.9 %logit_grads_chunk.4.refs_0_ = bf16[3168,256]{1,0:T(8,128)(2,1)S(1)} custom-call(f32[3168,256]{1,0:T(8,128)S(1)} %copy-done.16, f32[3168,256]{1,0:T(8,128)} %collective-permute-done.5.refs_1_, bf16[9504,128]{1,0:T(8,128)(2,1)S(1)} %copy-done.1, bf16[9504,128]{1,0:T(8,128)(2,1)S(1)} %get-tuple-element.99.refs_3_, f32[8,256]{1,0:T(8,128)S(1)} %get-tuple-element.58.refs_4_), custom_call_target="tpu_custom_call" | custom-call | flops 405504 | bytes 608256 | tf_op jit(solution)/shard_map/logit_grads_chunk/pallas_call | solution.py:298
  107.0 3.9 %logit_grads_chunk.3.refs_0_ = bf16[3168,256]{1,0:T(8,128)(2,1)S(1)} custom-call(f32[3168,256]{1,0:T(8,128)S(1)} %copy-done.14, f32[3168,256]{1,0:T(8,128)} %collective-permute-done.4.refs_1_, bf16[9504,128]{1,0:T(8,128)(2,1)S(1)} %copy-done.1, bf16[9504,128]{1,0:T(8,128)(2,1)S(1)} %get-tuple-element.99.refs_3_, f32[8,256]{1,0:T(8,128)S(1)} %get-tuple-element.58.refs_4_), custom_call_target="tpu_custom_call" | custom-call | flops 405504 | bytes 608256 | tf_op jit(solution)/shard_map/logit_grads_chunk/pallas_call | solution.py:298
  111.0 8.1 %grad_hidden_chunk.6 = (bf16[512,3168]{1,0:T(8,128)(2,1)S(1)}, f32[512,1024]{1,0:T(8,128)S(1)}) custom-call(bf16[3168,256]{1,0:T(8,128)(2,1)S(1)} %logit_grads_chunk.5.refs_0_, bf16[3168,256]{1,0:T(8,128)(2,1)S(1)} %collective-permute-done.15.refs_1_, bf16[9504,1792]{1,0:T(8,128)(2,1)} %bitcast.19), custom_call_target="tpu_custom_call" | custom-call | flops 207618048 | bytes 608256 | tf_op jit(solution)/shard_map/grad_hidden_chunk/pallas_call | solution.py:363
  120.8 7.7 %grad_hidden_chunk.7 = (bf16[512,3168]{1,0:T(8,128)(2,1)S(1)}, f32[512,1024]{1,0:T(8,128)S(1)}) custom-call(bf16[3168,256]{1,0:T(8,128)(2,1)S(1)} %logit_grads_chunk.4.refs_0_, bf16[3168,256]{1,0:T(8,128)(2,1)S(1)} %collective-permute-done.14.refs_1_, bf16[9504,1792]{1,0:T(8,128)(2,1)} %bitcast.20, f32[512,1024]{1,0:T(8,128)S(1)} %get-tuple-element.59.refs_3_), custom_call_target="tpu_custom_call" | custom-call | flops 207618048 | bytes 608256 | tf_op jit(solution)/shard_map/grad_hidden_chunk/pallas_call | solution.py:363
  130.3 7.1 %grad_hidden_chunk.8 = (bf16[512,3168]{1,0:T(8,128)(2,1)S(1)}, bf16[256,1024]{1,0:T(8,128)(2,1)S(1)}, bf16[256,1024]{1,0:T(8,128)(2,1)S(1)}) custom-call(bf16[3168,256]{1,0:T(8,128)(2,1)S(1)} %logit_grads_chunk.3.refs_0_, bf16[3168,256]{1,0:T(8,128)(2,1)S(1)} %collective-permute-done.13.refs_1_, bf16[9504,1792]{1,0:T(8,128)(2,1)} %bitcast.21, ...), custom_call_target="tpu_custom_call" | custom-call | flops 207618048 | bytes 608256 | tf_op jit(solution)/shard_map/grad_hidden_chunk/pallas_call | solution.py:363
  142.7 5.2 %grad_hidden_chunk.9.refs_2_ = f32[512,768]{1,0:T(8,128)S(1)} custom-call(bf16[512,3168]{1,0:T(8,128)(2,1)S(1)} %copy-done.22, bf16[9504,1792]{1,0:T(8,128)(2,1)} %bitcast.22), custom_call_target="tpu_custom_call" | custom-call | flops 155713536 | bytes 506880 | tf_op jit(solution)/shard_map/grad_hidden_chunk/pallas_call | solution.py:363
  147.9 5.2 %grad_hidden_chunk.10.refs_2_ = f32[512,768]{1,0:T(8,128)S(1)} custom-call(bf16[512,3168]{1,0:T(8,128)(2,1)S(1)} %copy-done.26, bf16[9504,1792]{1,0:T(8,128)(2,1)} %bitcast.23, f32[512,768]{1,0:T(8,128)S(1)} %grad_hidden_chunk.9.refs_2_), custom_call_target="tpu_custom_call" | custom-call | flops 155713536 | bytes 506880 | tf_op jit(solution)/shard_map/grad_hidden_chunk/pallas_call | solution.py:363
  153.1 5.2 %grad_hidden_chunk.11 = (bf16[256,768]{1,0:T(8,128)(2,1)S(1)}, bf16[256,768]{1,0:T(8,128)(2,1)S(1)}) custom-call(bf16[512,3168]{1,0:T(8,128)(2,1)S(1)} %copy-done.24, bf16[9504,1792]{1,0:T(8,128)(2,1)} %bitcast.24, f32[512,768]{1,0:T(8,128)S(1)} %grad_hidden_chunk.10.refs_2_), custom_call_target="tpu_custom_call" | custom-call | flops 155713536 | bytes 506880 | tf_op jit(solution)/shard_map/grad_hidden_chunk/pallas_call | solution.py:363
  159.8 8.5 %grad_head_chunk.3 = (bf16[9504,1792]{1,0:T(8,128)(2,1)}, f32[8,128]{1,0:T(8,128)}) custom-call(bf16[512,1792]{1,0:T(8,128)(2,1)S(1)} %copy-done.3, bf16[3168,256]{1,0:T(8,128)(2,1)S(1)} %copy-done.9, bf16[3168,256]{1,0:T(8,128)(2,1)S(1)} %copy-done.20), custom_call_target="tpu_custom_call" | custom-call | flops 363331584 | bytes 1027072 | tf_op jit(solution)/shard_map/grad_head_chunk/pallas_call | solution.py:402
  170.9 3.6 %collective-permute-start.21 = (bf16[32,1024]{1,0:T(8,128)(2,1)S(1)}, bf16[32,1024]{1,0:T(8,128)(2,1)S(1)}, u32[]{:S(2)}, u32[]{:S(2)}) collective-permute-start(bf16[32,1024]{1,0:T(8,128)(2,1)S(1)} %get-tuple-element.102), channel_id=1, source_target_pairs={{0,6},{2,4},{4,2},{6,0},{1,7},{3,5},{5,3},{7,1},{8,14},{10,12},{12... | collective-permute-start | bytes 196616 | tf_op jit(solution)/shard_map/ppermute | solution.py:422
  174.6 8.5 %grad_head_chunk.4 = (bf16[9504,1792]{1,0:T(8,128)(2,1)}, f32[8,128]{1,0:T(8,128)}) custom-call(bf16[512,1792]{1,0:T(8,128)(2,1)S(1)} %copy-done.3, bf16[3168,256]{1,0:T(8,128)(2,1)S(1)} %copy-done.7, bf16[3168,256]{1,0:T(8,128)(2,1)S(1)} %copy-done.18, bf16[9504,1792]{1,0:T(8,128)(2,1)} %get-tuple-element.76.refs_2_), custom_call_target="tpu_custom_call", output_to_operand_aliasing={{0}: (3, {})} | custom-call | flops 363331584 | bytes 1027072 | tf_op jit(solution)/shard_map/grad_head_chunk/pallas_call | solution.py:402
  184.0 3.6 %collective-permute-start.28 = (bf16[32,768]{1,0:T(8,128)(2,1)S(1)}, bf16[32,768]{1,0:T(8,128)(2,1)S(1)}, u32[]{:S(2)}, u32[]{:S(2)}) collective-permute-start(bf16[32,768]{1,0:T(8,128)(2,1)S(1)} %get-tuple-element.105), channel_id=1, source_target_pairs={{0,6},{2,4},{4,2},{6,0},{1,7},{3,5},{5,3},{7,1},{8,14},{10,12},{12... | collective-permute-start | bytes 147464 | tf_op jit(solution)/shard_map/ppermute | solution.py:422
  187.7 8.5 %grad_head_chunk.5 = (bf16[9504,1792]{1,0:T(8,128)(2,1)}, f32[8,128]{1,0:T(8,128)}) custom-call(bf16[512,1792]{1,0:T(8,128)(2,1)S(1)} %copy-done.3, bf16[3168,256]{1,0:T(8,128)(2,1)S(1)} %copy-done.5, bf16[3168,256]{1,0:T(8,128)(2,1)S(1)} %collective-permute-done.13.refs_1_, ...), custom_call_target="tpu_custom_call", output_to_operand_aliasing={{0}: (3, {})} | custom-call | flops 363331584 | bytes 1027072 | tf_op jit(solution)/shard_map/grad_head_chunk/pallas_call | solution.py:402
  197.0 3.8 %collective-permute-start.29 = (bf16[32,768]{1,0:T(8,128)(2,1)S(1)}, bf16[32,768]{1,0:T(8,128)(2,1)S(1)}, u32[]{:S(2)}, u32[]{:S(2)}) collective-permute-start(bf16[32,768]{1,0:T(8,128)(2,1)S(1)} %get-tuple-element.98), channel_id=1, source_target_pairs={{0,2},{2,0},{4,6},{6,4},{1,3},{3,1},{5,7},{7,5},{8,10},{10,8},{12,... | collective-permute-start | bytes 147464 | tf_op jit(solution)/shard_map/ppermute | solution.py:422
  (152 shorter events, 56.3 us)
Async XLA Ops:
  0.6 13.8 %collective-permute-start.1 = (bf16[128,1792]{1,0:T(8,128)(2,1)}, bf16[128,1792]{1,0:T(8,128)(2,1)S(1)}, u32[]{:S(2)}, u32[]{:S(2)}) collective-permute-start(bf16[128,1792]{1,0:T(8,128)(2,1)} %refs_1_), channel_id=1, source_target_pairs={{0,16},{8,24},{16,0},{24,8},{1,17},{9,25},{17,1},{25,9},{2,18},{10... | collective-permute-start | bytes 1376264 | tf_op jit(solution)/shard_map/ppermute | solution.py:422
  3.7 13.1 %collective-permute-start = (bf16[128,1792]{1,0:T(8,128)(2,1)}, bf16[128,1792]{1,0:T(8,128)(2,1)S(1)}, u32[]{:S(2)}, u32[]{:S(2)}) collective-permute-start(bf16[128,1792]{1,0:T(8,128)(2,1)} %refs_1_), channel_id=1, source_target_pairs={{0,8},{8,0},{16,24},{24,16},{1,9},{9,1},{17,25},{25,17},{2,10},{10... | collective-permute-start | bytes 1376264 | tf_op jit(solution)/shard_map/ppermute | solution.py:422
  15.1 7.5 %collective-permute-start.2 = (bf16[64,1792]{1,0:T(8,128)(2,1)}, bf16[64,1792]{1,0:T(8,128)(2,1)}, u32[]{:S(2)}, u32[]{:S(2)}) collective-permute-start(bf16[64,1792]{1,0:T(8,128)(2,1)} %slice.16), channel_id=1, source_target_pairs={{0,8},{8,0},{16,24},{24,16},{1,9},{9,1},{17,25},{25,17},{2,10},{10... | collective-permute-start | bytes 688136 | tf_op jit(solution)/shard_map/ppermute | solution.py:422
  17.5 6.5 %collective-permute-start.3 = (bf16[64,1792]{1,0:T(8,128)(2,1)}, bf16[64,1792]{1,0:T(8,128)(2,1)}, u32[]{:S(2)}, u32[]{:S(2)}) collective-permute-start(bf16[64,1792]{1,0:T(8,128)(2,1)} %slice.17), channel_id=1, source_target_pairs={{0,16},{8,24},{16,0},{24,8},{1,17},{9,25},{17,1},{25,9},{2,18},{10... | collective-permute-start | bytes 688136 | tf_op jit(solution)/shard_map/ppermute | solution.py:422
  38.0 25.9 %collective-permute-start.6 = (f32[3168,256]{1,0:T(8,128)}, f32[3168,256]{1,0:T(8,128)}, u32[]{:S(2)}, u32[]{:S(2)}) collective-permute-start(f32[3168,256]{1,0:T(8,128)} %get-tuple-element.56), channel_id=1, source_target_pairs={{0,1},{1,0},{2,3},{3,2},{4,5},{5,4},{6,7},{7,6},{8,9},{9,8},{10,11... | collective-permute-start | bytes 9732104 | tf_op jit(solution)/shard_map/ppermute | solution.py:422
  51.0 21.9 %collective-permute-start.5 = (f32[3168,256]{1,0:T(8,128)}, f32[3168,256]{1,0:T(8,128)}, u32[]{:S(2)}, u32[]{:S(2)}) collective-permute-start(f32[3168,256]{1,0:T(8,128)} %get-tuple-element.54), channel_id=1, source_target_pairs={{0,1},{1,0},{2,3},{3,2},{4,5},{5,4},{6,7},{7,6},{8,9},{9,8},{10,11... | collective-permute-start | bytes 9732104 | tf_op jit(solution)/shard_map/ppermute | solution.py:422
  63.3 14.7 %collective-permute-start.4 = (f32[3168,256]{1,0:T(8,128)}, f32[3168,256]{1,0:T(8,128)}, u32[]{:S(2)}, u32[]{:S(2)}) collective-permute-start(f32[3168,256]{1,0:T(8,128)} %get-tuple-element.52), channel_id=1, source_target_pairs={{0,1},{1,0},{2,3},{3,2},{4,5},{5,4},{6,7},{7,6},{8,9},{9,8},{10,11... | collective-permute-start | bytes 9732104 | tf_op jit(solution)/shard_map/ppermute | solution.py:422
  102.9 8.0 %collective-permute-start.15 = (bf16[3168,256]{1,0:T(8,128)(2,1)S(1)}, bf16[3168,256]{1,0:T(8,128)(2,1)S(1)}, u32[]{:S(2)}, u32[]{:S(2)}) collective-permute-start(bf16[3168,256]{1,0:T(8,128)(2,1)S(1)} %logit_grads_chunk.5.refs_0_), channel_id=1, source_target_pairs={{0,1},{1,0},{2,3},{3,2},{4,5},{5,4},{6,7},{7,6},{8,9},{9,8},{10,11... | collective-permute-start | bytes 4866056 | tf_op jit(solution)/shard_map/ppermute | solution.py:422
  106.9 13.9 %collective-permute-start.14 = (bf16[3168,256]{1,0:T(8,128)(2,1)S(1)}, bf16[3168,256]{1,0:T(8,128)(2,1)S(1)}, u32[]{:S(2)}, u32[]{:S(2)}) collective-permute-start(bf16[3168,256]{1,0:T(8,128)(2,1)S(1)} %logit_grads_chunk.4.refs_0_), channel_id=1, source_target_pairs={{0,1},{1,0},{2,3},{3,2},{4,5},{5,4},{6,7},{7,6},{8,9},{9,8},{10,11... | collective-permute-start | bytes 4866056 | tf_op jit(solution)/shard_map/ppermute | solution.py:422
  110.9 19.4 %collective-permute-start.13 = (bf16[3168,256]{1,0:T(8,128)(2,1)S(1)}, bf16[3168,256]{1,0:T(8,128)(2,1)S(1)}, u32[]{:S(2)}, u32[]{:S(2)}) collective-permute-start(bf16[3168,256]{1,0:T(8,128)(2,1)S(1)} %logit_grads_chunk.3.refs_0_), channel_id=1, source_target_pairs={{0,1},{1,0},{2,3},{3,2},{4,5},{5,4},{6,7},{7,6},{8,9},{9,8},{10,11... | collective-permute-start | bytes 4866056 | tf_op jit(solution)/shard_map/ppermute | solution.py:422
  139.1 19.8 %collective-permute-start.16 = (bf16[256,1024]{1,0:T(8,128)(2,1)S(1)}, bf16[256,1024]{1,0:T(8,128)(2,1)S(1)}, u32[]{:S(2)}, u32[]{:S(2)}) collective-permute-start(bf16[256,1024]{1,0:T(8,128)(2,1)S(1)} %get-tuple-element.62), channel_id=1, source_target_pairs={{0,8},{8,0},{16,24},{24,16},{1,9},{9,1},{17,25},{25,17},{2,10},{10... | collective-permute-start | bytes 1572872 | tf_op jit(solution)/shard_map/ppermute | solution.py:422
  158.3 10.8 %collective-permute-start.19 = (bf16[256,768]{1,0:T(8,128)(2,1)S(1)}, bf16[256,768]{1,0:T(8,128)(2,1)S(1)}, u32[]{:S(2)}, u32[]{:S(2)}) collective-permute-start(bf16[256,768]{1,0:T(8,128)(2,1)S(1)} %get-tuple-element.73), channel_id=1, source_target_pairs={{0,8},{8,0},{16,24},{24,16},{1,9},{9,1},{17,25},{25,17},{2,10},{10... | collective-permute-start | bytes 1179656 | tf_op jit(solution)/shard_map/ppermute | solution.py:422
  159.2 10.8 %collective-permute-start.17 = (bf16[128,1024]{1,0:T(8,128)(2,1)S(1)}, bf16[128,1024]{1,0:T(8,128)(2,1)S(1)}, u32[]{:S(2)}, u32[]{:S(2)}) collective-permute-start(bf16[128,1024]{1,0:T(8,128)(2,1)S(1)} %dynamic-slice_convert_fusion), channel_id=1, source_target_pairs={{0,16},{8,24},{16,0},{24,8},{1,17},{9,25},{17,1},{25,9},{2,18},{10... | collective-permute-start | bytes 786440 | tf_op jit(solution)/shard_map/ppermute | solution.py:422
  169.2 13.8 %collective-permute-start.23 = (bf16[128,768]{1,0:T(8,128)(2,1)S(1)}, bf16[128,768]{1,0:T(8,128)(2,1)S(1)}, u32[]{:S(2)}, u32[]{:S(2)}) collective-permute-start(bf16[128,768]{1,0:T(8,128)(2,1)S(1)} %dynamic-slice_convert_fusion.1), channel_id=1, source_target_pairs={{0,16},{8,24},{16,0},{24,8},{1,17},{9,25},{17,1},{25,9},{2,18},{10... | collective-permute-start | bytes 589832 | tf_op jit(solution)/shard_map/ppermute | solution.py:422
  170.1 13.9 %collective-permute-start.18 = (bf16[32,1024]{1,0:T(8,128)(2,1)S(1)}, bf16[32,1024]{1,0:T(8,128)(2,1)S(1)}, u32[]{:S(2)}, u32[]{:S(2)}) collective-permute-start(bf16[32,1024]{1,0:T(8,128)(2,1)S(1)} %get-tuple-element.101), channel_id=1, source_target_pairs={{0,2},{2,0},{4,6},{6,4},{1,3},{3,1},{5,7},{7,5},{8,10},{10,8},{12,... | collective-permute-start | bytes 196616 | tf_op jit(solution)/shard_map/ppermute | solution.py:422
  170.2 17.4 %collective-permute-start.20 = (bf16[32,1024]{1,0:T(8,128)(2,1)S(1)}, bf16[32,1024]{1,0:T(8,128)(2,1)S(1)}, u32[]{:S(2)}, u32[]{:S(2)}) collective-permute-start(bf16[32,1024]{1,0:T(8,128)(2,1)S(1)} %get-tuple-element.103), channel_id=1, source_target_pairs={{0,4},{2,6},{4,0},{6,2},{1,5},{3,7},{5,1},{7,3},{8,12},{10,14},{12... | collective-permute-start | bytes 196616 | tf_op jit(solution)/shard_map/ppermute | solution.py:422
  170.9 16.7 %collective-permute-start.21 = (bf16[32,1024]{1,0:T(8,128)(2,1)S(1)}, bf16[32,1024]{1,0:T(8,128)(2,1)S(1)}, u32[]{:S(2)}, u32[]{:S(2)}) collective-permute-start(bf16[32,1024]{1,0:T(8,128)(2,1)S(1)} %get-tuple-element.102), channel_id=1, source_target_pairs={{0,6},{2,4},{4,2},{6,0},{1,7},{3,5},{5,3},{7,1},{8,14},{10,12},{12... | collective-permute-start | bytes 196616 | tf_op jit(solution)/shard_map/ppermute | solution.py:422
  183.1 13.1 %collective-permute-start.26 = (bf16[32,768]{1,0:T(8,128)(2,1)S(1)}, bf16[32,768]{1,0:T(8,128)(2,1)S(1)}, u32[]{:S(2)}, u32[]{:S(2)}) collective-permute-start(bf16[32,768]{1,0:T(8,128)(2,1)S(1)} %get-tuple-element.104), channel_id=1, source_target_pairs={{0,2},{2,0},{4,6},{6,4},{1,3},{3,1},{5,7},{7,5},{8,10},{10,8},{12,... | collective-permute-start | bytes 147464 | tf_op jit(solution)/shard_map/ppermute | solution.py:422
  183.2 13.0 %collective-permute-start.27 = (bf16[32,768]{1,0:T(8,128)(2,1)S(1)}, bf16[32,768]{1,0:T(8,128)(2,1)S(1)}, u32[]{:S(2)}, u32[]{:S(2)}) collective-permute-start(bf16[32,768]{1,0:T(8,128)(2,1)S(1)} %get-tuple-element.106), channel_id=1, source_target_pairs={{0,4},{2,6},{4,0},{6,2},{1,5},{3,7},{5,1},{7,3},{8,12},{10,14},{12... | collective-permute-start | bytes 147464 | tf_op jit(solution)/shard_map/ppermute | solution.py:422
  184.0 12.3 %collective-permute-start.28 = (bf16[32,768]{1,0:T(8,128)(2,1)S(1)}, bf16[32,768]{1,0:T(8,128)(2,1)S(1)}, u32[]{:S(2)}, u32[]{:S(2)}) collective-permute-start(bf16[32,768]{1,0:T(8,128)(2,1)S(1)} %get-tuple-element.105), channel_id=1, source_target_pairs={{0,6},{2,4},{4,2},{6,0},{1,7},{3,5},{5,3},{7,1},{8,14},{10,12},{12... | collective-permute-start | bytes 147464 | tf_op jit(solution)/shard_map/ppermute | solution.py:422
  196.3 6.7 %collective-permute-start.31 = (bf16[32,768]{1,0:T(8,128)(2,1)S(1)}, bf16[32,768]{1,0:T(8,128)(2,1)S(1)}, u32[]{:S(2)}, u32[]{:S(2)}) collective-permute-start(bf16[32,768]{1,0:T(8,128)(2,1)S(1)} %get-tuple-element.98), channel_id=1, source_target_pairs={{0,6},{2,4},{4,2},{6,0},{1,7},{3,5},{5,3},{7,1},{8,14},{10,12},{12... | collective-permute-start | bytes 147464 | tf_op jit(solution)/shard_map/ppermute | solution.py:422
  196.6 8.7 %collective-permute-start.30 = (bf16[32,768]{1,0:T(8,128)(2,1)S(1)}, bf16[32,768]{1,0:T(8,128)(2,1)S(1)}, u32[]{:S(2)}, u32[]{:S(2)}) collective-permute-start(bf16[32,768]{1,0:T(8,128)(2,1)S(1)} %get-tuple-element.98), channel_id=1, source_target_pairs={{0,4},{2,6},{4,0},{6,2},{1,5},{3,7},{5,1},{7,3},{8,12},{10,14},{12... | collective-permute-start | bytes 147464 | tf_op jit(solution)/shard_map/ppermute | solution.py:422
  197.0 8.2 %collective-permute-start.29 = (bf16[32,768]{1,0:T(8,128)(2,1)S(1)}, bf16[32,768]{1,0:T(8,128)(2,1)S(1)}, u32[]{:S(2)}, u32[]{:S(2)}) collective-permute-start(bf16[32,768]{1,0:T(8,128)(2,1)S(1)} %get-tuple-element.98), channel_id=1, source_target_pairs={{0,2},{2,0},{4,6},{6,4},{1,3},{3,1},{5,7},{7,5},{8,10},{10,8},{12,... | collective-permute-start | bytes 147464 | tf_op jit(solution)/shard_map/ppermute | solution.py:422
  200.9 6.1 %collective-permute-start.25 = (bf16[32,1024]{1,0:T(8,128)(2,1)S(1)}, bf16[32,1024]{1,0:T(8,128)(2,1)S(1)}, u32[]{:S(2)}, u32[]{:S(2)}) collective-permute-start(bf16[32,1024]{1,0:T(8,128)(2,1)S(1)} %get-tuple-element.96), channel_id=1, source_target_pairs={{0,6},{2,4},{4,2},{6,0},{1,7},{3,5},{5,3},{7,1},{8,14},{10,12},{12... | collective-permute-start | bytes 196616 | tf_op jit(solution)/shard_map/ppermute | solution.py:422
  (39 other events, 253.8 us)
where the time goes:
time: 210 us; the launch traced here: 209 us
  Pallas kernels  124 us (59%)
  starting transfers between devices  36.9 us (18%)
  waiting for transfers between devices  22.8 us (11%)
  local copies, waits for them, and re-layouts  22.3 us (11%)
    pallas_call x6, Pallas kernels, hidden_chunk(): pl.pallas_call(functools.partial(hidden_body, len(grads), owners, has_acc...  38.5 us
    ppermute x32, starting transfers between devices, swap(): return lax.ppermute(x, axis, [(i, i ^ k) for i in range(n)])  36.9 us
    pallas_call x3, Pallas kernels, student_chunk(): pl.pallas_call(functools.partial(student_body, owners, places), grid=(row...  33.2 us
    pallas_call x3, Pallas kernels, head_chunk(): pl.pallas_call(functools.partial(head_body, len(grads)), grid=(rows // ti...  25.5 us
    ppermute x32, waiting for transfers between devices, swap(): return lax.ppermute(x, axis, [(i, i ^ k) for i in range(n)])  22.8 us
    unnamed x62, local copies, waits for them, and re-layouts  16.8 us
    pallas_call x3, Pallas kernels, totals_chunk(): pl.pallas_call(functools.partial(totals_body, len(parts), len(teachers),...  15.5 us
    pallas_call x3, Pallas kernels, grads_chunk(): pl.pallas_call(functools.partial(grads_body, len(parts)), grid=(rows // t...  11.1 us
  transfers between devices with their start and end apart: 32, of which 11 were waited for; matrix products, arithmetic and copies ran while one was open for 3% of the time, Pallas kernels for 46%

commit v1 on v0

--- a/solution.py
+++ b/solution.py
@@ -13,11 +13,17 @@
 MIB = 1 << 20
 WEIGHT = 1 / 16
 TILE = 528
+ALL = 63
+UNREAD = pl.BlockSpec(memory_space=pl.ANY)
+SLICE = 48
 COLUMNS = 256
 
 
-def divide(total, parts, unit):
-    return parts if total % (unit * parts) == 0 else 1
+def chunks_of(total, parts):
+    if total % (16 * parts):
+        parts = 1
+    size = total // parts
+    return [(c * size, size) for c in range(parts)]
 
 
 def tile_of(rows, want):
@@ -66,25 +72,34 @@
 
 
 def add_totals(parts, teacher_refs, state_ref, sub):
-    student = parts[0][...]
-    for part in parts[1:]:
-        student = student + part[...]
-    target = jnp.concatenate([ref[...] for ref in teacher_refs], axis=1).astype(F32)
+    total = teacher_refs[0].shape[0]
+    size = tile_of(total, SLICE)
+    slices = [slice(at, at + size) for at in range(0, total, size)]
+
+    def load(rows):
+        student = parts[0][rows]
+        for part in parts[1:]:
+            student = student + part[rows]
+        target = jnp.concatenate([ref[rows] for ref in teacher_refs], axis=1).astype(F32)
+        return student, target
+
     old = [state_ref[sub * r : sub * (r + 1)] for r in range(5)]
-    top_s = jnp.maximum(old[0], fold(jnp.maximum, student, sub))
-    top_t = jnp.maximum(old[1], fold(jnp.maximum, target, sub))
-    exp_s = jnp.exp(spread(jnp.subtract, student, top_s, sub))
-    exp_t = jnp.exp(spread(jnp.subtract, target, top_t, sub))
+    top_s, top_t = old[:2]
+    for rows in slices:
+        student, target = load(rows)
+        top_s = jnp.maximum(top_s, fold(jnp.maximum, student, sub))
+        top_t = jnp.maximum(top_t, fold(jnp.maximum, target, sub))
     scale_s = jnp.exp(old[0] - top_s)
     scale_t = jnp.exp(old[1] - top_t)
-    new = [
-        top_s,
-        top_t,
-        old[2] * scale_s + fold(jnp.add, exp_s, sub),
-        old[3] * scale_t + fold(jnp.add, exp_t, sub),
-        old[4] * scale_t + fold(jnp.add, exp_t * (target - student), sub),
-    ]
-    for r, value in enumerate(new):
+    sum_s, sum_t, cross = old[2] * scale_s, old[3] * scale_t, old[4] * scale_t
+    for rows in slices:
+        student, target = load(rows)
+        exp_s = jnp.exp(spread(jnp.subtract, student, top_s, sub))
+        exp_t = jnp.exp(spread(jnp.subtract, target, top_t, sub))
+        sum_s += fold(jnp.add, exp_s, sub)
+        sum_t += fold(jnp.add, exp_t, sub)
+        cross += fold(jnp.add, exp_t * (target - student), sub)
+    for r, value in enumerate([top_s, top_t, sum_s, sum_t, cross]):
         state_ref[sub * r : sub * (r + 1)] = value
 
 
@@ -130,20 +145,23 @@
             out_ref[...] = state_ref[...]
 
 
-def totals_chunk(parts, teachers, first, before, last):
+def row_blocks(arrays, tile, skip=0):
+    return [pl.BlockSpec((tile, x.shape[1]), lambda i: (i + skip, 0)) for x in arrays]
+
+
+def totals_chunk(parts, teachers, before, last):
     rows, width = parts[0].shape
-    total = teachers[0].shape[0]
     sub = before.shape[0] // 5
     tile = tile_of(rows, TILE)
     out = (8 if last else 5 * sub, width)
     return pl.pallas_call(
         functools.partial(totals_body, len(parts), len(teachers), sub, last),
         grid=(rows // tile,),
-        in_specs=chunk_specs([*parts, *teachers], tile, first, total) + [whole(before.shape)],
+        in_specs=row_blocks([*parts, *teachers], tile) + [whole(before.shape)],
         out_specs=whole(out),
         out_shape=jax.ShapeDtypeStruct(out, F32),
         scratch_shapes=[pltpu.VMEM((5 * sub, width), F32)],
-        compiler_params=params(12),
+        compiler_params=params(ALL),
         cost_estimate=cost(
             12 * rows * width, (4 * len(parts) + 2) * rows * width, 2 * rows * width
         ),
@@ -151,8 +169,8 @@
     )(*parts, *teachers, before)
 
 
-def student_body(owners, places, *refs):
-    refs = list(refs)
+def student_body(owners, places, after, *refs):
+    refs = list(refs[after:])
     if places is not None:
         own_ref = refs.pop(0)
         piece_refs = [refs.pop(0) for _ in places]
@@ -174,12 +192,13 @@
         turned_ref = refs.pop(0)
     head_ref, *out_refs = refs
     width = out_refs[0].shape[1]
-    full = jnp.dot(head_ref[...], turned_ref[...], preferred_element_type=F32)
     for k, out_ref in enumerate(out_refs):
-        out_ref[...] = full[:, k * width : (k + 1) * width]
-
-
-def student_chunk(states, head_t, first, rows, owners, tokens):
+        out_ref[...] = jnp.dot(
+            head_ref[...], turned_ref[:, k * width : (k + 1) * width], preferred_element_type=F32
+        )
+
+
+def student_chunk(states, head_t, first, rows, owners, tokens, after):
     depth = head_t.shape[1]
     width = tokens // owners
     tile = tile_of(rows, TILE)
@@ -199,17 +218,19 @@
     else:
         args, specs = [states], [whole((depth, tokens))]
     return pl.pallas_call(
-        functools.partial(student_body, owners, places),
+        functools.partial(student_body, owners, places, len(after)),
         grid=(rows // tile,),
-        in_specs=specs + [pl.BlockSpec((tile, depth), lambda i: (i + base, 0))],
+        in_specs=[UNREAD] * len(after)
+        + specs
+        + [pl.BlockSpec((tile, depth), lambda i: (i + base, 0))],
         out_specs=outs,
         out_shape=shapes,
-        compiler_params=params(28),
+        compiler_params=params(ALL),
         cost_estimate=cost(
             2 * rows * tokens * depth, 2 * rows * depth + 2 * tokens * depth + 4 * rows * tokens
         ),
         name="student_chunk",
-    )(*args, head_t)
+    )(*after, *args, head_t)
 
 
 def merge(refs, shifts, width):
@@ -292,17 +313,16 @@
         ).astype(BF16)
 
 
-def grads_chunk(parts, teachers, coef, first):
+def grads_chunk(parts, teachers, coef):
     rows, width = parts[0].shape
     tile = tile_of(rows, 2 * TILE)
     return pl.pallas_call(
         functools.partial(grads_body, len(parts)),
         grid=(rows // tile,),
-        in_specs=chunk_specs([*parts, *teachers], tile, first, teachers[0].shape[0])
-        + [whole(coef.shape)],
+        in_specs=row_blocks([*parts, *teachers], tile) + [whole(coef.shape)],
         out_specs=pl.BlockSpec((tile, width), lambda i: (i, 0)),
         out_shape=jax.ShapeDtypeStruct((rows, width), BF16),
-        compiler_params=params(20),
+        compiler_params=params(14),
         cost_estimate=cost(
             8 * rows * width, (4 * len(parts) + 4) * rows * width, 2 * rows * width
         ),
@@ -310,71 +330,59 @@
     )(*parts, *teachers, coef)
 
 
-def chunk_specs(arrays, tile, first, total):
-    return [
-        pl.BlockSpec(
-            (tile, x.shape[1]),
-            functools.partial(lambda base, i: (i + base, 0), first // tile if x.shape[0] == total else 0),
-        )
-        for x in arrays
-    ]
-
-
-def hidden_body(count, owners, has_acc, emit, last, *refs):
+def hidden_body(count, after, has_acc, last, *refs):
+    refs = refs[after:]
     grads_refs, head_ref, *rest = (refs[:count], *refs[count:])
     before_ref = rest.pop(0) if has_acc else None
-    if emit:
-        turned_ref = rest.pop(0)
-
-        @pl.when(pl.program_id(0) == 0)
-        def _():
-            for k, ref in enumerate(grads_refs):
-                width = ref.shape[1]
-                turned_ref[k * width : (k + 1) * width] = ref[...].T
-
-    else:
-        turned_ref = grads_refs[0]
+    *out_refs, turned_ref = rest
+
+    @pl.when(pl.program_id(0) == 0)
+    def _():
+        for k, ref in enumerate(grads_refs):
+            width = ref.shape[1]
+            turned_ref[k * width : (k + 1) * width] = ref[...].T
+
     total = jnp.dot(turned_ref[...], head_ref[...], preferred_element_type=F32)
     if has_acc:
         total = total + before_ref[...]
     if not last:
-        rest[0][...] = total
+        out_refs[0][...] = total
         return
-    shard = total.shape[0] // (owners * len(rest))
-    for k in range(owners):
-        for w, out_ref in enumerate(rest):
-            at = (k * len(rest) + w) * shard
+    waves = len(out_refs)
+    shard = total.shape[0] // (count * waves)
+    for k in range(count):
+        for w, out_ref in enumerate(out_refs):
+            at = (k * waves + w) * shard
             out_ref[k * shard : (k + 1) * shard] = total[at : at + shard].astype(BF16)
 
 
-def hidden_chunk(grads, head_t, first, rows, owners, waves, tile, tiles, emit, before, last):
+def hidden_chunk(grads, head_t, first, waves, tile, tiles, before, last, after):
+    rows = grads[0].shape[0]
     width = COLUMNS if head_t.shape[1] % COLUMNS == 0 else 128
     base = first // rows
-    tokens = sum(g.shape[1] for g in grads) if emit else grads[0].shape[0]
-    block = pl.BlockSpec((tokens, width), lambda i: (0, i))
+    tokens = sum(g.shape[1] for g in grads)
     size = tiles * width
     pieces = waves if last else 1
-    out_specs = [pl.BlockSpec((tokens // pieces, width), lambda i: (0, i))] * pieces
-    out_shape = [jax.ShapeDtypeStruct((tokens // pieces, size), BF16 if last else F32)] * pieces
-    if emit:
-        out_specs = [whole((tokens, rows))] + out_specs
-        out_shape = [jax.ShapeDtypeStruct((tokens, rows), BF16)] + out_shape
+    block = lambda count: pl.BlockSpec((count, width), lambda i: (0, i))
     has_acc = before is not None
     return pl.pallas_call(
-        functools.partial(hidden_body, len(grads), owners, has_acc, emit, last),
+        functools.partial(hidden_body, len(grads), len(after), has_acc, last),
         grid=(tiles,),
-        in_specs=[whole(g.shape) for g in grads]
+        in_specs=[UNREAD] * len(after)
+        + [whole(g.shape) for g in grads]
         + [pl.BlockSpec((rows, width), lambda i: (base, i + tile))]
-        + [block] * has_acc,
-        out_specs=out_specs,
-        out_shape=out_shape,
+        + [block(tokens)] * has_acc,
+        out_specs=[block(tokens // pieces)] * pieces,
+        out_shape=[jax.ShapeDtypeStruct((tokens // pieces, size), BF16 if last else F32)] * pieces,
+        scratch_shapes=[pltpu.VMEM((tokens, rows), BF16)],
         compiler_params=params(32),
         cost_estimate=cost(2 * rows * tokens * size, 2 * rows * (size + tokens)),
         name="grad_hidden_chunk",
-    )(*grads, head_t, *([before] if has_acc else []))
-
-
-def head_body(count, hidden_ref, *refs):
+    )(*after, *grads, head_t, *([before] if has_acc else []))
+
+
+def head_body(count, after, *refs):
+    hidden_ref, *refs = refs[after:]
     grads = jnp.concatenate([ref[...] for ref in refs[:count]], axis=1)
     out_ref, flag_ref = refs[-2:]
 
@@ -389,18 +397,17 @@
         ).astype(BF16)
 
 
-def head_chunk(hidden, grads, first, total, before):
-    rows = grads[0].shape[0]
+def head_chunk(hidden, grads, first, skip, rows, total, before, after):
     tokens, depth = hidden.shape
     tile = tile_of(rows, TILE)
-    base = first // tile
-    specs = [whole(hidden.shape)] + chunk_specs(grads, tile, first, total)
+    base = (first + skip) // tile
+    specs = [UNREAD] * len(after) + [whole(hidden.shape)] + row_blocks(grads, tile, skip // tile)
     extra, aliases = [], {}
     if before is not None:
-        specs.append(pl.BlockSpec(memory_space=pl.ANY))
-        extra, aliases = [before], {1 + len(grads): 0}
+        specs.append(UNREAD)
+        extra, aliases = [before], {len(after) + 1 + len(grads): 0}
     return pl.pallas_call(
-        functools.partial(head_body, len(grads)),
+        functools.partial(head_body, len(grads), len(after)),
         grid=(rows // tile,),
         in_specs=specs,
         out_specs=[pl.BlockSpec((tile, depth), lambda i: (i + base, 0)), whole((8, 128))],
@@ -414,7 +421,7 @@
             2 * rows * tokens * depth, 2 * rows * depth + 2 * tokens * depth + 2 * rows * tokens
         ),
         name="grad_head_chunk",
-    )(hidden, *grads, *extra)
+    )(*after, hidden, *grads, *extra)
 
 
 def swap(x, axis, k):
@@ -448,7 +455,7 @@
     def over_inner(self, flag):
         total = self.partial[0].astype(F32)
         for w in range(1, self.waves):
-            total += tie(swap(self.partial[w], "dp", w), flag).astype(F32)
+            total += late(swap(self.partial[w], "dp", w), flag)
         self.total = total
         return total
 
@@ -456,39 +463,24 @@
         total = rows_at(self.total, self.own, self.shard)
         for a in range(1, self.owners):
             sent = rows_at(self.total, self.own ^ a, self.shard).astype(BF16)
-            total += tie(swap(sent, "dp", a * self.waves), flag).astype(F32)
+            total += late(swap(sent, "dp", a * self.waves), flag)
         self.total = total
         return total
 
-    def scatter_vocab(self, flag):
+    def over_vocab(self, step, flag):
         n = lax.axis_size("vocab")
-        if n > 4 or self.shard % (8 * n):
-            self.block = lax.psum(self.total, "vocab")
-            return self.block
-        mine, size = lax.axis_index("vocab"), self.shard // n
-        block = rows_at(self.total, mine, size)
-        for c in range(1, n):
-            sent = rows_at(self.total, mine ^ c, size).astype(BF16)
-            block += tie(swap(sent, "vocab", c), flag).astype(F32)
-        self.block = block.astype(BF16)
-        return self.block
-
-    def gather_vocab(self, flag):
-        if self.block.shape[0] == self.shard:
-            return self.block
-        n = lax.axis_size("vocab")
-        mine, size = lax.axis_index("vocab"), self.shard // n
-        result = jnp.zeros(self.total.shape, F32)
-        for c in range(n):
-            piece = tie(swap(self.block, "vocab", c), flag) if c else self.block
-            result = lax.dynamic_update_slice_in_dim(
-                result, piece.astype(F32), (mine ^ c) * size, 0
-            )
-        return result
-
-
-def tie(x, *after):
-    return lax.optimization_barrier((x, *after))[0]
+        if n > 4:
+            if step == 1:
+                self.total = lax.psum(self.total, "vocab")
+        elif step < n:
+            sent = self.total.astype(BF16)
+            self.total = sent.astype(F32) + late(swap(sent, "vocab", step), flag)
+        return self.total
+
+
+def late(x, flag):
+    x = x.astype(F32)
+    return x if flag is None else x + flag[0, 0]
 
 
 def per_device(hidden, head_weight, teacher_logits, response_start):
@@ -503,9 +495,6 @@
     head_t = head_weight.T
     teacher_t = teacher_logits.T
 
-    def in_wave(x, w):
-        return lax.dynamic_slice_in_dim(x, (inner ^ w) * shard, shard, axis=1)
-
     positions = mp * own_rows + jnp.concatenate(
         [(inner ^ w) * shard + jnp.arange(shard, dtype=jnp.int32) for w in range(waves)]
     )
@@ -515,10 +504,17 @@
         jnp.where(sequence[:, None] == seq_ids[None, :], response_start[None, :], 0), axis=1
     )
     mask = (positions % LEN >= starts).astype(F32)[None, :]
-    teachers = [in_wave(teacher_t, w) for w in range(waves)]
+    chunks = chunks_of(columns, 3)
+    teachers = [
+        [
+            lax.dynamic_slice(teacher_t, (first, (inner ^ w) * shard), (rows, shard))
+            for w in range(waves)
+        ]
+        for first, rows in chunks
+    ]
 
     near = {k: swap(hidden, "dp", k) for k in range(1, n_dp) if k < waves or k % waves == 0}
-    pieces = [(tie(hidden, *teachers), 0, 0)]
+    pieces = [(hidden, 0, 0)]
     for k in range(1, n_dp):
         a, w = k // waves, k % waves
         if k in near:
@@ -528,9 +524,6 @@
             pieces.append((swap(near[a * waves][:half], "dp", w), a, w * shard))
             pieces.append((swap(near[w][half:], "dp", a * waves), a, w * shard + half))
 
-    chunks = divide(columns, 3, 16)
-    rows = columns // chunks
-    firsts = [c * rows for c in range(chunks)]
     sub = 8 if columns % 8 == 0 else 1
 
     def exchanged(outs):
@@ -538,14 +531,15 @@
 
     parts = []
     states = (own.astype(jnp.int32).reshape(1), pieces)
-    for first in firsts:
-        outs = student_chunk(states, head_t, first, rows, n_mp, n_dp * shard)
+    for first, rows in chunks:
+        after = [] if first else [x for chunk in teachers for x in chunk]
+        outs = student_chunk(states, head_t, first, rows, n_mp, n_dp * shard, after)
         if len(outs) > n_mp:
             ordered, states = outs[n_mp:]
         parts.append(exchanged(outs[:n_mp]))
     totals = start_totals(sub, own_rows)
-    for c, first in enumerate(firsts):
-        totals = totals_chunk(parts[c], teachers, first, totals, c == chunks - 1)
+    for c in range(len(chunks)):
+        totals = totals_chunk(parts[c], teachers[c], totals, c == len(chunks) - 1)
     totals = merge_over(totals, "dp", waves)
     coef, kl = merge_over(totals, "vocab", waves, mask)
     token_kl = jnp.zeros((1, own_rows), F32)
@@ -555,46 +549,44 @@
         )
 
     all_grads = []
-    for c, first in enumerate(firsts):
-        all_grads.append(exchanged([grads_chunk(parts[c], teachers, coef, first)] * n_mp))
+    for c in range(len(chunks)):
+        all_grads.append(exchanged([grads_chunk(parts[c], teachers[c], coef)] * n_mp))
 
     tiles = depth // (COLUMNS if depth % COLUMNS == 0 else 128)
     split = (tiles + 1) // 2
     reductions = []
-    turned = [None] * chunks
+    outs = []
     for at, count in ((0, split), (split, tiles - split)):
-        acc = None
-        for c, first in enumerate(firsts):
-            inputs = all_grads[c] if at == 0 else [turned[c]]
+        acc, after = None, outs
+        for c, (first, rows) in enumerate(chunks):
+            last = c == len(chunks) - 1
             outs = hidden_chunk(
-                inputs, head_t, first, rows, n_mp, waves, at, count, at == 0, acc, c == chunks - 1
+                all_grads[c], head_t, first, waves, at, count, acc, last, after
             )
-            if at == 0:
-                turned[c], *outs = outs
-            acc = outs[0]
-        turned[0] = tie(turned[0], *outs)
+            acc, after = outs[0], []
         reductions.append(Reduction(outs, shard, own))
-    results = [reductions[0].over_inner(reductions[-1].partial[0])]
+
+    one, two = reductions
+    results = [one.over_inner(None)]
     plan = [
-        lambda flag: [reductions[0].over_outer(flag)]
-        + [r.over_inner(flag) for r in reductions[1:]],
-        lambda flag: [reductions[0].scatter_vocab(flag)]
-        + [r.over_outer(flag) for r in reductions[1:]],
-        lambda flag: [reductions[0].gather_vocab(flag)]
-        + [r.scatter_vocab(flag) for r in reductions[1:]],
+        lambda flag: [one.over_outer(flag), two.over_inner(flag)],
+        lambda flag: [one.over_vocab(1, flag), two.over_outer(flag)],
+        lambda flag: [one.over_vocab(2, flag), two.over_vocab(1, flag)],
+        lambda flag: [one.total, two.over_vocab(2, flag)],
     ]
+    calls = [(c, 0, rows) for c, (_, rows) in enumerate(chunks)]
+    if calls[-1][2] % (2 * TILE) == 0:
+        c, _, rows = calls.pop()
+        calls += [(c, 0, rows // 2), (c, rows // 2, rows // 2)]
     grad_head = None
-    for c, first in enumerate(firsts):
+    for c, skip, rows in calls:
         grad_head, flag = head_chunk(
-            tie(ordered, *results), all_grads[c], first, columns, grad_head
+            ordered, all_grads[c], chunks[c][0], skip, rows, columns, grad_head, results
         )
-        if plan:
-            results = plan.pop(0)(flag)
+        results = plan.pop(0)(flag)
     while plan:
         results = plan.pop(0)(flag)
-    grad_hidden = jnp.concatenate(
-        [results[0]] + [r.gather_vocab(flag) for r in reductions[1:]], axis=1
-    )
+    grad_hidden = jnp.concatenate(results, axis=1)
     return (token_kl.reshape(own_rows), grad_hidden, grad_head.T)
 
 

time: 210 us -> 213 us (1.014)
  Pallas kernels: 124 us -> 135 us
  starting transfers between devices: 36.9 us -> 26 us
  other arithmetic: 1.61 us -> 7.35 us
  local copies, waits for them, and re-layouts: 22.3 us -> 17 us
  waiting for transfers between devices: 22.8 us -> 25.9 us
    ppermute x32 -> x24, starting transfers between devices: 36.9 us -> 26 us  [swap(): return lax.ppermute(x, axis, [(i, i ^ k) for i in range(n)])]
    pallas_call x12 -> x13, Pallas kernels: 97.3 us -> 104 us  [the longest x6 41.2 us: hidden_chunk(): pl.pallas_call(functools.partial(hidden_body, len(grads), len(after), has...]
    unnamed x62 -> x56, local copies, waits for them, and re-layouts: 16.8 us -> 9.89 us
    ppermute x32 -> x24, waiting for transfers between devices: 22.8 us -> 25.9 us  [swap(): return lax.ppermute(x, axis, [(i, i ^ k) for i in range(n)])]
    add x4, other arithmetic: 0.35 us -> 3.38 us  [the longest x2 1.96 us: over_inner(): total += late(swap(self.partial[w], 'dp', w), flag)]
    pallas_call x3, Pallas kernels: 15.5 us -> 18.4 us  [totals_chunk(): pl.pallas_call(functools.partial(totals_body, len(parts), len(teachers),...]
    convert_element_type x0 -> x4, other arithmetic: none -> 2.87 us  [over_vocab(): sent = self.total.astype(BF16)]
  transfers between devices with their start and end apart: 32 -> 24, of which waited for: 11 -> 7; matrix products, arithmetic and copies ran while one was open for 3% -> 6% of each run, Pallas kernels for 46% -> 49%
where the time goes in v1:
time: 213 us; the launch traced here: 212 us
  Pallas kernels  135 us (63%)
  starting transfers between devices  26 us (12%)
  waiting for transfers between devices  25.9 us (12%)
  local copies, waits for them, and re-layouts  17 us (8%)
  other arithmetic  7.35 us (3%)
    pallas_call x6, Pallas kernels, hidden_chunk(): pl.pallas_call(functools.partial(hidden_body, len(grads), len(after), has...  41.2 us
    pallas_call x3, Pallas kernels, student_chunk(): pl.pallas_call(functools.partial(student_body, owners, places, len(after)...  36.4 us
    pallas_call x4, Pallas kernels, head_chunk(): pl.pallas_call(functools.partial(head_body, len(grads), len(after)), grid...  26.8 us
    ppermute x24, starting transfers between devices, swap(): return lax.ppermute(x, axis, [(i, i ^ k) for i in range(n)])  26 us
    ppermute x24, waiting for transfers between devices, swap(): return lax.ppermute(x, axis, [(i, i ^ k) for i in range(n)])  25.9 us
    pallas_call x3, Pallas kernels, totals_chunk(): pl.pallas_call(functools.partial(totals_body, len(parts), len(teachers),...  18.4 us
    pallas_call x3, Pallas kernels, grads_chunk(): pl.pallas_call(functools.partial(grads_body, len(parts)), grid=(rows // t...  11.9 us
    unnamed x56, local copies, waits for them, and re-layouts  9.89 us
  transfers between devices with their start and end apart: 24, of which 7 were waited for; matrix products, arithmetic and copies ran while one was open for 6% of the time, Pallas kernels for 49%

profile of v1, /device:TPU:0, one launch (start us, length us, event | category | flops | bytes accessed | tf_op | source)
XLA Modules:
  0.0 212.0 jit_solution(324632730214685431)
XLA Ops:
  0.6 3.0 %collective-permute-start = (bf16[128,1792]{1,0:T(8,128)(2,1)}, bf16[128,1792]{1,0:T(8,128)(2,1)S(1)}, u32[]{:S(2)}, u32[]{:S(2)}) collective-permute-start(bf16[128,1792]{1,0:T(8,128)(2,1)} %refs_7_.1), channel_id=1, source_target_pairs={{0,8},{8,0},{16,24},{24,16},{1,9},{9,1},{17,25},{25,17},{2,10},{10... | collective-permute-start | bytes 1376264 | tf_op jit(solution)/shard_map/ppermute | solution.py:429
  5.2 9.2 %collective-permute-done.refs_8_ = bf16[128,1792]{1,0:T(8,128)(2,1)S(1)} collective-permute-done((bf16[128,1792]{1,0:T(8,128)(2,1)}, bf16[128,1792]{1,0:T(8,128)(2,1)S(1)}, u32[]{:S(2)}, u32[]{:S(2)}) %collective-permute-start) | collective-permute-done | bytes 458784 | tf_op jit(solution)/shard_map/ppermute | solution.py:429
  17.8 4.6 %dynamic-slice_bitcast_fusion = (bf16[3168,128]{1,0:T(8,128)(2,1)}, bf16[3168,128]{1,0:T(8,128)(2,1)}, bf16[3168,128]{1,0:T(8,128)(2,1)}, bf16[3168,128]{1,0:T(8...) fusion(bf16[256,9504]{0,1:T(8,128)(2,1)} %param.6, s32[]{:T(128)S(6)} %select_n.59, s32[]{:T(128)S(6)} %select_n.58), kind=kLoop, calls=%fused_computation.2 | loop fusion | bytes 9732104 | tf_op jit(solution)/shard_map/dynamic_slice | solution.py:510
  23.9 12.8 %student_chunk.3 = (f32[3168,256]{1,0:T(8,128)}, f32[3168,256]{1,0:T(8,128)}, bf16[512,1792]{1,0:T(8,128)(2,1)}, bf16[1792,512]{1,0:T(8,128)(2,1)}) custom-call(bf16[3168,128]{1,0:T(8,128)(2,1)} %get-tuple-element.59.refs_0_.refs_2_, bf16[3168,128]{1,0:T(8,128)(2,1)} %get-tuple-element.58.refs_1_.refs_3_, bf16[3168,128]{1,0:T(8,128)(2,1)} %get-tuple-element.57.refs_2_, ...), custom_call_target="tpu_custom_call" | custom-call | flops 363331584 | bytes 1229824 | tf_op jit(solution)/shard_map/student_chunk/pallas_call | solution.py:220
  36.7 11.8 %student_chunk.5 = (f32[3168,256]{1,0:T(8,128)}, f32[3168,256]{1,0:T(8,128)}) custom-call(bf16[1792,512]{1,0:T(8,128)(2,1)} %get-tuple-element.25.refs_0_, bf16[9504,1792]{1,0:T(8,128)(2,1)} %bitcast.29), custom_call_target="tpu_custom_call" | custom-call | flops 363331584 | bytes 1229824 | tf_op jit(solution)/shard_map/student_chunk/pallas_call | solution.py:220
  49.0 11.8 %student_chunk.4 = (f32[3168,256]{1,0:T(8,128)}, f32[3168,256]{1,0:T(8,128)}) custom-call(bf16[1792,512]{1,0:T(8,128)(2,1)} %get-tuple-element.25.refs_0_, bf16[9504,1792]{1,0:T(8,128)(2,1)} %bitcast.30), custom_call_target="tpu_custom_call" | custom-call | flops 363331584 | bytes 1229824 | tf_op jit(solution)/shard_map/student_chunk/pallas_call | solution.py:220
  61.0 6.1 %totals_chunk.3.refs_4_ = f32[40,256]{1,0:T(8,128)} custom-call(f32[3168,256]{1,0:T(8,128)} %get-tuple-element.30.refs_0_, f32[3168,256]{1,0:T(8,128)} %collective-permute-done.6.refs_1_, bf16[3168,128]{1,0:T(8,128)(2,1)} %get-tuple-element.59.refs_0_.refs_2_, bf16[3168,128]{1,0:T(8,128)(2,1)} %get-tuple-element.58.refs_1_.refs_3_, ...), custom_call_target="tpu_custom_call" | custom-call | flops 608256 | bytes 506880 | tf_op jit(solution)/shard_map/totals_chunk/pallas_call | solution.py:157
  67.1 6.1 %totals_chunk.4.refs_4_ = f32[40,256]{1,0:T(8,128)} custom-call(f32[3168,256]{1,0:T(8,128)} %get-tuple-element.28.refs_0_, f32[3168,256]{1,0:T(8,128)} %collective-permute-done.5.refs_1_, bf16[3168,128]{1,0:T(8,128)(2,1)} %get-tuple-element.57.refs_2_, bf16[3168,128]{1,0:T(8,128)(2,1)} %get-tuple-element.56.refs_3_, f32[40,256]{1,0:T(8,128)} %totals_chunk.3.refs_4_), custom_call_target="tpu_custom_call" | custom-call | flops 608256 | bytes 506880 | tf_op jit(solution)/shard_map/totals_chunk/pallas_call | solution.py:157
  73.2 6.2 %totals_chunk.5.refs_0_ = f32[8,256]{1,0:T(8,128)} custom-call(f32[3168,256]{1,0:T(8,128)} %get-tuple-element.26.refs_0_, f32[3168,256]{1,0:T(8,128)} %collective-permute-done.4.refs_1_, bf16[3168,128]{1,0:T(8,128)(2,1)} %get-tuple-element.60.refs_4_.refs_2_, bf16[3168,128]{1,0:T(8,128)(2,1)} %get-tuple-element.55.refs_5_.refs_3_, f32[40,256]{1,0:T(8,128)} %totals_chunk.4.refs_4_), custom_call_target="tpu_custom_call" | custom-call | flops 608256 | bytes 506880 | tf_op jit(solution)/shard_map/totals_chunk/pallas_call | solution.py:157
  86.2 3.7 %collective-permute-start.12 = (f32[8,256]{1,0:T(8,128)S(1)}, f32[8,256]{1,0:T(8,128)S(1)}, u32[]{:S(2)}, u32[]{:S(2)}) collective-permute-start(f32[8,256]{1,0:T(8,128)S(1)} %merge_totals.1.refs_0_), channel_id=1, source_target_pairs={{0,6},{2,4},{4,2},{6,0},{1,7},{3,5},{5,3},{7,1},{8,14},{10,12},{12... | collective-permute-start | bytes 24584 | tf_op jit(solution)/shard_map/ppermute | solution.py:429
  97.6 3.8 %logit_grads_chunk.5.refs_0_.refs_2_ = bf16[3168,256]{1,0:T(8,128)(2,1)S(1)} custom-call(f32[3168,256]{1,0:T(8,128)S(1)} %copy-done.9, f32[3168,256]{1,0:T(8,128)} %collective-permute-done.6.refs_1_, bf16[3168,128]{1,0:T(8,128)(2,1)S(1)} %copy-done.17, bf16[3168,128]{1,0:T(8,128)(2,1)S(1)} %copy-done.16, f32[8,256]{1,0:T(8,128)S(1)} %get-tuple-element.33.refs_4_), custom_call_target="tpu_custom_call" | custom-call | flops 405504 | bytes 608256 | tf_op jit(solution)/shard_map/logit_grads_chunk/pallas_call | solution.py:319
  101.5 4.2 %logit_grads_chunk.4.refs_0_.refs_3_ = bf16[3168,256]{1,0:T(8,128)(2,1)S(1)} custom-call(f32[3168,256]{1,0:T(8,128)S(1)} %copy-done.11, f32[3168,256]{1,0:T(8,128)} %collective-permute-done.5.refs_1_, bf16[3168,128]{1,0:T(8,128)(2,1)S(1)} %copy-done.15, bf16[3168,128]{1,0:T(8,128)(2,1)S(1)} %copy-done.14, f32[8,256]{1,0:T(8,128)S(1)} %get-tuple-element.33.refs_4_), custom_call_target="tpu_custom_call" | custom-call | flops 405504 | bytes 608256 | tf_op jit(solution)/shard_map/logit_grads_chunk/pallas_call | solution.py:319
  105.9 3.8 %logit_grads_chunk.3.refs_0_.refs_3_ = bf16[3168,256]{1,0:T(8,128)(2,1)S(1)} custom-call(f32[3168,256]{1,0:T(8,128)S(1)} %copy-done.10, f32[3168,256]{1,0:T(8,128)} %collective-permute-done.4.refs_1_, bf16[3168,128]{1,0:T(8,128)(2,1)S(1)} %copy-done.13, bf16[3168,128]{1,0:T(8,128)(2,1)S(1)} %copy-done.12, f32[8,256]{1,0:T(8,128)S(1)} %get-tuple-element.33.refs_4_), custom_call_target="tpu_custom_call" | custom-call | flops 405504 | bytes 608256 | tf_op jit(solution)/shard_map/logit_grads_chunk/pallas_call | solution.py:319
  109.8 7.7 %grad_hidden_chunk.6.refs_3_ = f32[512,1024]{1,0:T(8,128)S(1)} custom-call(bf16[3168,256]{1,0:T(8,128)(2,1)S(1)} %logit_grads_chunk.5.refs_0_.refs_2_, bf16[3168,256]{1,0:T(8,128)(2,1)S(1)} %collective-permute-done.15.refs_1_.refs_3_, bf16[9504,1792]{1,0:T(8,128)(2,1)} %bitcast.31), custom_call_target="tpu_custom_call" | custom-call | flops 207618048 | bytes 608256 | tf_op jit(solution)/shard_map/grad_hidden_chunk/pallas_call | solution.py:368
  117.6 7.7 %grad_hidden_chunk.7.refs_3_ = f32[512,1024]{1,0:T(8,128)S(1)} custom-call(bf16[3168,256]{1,0:T(8,128)(2,1)S(1)} %logit_grads_chunk.4.refs_0_.refs_3_, bf16[3168,256]{1,0:T(8,128)(2,1)S(1)} %collective-permute-done.14.refs_1_.refs_4_, bf16[9504,1792]{1,0:T(8,128)(2,1)} %bitcast.32, f32[512,1024]{1,0:T(8,128)S(1)} %grad_hidden_chunk.6.refs_3_), custom_call_target="tpu_custom_call" | custom-call | flops 207618048 | bytes 608256 | tf_op jit(solution)/shard_map/grad_hidden_chunk/pallas_call | solution.py:368
  125.3 7.8 %grad_hidden_chunk.8 = (bf16[256,1024]{1,0:T(8,128)(2,1)S(1)}, bf16[256,1024]{1,0:T(8,128)(2,1)}) custom-call(bf16[3168,256]{1,0:T(8,128)(2,1)S(1)} %logit_grads_chunk.3.refs_0_.refs_3_, bf16[3168,256]{1,0:T(8,128)(2,1)S(1)} %collective-permute-done.13.refs_1_.refs_4_, bf16[9504,1792]{1,0:T(8,128)(2,1)} %bitcast.33, f32[512,1024]{1,0:T(8,128)S(1)} %grad_hidden_chunk.7.refs_3_), custom_call_target="tpu_custom_call" | custom-call | flops 207618048 | bytes 608256 | tf_op jit(solution)/shard_map/grad_hidden_chunk/pallas_call | solution.py:368
  139.3 6.1 %grad_hidden_chunk.9.refs_3_ = f32[512,768]{1,0:T(8,128)S(1)} custom-call(bf16[256,1024]{1,0:T(8,128)(2,1)S(1)} %copy-done.19, bf16[256,1024]{1,0:T(8,128)(2,1)} %get-tuple-element.35.refs_1_, bf16[3168,256]{1,0:T(8,128)(2,1)S(1)} %copy-done.4, bf16[3168,256]{1,0:T(8,128)(2,1)S(1)} %copy-done.8, bf16[9504,1792]{1,0:T(8,128)(2,1)} %bitcast.34), custom_call_target="tpu_custom_call" | custom-call | flops 155713536 | bytes 506880 | tf_op jit(solution)/shard_map/grad_hidden_chunk/pallas_call | solution.py:368
  145.4 5.9 %grad_hidden_chunk.10.refs_3_ = f32[512,768]{1,0:T(8,128)S(1)} custom-call(bf16[3168,256]{1,0:T(8,128)(2,1)S(1)} %copy-done.2, bf16[3168,256]{1,0:T(8,128)(2,1)S(1)} %copy-done.6, bf16[9504,1792]{1,0:T(8,128)(2,1)} %bitcast.35, f32[512,768]{1,0:T(8,128)S(1)} %grad_hidden_chunk.9.refs_3_), custom_call_target="tpu_custom_call" | custom-call | flops 155713536 | bytes 506880 | tf_op jit(solution)/shard_map/grad_hidden_chunk/pallas_call | solution.py:368
  151.4 6.0 %grad_hidden_chunk.11 = (bf16[256,768]{1,0:T(8,128)(2,1)S(1)}, bf16[256,768]{1,0:T(8,128)(2,1)S(1)}) custom-call(bf16[3168,256]{1,0:T(8,128)(2,1)S(1)} %logit_grads_chunk.3.refs_0_.refs_3_, bf16[3168,256]{1,0:T(8,128)(2,1)S(1)} %collective-permute-done.13.refs_1_.refs_4_, bf16[9504,1792]{1,0:T(8,128)(2,1)} %bitcast.36, f32[512,768]{1,0:T(8,128)S(1)} %grad_hidden_chunk.10.refs_3_), custom_call_target="tpu_custom_call" | custom-call | flops 155713536 | bytes 506880 | tf_op jit(solution)/shard_map/grad_hidden_chunk/pallas_call | solution.py:368
  160.5 8.5 %grad_head_chunk.4 = (bf16[9504,1792]{1,0:T(8,128)(2,1)}, f32[8,128]{1,0:T(8,128)S(1)}) custom-call(f32[256,1024]{1,0:T(8,128)S(1)} %convert_add_fusion.refs_0_, bf16[512,1792]{1,0:T(8,128)(2,1)S(1)} %copy-done, bf16[3168,256]{1,0:T(8,128)(2,1)S(1)} %copy-done.4, bf16[3168,256]{1,0:T(8,128)(2,1)S(1)} %copy-done.8), custom_call_target="tpu_custom_call" | custom-call | flops 363331584 | bytes 1027072 | tf_op jit(solution)/shard_map/grad_head_chunk/pallas_call | solution.py:409
  172.3 8.5 %grad_head_chunk.5 = (bf16[9504,1792]{1,0:T(8,128)(2,1)}, f32[8,128]{1,0:T(8,128)S(1)}) custom-call(f32[128,1024]{1,0:T(8,128)S(1)} %get-tuple-element.52.refs_0_, f32[256,768]{1,0:T(8,128)S(1)} %add_add_fusion.refs_1_, bf16[512,1792]{1,0:T(8,128)(2,1)S(1)} %copy-done, bf16[3168,256]{1,0:T(8,128)(2,1)S(1)} %copy-done.2, ...), custom_call_target="tpu_custom_call", output_to_operand_aliasing={{0}: (5, {})} | custom-call | flops 363331584 | bytes 1027072 | tf_op jit(solution)/shard_map/grad_head_chunk/pallas_call | solution.py:409
  186.9 4.9 %grad_head_chunk.6 = (bf16[9504,1792]{1,0:T(8,128)(2,1)}, f32[8,128]{1,0:T(8,128)S(1)}) custom-call(f32[128,1024]{1,0:T(8,128)S(1)} %get-tuple-element.48.refs_0_, f32[128,768]{1,0:T(8,128)S(1)} %get-tuple-element.54.refs_1_, bf16[512,1792]{1,0:T(8,128)(2,1)S(1)} %copy-done, ...), custom_call_target="tpu_custom_call", output_to_operand_aliasing={{0}: (5, {})} | custom-call | flops 181665792 | bytes 570880 | tf_op jit(solution)/shard_map/grad_head_chunk/pallas_call | solution.py:409
  194.0 10.2 %collective-permute-done.20 = bf16[128,1024]{1,0:T(8,128)(2,1)S(1)} collective-permute-done((bf16[128,1024]{1,0:T(8,128)(2,1)S(1)}, bf16[128,1024]{1,0:T(8,128)(2,1)S(1)}, u32[]{:S(2)}, u32[]{:S(2)}) %collective-permute-start.20) | collective-permute-done | bytes 262176 | tf_op jit(solution)/shard_map/ppermute | solution.py:429
  204.9 4.9 %grad_head_chunk.7 = (bf16[9504,1792]{1,0:T(8,128)(2,1)}, f32[8,128]{1,0:T(8,128)S(1)}) custom-call(f32[128,1024]{1,0:T(8,128)S(1)} %add_add_fusion.1.refs_0_, f32[128,768]{1,0:T(8,128)S(1)} %get-tuple-element.50.refs_1_, bf16[512,1792]{1,0:T(8,128)(2,1)S(1)} %copy-done, ...), custom_call_target="tpu_custom_call", output_to_operand_aliasing={{0}: (5, {})} | custom-call | flops 181665792 | bytes 570880 | tf_op jit(solution)/shard_map/grad_head_chunk/pallas_call | solution.py:409
  (127 shorter events, 45.5 us)
Async XLA Ops:
  0.6 13.7 %collective-permute-start = (bf16[128,1792]{1,0:T(8,128)(2,1)}, bf16[128,1792]{1,0:T(8,128)(2,1)S(1)}, u32[]{:S(2)}, u32[]{:S(2)}) collective-permute-start(bf16[128,1792]{1,0:T(8,128)(2,1)} %refs_7_.1), channel_id=1, source_target_pairs={{0,8},{8,0},{16,24},{24,16},{1,9},{9,1},{17,25},{25,17},{2,10},{10... | collective-permute-start | bytes 1376264 | tf_op jit(solution)/shard_map/ppermute | solution.py:429
  3.6 12.6 %collective-permute-start.1 = (bf16[128,1792]{1,0:T(8,128)(2,1)}, bf16[128,1792]{1,0:T(8,128)(2,1)S(1)}, u32[]{:S(2)}, u32[]{:S(2)}) collective-permute-start(bf16[128,1792]{1,0:T(8,128)(2,1)} %refs_7_.1), channel_id=1, source_target_pairs={{0,16},{8,24},{16,0},{24,8},{1,17},{9,25},{17,1},{25,9},{2,18},{10... | collective-permute-start | bytes 1376264 | tf_op jit(solution)/shard_map/ppermute | solution.py:429
  14.4 8.1 %collective-permute-start.3 = (bf16[64,1792]{1,0:T(8,128)(2,1)S(1)}, bf16[64,1792]{1,0:T(8,128)(2,1)S(1)}, u32[]{:S(2)}, u32[]{:S(2)}) collective-permute-start(bf16[64,1792]{1,0:T(8,128)(2,1)S(1)} %slice.36), channel_id=1, source_target_pairs={{0,16},{8,24},{16,0},{24,8},{1,17},{9,25},{17,1},{25,9},{2,18},{10... | collective-permute-start | bytes 688136 | tf_op jit(solution)/shard_map/ppermute | solution.py:429
  16.2 6.3 %collective-permute-start.2 = (bf16[64,1792]{1,0:T(8,128)(2,1)S(1)}, bf16[64,1792]{1,0:T(8,128)(2,1)S(1)}, u32[]{:S(2)}, u32[]{:S(2)}) collective-permute-start(bf16[64,1792]{1,0:T(8,128)(2,1)S(1)} %slice.35), channel_id=1, source_target_pairs={{0,8},{8,0},{16,24},{24,16},{1,9},{9,1},{17,25},{25,17},{2,10},{10... | collective-permute-start | bytes 688136 | tf_op jit(solution)/shard_map/ppermute | solution.py:429
  36.7 24.3 %collective-permute-start.6 = (f32[3168,256]{1,0:T(8,128)}, f32[3168,256]{1,0:T(8,128)}, u32[]{:S(2)}, u32[]{:S(2)}) collective-permute-start(f32[3168,256]{1,0:T(8,128)} %get-tuple-element.31), channel_id=1, source_target_pairs={{0,1},{1,0},{2,3},{3,2},{4,5},{5,4},{6,7},{7,6},{8,9},{9,8},{10,11... | collective-permute-start | bytes 9732104 | tf_op jit(solution)/shard_map/ppermute | solution.py:429
  48.5 18.5 %collective-permute-start.5 = (f32[3168,256]{1,0:T(8,128)}, f32[3168,256]{1,0:T(8,128)}, u32[]{:S(2)}, u32[]{:S(2)}) collective-permute-start(f32[3168,256]{1,0:T(8,128)} %get-tuple-element.29), channel_id=1, source_target_pairs={{0,1},{1,0},{2,3},{3,2},{4,5},{5,4},{6,7},{7,6},{8,9},{9,8},{10,11... | collective-permute-start | bytes 9732104 | tf_op jit(solution)/shard_map/ppermute | solution.py:429
  60.8 12.4 %collective-permute-start.4 = (f32[3168,256]{1,0:T(8,128)}, f32[3168,256]{1,0:T(8,128)}, u32[]{:S(2)}, u32[]{:S(2)}) collective-permute-start(f32[3168,256]{1,0:T(8,128)} %get-tuple-element.27), channel_id=1, source_target_pairs={{0,1},{1,0},{2,3},{3,2},{4,5},{5,4},{6,7},{7,6},{8,9},{9,8},{10,11... | collective-permute-start | bytes 9732104 | tf_op jit(solution)/shard_map/ppermute | solution.py:429
  79.4 4.8 %collective-permute-start.9 = (f32[8,256]{1,0:T(8,128)}, f32[8,256]{1,0:T(8,128)S(1)}, u32[]{:S(2)}, u32[]{:S(2)}) collective-permute-start(f32[8,256]{1,0:T(8,128)} %totals_chunk.5.refs_0_), channel_id=1, source_target_pairs={{0,24},{8,16},{16,8},{24,0},{1,25},{9,17},{17,9},{25,1},{2,26},{10... | collective-permute-start | bytes 24584 | tf_op jit(solution)/shard_map/ppermute | solution.py:429
  80.5 3.9 %collective-permute-start.8 = (f32[8,256]{1,0:T(8,128)}, f32[8,256]{1,0:T(8,128)S(1)}, u32[]{:S(2)}, u32[]{:S(2)}) collective-permute-start(f32[8,256]{1,0:T(8,128)} %totals_chunk.5.refs_0_), channel_id=1, source_target_pairs={{0,16},{8,24},{16,0},{24,8},{1,17},{9,25},{17,1},{25,9},{2,18},{10... | collective-permute-start | bytes 24584 | tf_op jit(solution)/shard_map/ppermute | solution.py:429
  81.6 3.9 %collective-permute-start.7 = (f32[8,256]{1,0:T(8,128)}, f32[8,256]{1,0:T(8,128)S(1)}, u32[]{:S(2)}, u32[]{:S(2)}) collective-permute-start(f32[8,256]{1,0:T(8,128)} %totals_chunk.5.refs_0_), channel_id=1, source_target_pairs={{0,8},{8,0},{16,24},{24,16},{1,9},{9,1},{17,25},{25,17},{2,10},{10... | collective-permute-start | bytes 24584 | tf_op jit(solution)/shard_map/ppermute | solution.py:429
  86.2 5.5 %collective-permute-start.12 = (f32[8,256]{1,0:T(8,128)S(1)}, f32[8,256]{1,0:T(8,128)S(1)}, u32[]{:S(2)}, u32[]{:S(2)}) collective-permute-start(f32[8,256]{1,0:T(8,128)S(1)} %merge_totals.1.refs_0_), channel_id=1, source_target_pairs={{0,6},{2,4},{4,2},{6,0},{1,7},{3,5},{5,3},{7,1},{8,14},{10,12},{12... | collective-permute-start | bytes 24584 | tf_op jit(solution)/shard_map/ppermute | solution.py:429
  89.9 4.5 %collective-permute-start.11 = (f32[8,256]{1,0:T(8,128)S(1)}, f32[8,256]{1,0:T(8,128)S(1)}, u32[]{:S(2)}, u32[]{:S(2)}) collective-permute-start(f32[8,256]{1,0:T(8,128)S(1)} %merge_totals.1.refs_0_), channel_id=1, source_target_pairs={{0,4},{2,6},{4,0},{6,2},{1,5},{3,7},{5,1},{7,3},{8,12},{10,14},{12... | collective-permute-start | bytes 24584 | tf_op jit(solution)/shard_map/ppermute | solution.py:429
  89.9 4.5 %collective-permute-start.10 = (f32[8,256]{1,0:T(8,128)S(1)}, f32[8,256]{1,0:T(8,128)S(1)}, u32[]{:S(2)}, u32[]{:S(2)}) collective-permute-start(f32[8,256]{1,0:T(8,128)S(1)} %merge_totals.1.refs_0_), channel_id=1, source_target_pairs={{0,2},{2,0},{4,6},{6,4},{1,3},{3,1},{5,7},{7,5},{8,10},{10,8},{12,... | collective-permute-start | bytes 24584 | tf_op jit(solution)/shard_map/ppermute | solution.py:429
  101.4 8.4 %collective-permute-start.15 = (bf16[3168,256]{1,0:T(8,128)(2,1)S(1)}, bf16[3168,256]{1,0:T(8,128)(2,1)S(1)}, u32[]{:S(2)}, u32[]{:S(2)}) collective-permute-start(bf16[3168,256]{1,0:T(8,128)(2,1)S(1)} %logit_grads_chunk.5.refs_0_.refs_2_), channel_id=1, source_target_pairs={{0,1},{1,0},{2,3},{3,2},{4,5},{5,4},{6,7},{7,6},{8,9},{9,8},{10,11... | collective-permute-start | bytes 4866056 | tf_op jit(solution)/shard_map/ppermute | solution.py:429
  105.8 11.8 %collective-permute-start.14 = (bf16[3168,256]{1,0:T(8,128)(2,1)S(1)}, bf16[3168,256]{1,0:T(8,128)(2,1)S(1)}, u32[]{:S(2)}, u32[]{:S(2)}) collective-permute-start(bf16[3168,256]{1,0:T(8,128)(2,1)S(1)} %logit_grads_chunk.4.refs_0_.refs_3_), channel_id=1, source_target_pairs={{0,1},{1,0},{2,3},{3,2},{4,5},{5,4},{6,7},{7,6},{8,9},{9,8},{10,11... | collective-permute-start | bytes 4866056 | tf_op jit(solution)/shard_map/ppermute | solution.py:429
  109.7 15.6 %collective-permute-start.13 = (bf16[3168,256]{1,0:T(8,128)(2,1)S(1)}, bf16[3168,256]{1,0:T(8,128)(2,1)S(1)}, u32[]{:S(2)}, u32[]{:S(2)}) collective-permute-start(bf16[3168,256]{1,0:T(8,128)(2,1)S(1)} %logit_grads_chunk.3.refs_0_.refs_3_), channel_id=1, source_target_pairs={{0,1},{1,0},{2,3},{3,2},{4,5},{5,4},{6,7},{7,6},{8,9},{9,8},{10,11... | collective-permute-start | bytes 4866056 | tf_op jit(solution)/shard_map/ppermute | solution.py:429
  133.9 24.3 %collective-permute-start.16 = (bf16[256,1024]{1,0:T(8,128)(2,1)}, bf16[256,1024]{1,0:T(8,128)(2,1)}, u32[]{:S(2)}, u32[]{:S(2)}) collective-permute-start(bf16[256,1024]{1,0:T(8,128)(2,1)} %get-tuple-element.35.refs_1_), channel_id=1, source_target_pairs={{0,8},{8,0},{16,24},{24,16},{1,9},{9,1},{17,25},{25,17},{2,10},{10... | collective-permute-start | bytes 1572872 | tf_op jit(solution)/shard_map/ppermute | solution.py:429
  157.4 12.1 %collective-permute-start.19 = (bf16[256,768]{1,0:T(8,128)(2,1)S(1)}, bf16[256,768]{1,0:T(8,128)(2,1)S(1)}, u32[]{:S(2)}, u32[]{:S(2)}) collective-permute-start(bf16[256,768]{1,0:T(8,128)(2,1)S(1)} %get-tuple-element.39), channel_id=1, source_target_pairs={{0,8},{8,0},{16,24},{24,16},{1,9},{9,1},{17,25},{25,17},{2,10},{10... | collective-permute-start | bytes 1179656 | tf_op jit(solution)/shard_map/ppermute | solution.py:429
  159.5 12.0 %collective-permute-start.17 = (bf16[128,1024]{1,0:T(8,128)(2,1)S(1)}, bf16[128,1024]{1,0:T(8,128)(2,1)S(1)}, u32[]{:S(2)}, u32[]{:S(2)}) collective-permute-start(bf16[128,1024]{1,0:T(8,128)(2,1)S(1)} %dynamic-slice_convert_fusion), channel_id=1, source_target_pairs={{0,16},{8,24},{16,0},{24,8},{1,17},{9,25},{17,1},{25,9},{2,18},{10... | collective-permute-start | bytes 786440 | tf_op jit(solution)/shard_map/ppermute | solution.py:429
  170.3 11.1 %collective-permute-start.21 = (bf16[128,768]{1,0:T(8,128)(2,1)S(1)}, bf16[128,768]{1,0:T(8,128)(2,1)S(1)}, u32[]{:S(2)}, u32[]{:S(2)}) collective-permute-start(bf16[128,768]{1,0:T(8,128)(2,1)S(1)} %dynamic-slice_convert_fusion.1), channel_id=1, source_target_pairs={{0,16},{8,24},{16,0},{24,8},{1,17},{9,25},{17,1},{25,9},{2,18},{10... | collective-permute-start | bytes 589832 | tf_op jit(solution)/shard_map/ppermute | solution.py:429
  172.2 11.9 %collective-permute-start.18 = (bf16[128,1024]{1,0:T(8,128)(2,1)S(1)}, bf16[128,1024]{1,0:T(8,128)(2,1)S(1)}, u32[]{:S(2)}, u32[]{:S(2)}) collective-permute-start(bf16[128,1024]{1,0:T(8,128)(2,1)S(1)} %get-tuple-element.51), channel_id=1, source_target_pairs={{0,2},{2,0},{4,6},{6,4},{1,3},{3,1},{5,7},{7,5},{8,10},{10,8},{12,... | collective-permute-start | bytes 786440 | tf_op jit(solution)/shard_map/ppermute | solution.py:429
  182.0 10.3 %collective-permute-start.22 = (bf16[128,768]{1,0:T(8,128)(2,1)S(1)}, bf16[128,768]{1,0:T(8,128)(2,1)S(1)}, u32[]{:S(2)}, u32[]{:S(2)}) collective-permute-start(bf16[128,768]{1,0:T(8,128)(2,1)S(1)} %get-tuple-element.53), channel_id=1, source_target_pairs={{0,2},{2,0},{4,6},{6,4},{1,3},{3,1},{5,7},{7,5},{8,10},{10,8},{12,... | collective-permute-start | bytes 589832 | tf_op jit(solution)/shard_map/ppermute | solution.py:429
  184.8 19.4 %collective-permute-start.20 = (bf16[128,1024]{1,0:T(8,128)(2,1)S(1)}, bf16[128,1024]{1,0:T(8,128)(2,1)S(1)}, u32[]{:S(2)}, u32[]{:S(2)}) collective-permute-start(bf16[128,1024]{1,0:T(8,128)(2,1)S(1)} %get-tuple-element.47), channel_id=1, source_target_pairs={{0,4},{2,6},{4,0},{6,2},{1,5},{3,7},{5,1},{7,3},{8,12},{10,14},{12... | collective-permute-start | bytes 786440 | tf_op jit(solution)/shard_map/ppermute | solution.py:429
  193.0 17.3 %collective-permute-start.23 = (bf16[128,768]{1,0:T(8,128)(2,1)S(1)}, bf16[128,768]{1,0:T(8,128)(2,1)S(1)}, u32[]{:S(2)}, u32[]{:S(2)}) collective-permute-start(bf16[128,768]{1,0:T(8,128)(2,1)S(1)} %get-tuple-element.49), channel_id=1, source_target_pairs={{0,4},{2,6},{4,0},{6,2},{1,5},{3,7},{5,1},{7,3},{8,12},{10,14},{12... | collective-permute-start | bytes 589832 | tf_op jit(solution)/shard_map/ppermute | solution.py:429
  (28 other events, 150.9 us)

commit v2 on v1

--- a/solution.py
+++ b/solution.py
@@ -15,7 +15,6 @@
 TILE = 528
 ALL = 63
 UNREAD = pl.BlockSpec(memory_space=pl.ANY)
-SLICE = 48
 COLUMNS = 256
 
 
@@ -72,34 +71,25 @@
 
 
 def add_totals(parts, teacher_refs, state_ref, sub):
-    total = teacher_refs[0].shape[0]
-    size = tile_of(total, SLICE)
-    slices = [slice(at, at + size) for at in range(0, total, size)]
-
-    def load(rows):
-        student = parts[0][rows]
-        for part in parts[1:]:
-            student = student + part[rows]
-        target = jnp.concatenate([ref[rows] for ref in teacher_refs], axis=1).astype(F32)
-        return student, target
-
+    student = parts[0][...]
+    for part in parts[1:]:
+        student = student + part[...]
+    target = jnp.concatenate([ref[...] for ref in teacher_refs], axis=1).astype(F32)
     old = [state_ref[sub * r : sub * (r + 1)] for r in range(5)]
-    top_s, top_t = old[:2]
-    for rows in slices:
-        student, target = load(rows)
-        top_s = jnp.maximum(top_s, fold(jnp.maximum, student, sub))
-        top_t = jnp.maximum(top_t, fold(jnp.maximum, target, sub))
+    top_s = jnp.maximum(old[0], fold(jnp.maximum, student, sub))
+    top_t = jnp.maximum(old[1], fold(jnp.maximum, target, sub))
+    exp_s = jnp.exp(spread(jnp.subtract, student, top_s, sub))
+    exp_t = jnp.exp(spread(jnp.subtract, target, top_t, sub))
     scale_s = jnp.exp(old[0] - top_s)
     scale_t = jnp.exp(old[1] - top_t)
-    sum_s, sum_t, cross = old[2] * scale_s, old[3] * scale_t, old[4] * scale_t
-    for rows in slices:
-        student, target = load(rows)
-        exp_s = jnp.exp(spread(jnp.subtract, student, top_s, sub))
-        exp_t = jnp.exp(spread(jnp.subtract, target, top_t, sub))
-        sum_s += fold(jnp.add, exp_s, sub)
-        sum_t += fold(jnp.add, exp_t, sub)
-        cross += fold(jnp.add, exp_t * (target - student), sub)
-    for r, value in enumerate([top_s, top_t, sum_s, sum_t, cross]):
+    new = [
+        top_s,
+        top_t,
+        old[2] * scale_s + fold(jnp.add, exp_s, sub),
+        old[3] * scale_t + fold(jnp.add, exp_t, sub),
+        old[4] * scale_t + fold(jnp.add, exp_t * (target - student), sub),
+    ]
+    for r, value in enumerate(new):
         state_ref[sub * r : sub * (r + 1)] = value
 
 
@@ -161,7 +151,7 @@
         out_specs=whole(out),
         out_shape=jax.ShapeDtypeStruct(out, F32),
         scratch_shapes=[pltpu.VMEM((5 * sub, width), F32)],
-        compiler_params=params(ALL),
+        compiler_params=params(12),
         cost_estimate=cost(
             12 * rows * width, (4 * len(parts) + 2) * rows * width, 2 * rows * width
         ),
@@ -192,10 +182,9 @@
         turned_ref = refs.pop(0)
     head_ref, *out_refs = refs
     width = out_refs[0].shape[1]
+    full = jnp.dot(head_ref[...], turned_ref[...], preferred_element_type=F32)
     for k, out_ref in enumerate(out_refs):
-        out_ref[...] = jnp.dot(
-            head_ref[...], turned_ref[:, k * width : (k + 1) * width], preferred_element_type=F32
-        )
+        out_ref[...] = full[:, k * width : (k + 1) * width]
 
 
 def student_chunk(states, head_t, first, rows, owners, tokens, after):
@@ -330,65 +319,135 @@
     )(*parts, *teachers, coef)
 
 
-def hidden_body(count, after, has_acc, last, *refs):
-    refs = refs[after:]
+def turn(grads_refs, turned_ref):
+    for k, ref in enumerate(grads_refs):
+        width = ref.shape[1]
+        turned_ref[k * width : (k + 1) * width] = ref[...].T
+
+
+def put_waves(total, owners, out_refs):
+    waves = len(out_refs)
+    shard = total.shape[0] // (owners * waves)
+    for k in range(owners):
+        for w, out_ref in enumerate(out_refs):
+            at = (k * waves + w) * shard
+            out_ref[k * shard : (k + 1) * shard] = total[at : at + shard].astype(BF16)
+
+
+def hidden_body(count, has_acc, last, *refs):
     grads_refs, head_ref, *rest = (refs[:count], *refs[count:])
     before_ref = rest.pop(0) if has_acc else None
     *out_refs, turned_ref = rest
 
     @pl.when(pl.program_id(0) == 0)
     def _():
-        for k, ref in enumerate(grads_refs):
-            width = ref.shape[1]
-            turned_ref[k * width : (k + 1) * width] = ref[...].T
+        turn(grads_refs, turned_ref)
 
     total = jnp.dot(turned_ref[...], head_ref[...], preferred_element_type=F32)
     if has_acc:
         total = total + before_ref[...]
-    if not last:
+    if last:
+        *out_refs, flag_ref = out_refs
+        flag_ref[...] = jnp.zeros(flag_ref.shape, F32)
+        put_waves(total, count, out_refs)
+    else:
         out_refs[0][...] = total
-        return
-    waves = len(out_refs)
-    shard = total.shape[0] // (count * waves)
-    for k in range(count):
-        for w, out_ref in enumerate(out_refs):
-            at = (k * waves + w) * shard
-            out_ref[k * shard : (k + 1) * shard] = total[at : at + shard].astype(BF16)
-
-
-def hidden_chunk(grads, head_t, first, waves, tile, tiles, before, last, after):
+
+
+def hidden_width(depth):
+    return COLUMNS if depth % COLUMNS == 0 else 128
+
+
+def hidden_chunk(grads, head_t, first, waves, tiles, before, last):
     rows = grads[0].shape[0]
-    width = COLUMNS if head_t.shape[1] % COLUMNS == 0 else 128
+    width = hidden_width(head_t.shape[1])
     base = first // rows
     tokens = sum(g.shape[1] for g in grads)
     size = tiles * width
     pieces = waves if last else 1
     block = lambda count: pl.BlockSpec((count, width), lambda i: (0, i))
     has_acc = before is not None
+    flag = jax.ShapeDtypeStruct((8, 128), F32)
     return pl.pallas_call(
-        functools.partial(hidden_body, len(grads), len(after), has_acc, last),
+        functools.partial(hidden_body, len(grads), has_acc, last),
         grid=(tiles,),
-        in_specs=[UNREAD] * len(after)
-        + [whole(g.shape) for g in grads]
-        + [pl.BlockSpec((rows, width), lambda i: (base, i + tile))]
+        in_specs=[whole(g.shape) for g in grads]
+        + [pl.BlockSpec((rows, width), lambda i: (base, i))]
         + [block(tokens)] * has_acc,
-        out_specs=[block(tokens // pieces)] * pieces,
-        out_shape=[jax.ShapeDtypeStruct((tokens // pieces, size), BF16 if last else F32)] * pieces,
+        out_specs=[block(tokens // pieces)] * pieces + [whole(flag.shape)] * last,
+        out_shape=[jax.ShapeDtypeStruct((tokens // pieces, size), BF16 if last else F32)] * pieces
+        + [flag] * last,
         scratch_shapes=[pltpu.VMEM((tokens, rows), BF16)],
-        compiler_params=params(32),
+        compiler_params=params(30),
         cost_estimate=cost(2 * rows * tokens * size, 2 * rows * (size + tokens)),
         name="grad_hidden_chunk",
-    )(*after, *grads, head_t, *([before] if has_acc else []))
+    )(*grads, head_t, *([before] if has_acc else []))
+
+
+def hidden_rest_body(chunks, owners, *refs):
+    grads_refs, head_ref, *out_refs = refs[1 : 1 + chunks * owners], *refs[1 + chunks * owners :]
+    *out_refs, turned_ref, acc_ref = out_refs
+    tile, chunk = pl.program_id(0), pl.program_id(1)
+    for c in range(chunks):
+
+        @pl.when((tile == 0) & (chunk == c))
+        def _():
+            turn(grads_refs[c * owners : (c + 1) * owners], turned_ref.at[c])
+
+    term = jnp.dot(turned_ref[chunk], head_ref[...], preferred_element_type=F32)
+
+    @pl.when(chunk == 0)
+    def _():
+        acc_ref[...] = term
+
+    @pl.when(chunk > 0)
+    def _():
+        acc_ref[...] += term
+
+    @pl.when(chunk == chunks - 1)
+    def _():
+        put_waves(acc_ref[...], owners, out_refs)
+
+
+def hidden_rest(all_grads, head_t, waves, tile, tiles, flag):
+    chunks, owners = len(all_grads), len(all_grads[0])
+    grads = [g for chunk in all_grads for g in chunk]
+    rows, per_owner = grads[0].shape
+    tokens = owners * per_owner
+    width = hidden_width(head_t.shape[1])
+    size = tiles * width
+    full = lambda shape: pl.BlockSpec(shape, lambda i, c: (0, 0))
+    return pl.pallas_call(
+        functools.partial(hidden_rest_body, chunks, owners),
+        grid=(tiles, chunks),
+        in_specs=[UNREAD]
+        + [full(g.shape) for g in grads]
+        + [pl.BlockSpec((rows, width), lambda i, c: (c, i + tile))],
+        out_specs=[pl.BlockSpec((tokens // waves, width), lambda i, c: (0, i))] * waves,
+        out_shape=[jax.ShapeDtypeStruct((tokens // waves, size), BF16)] * waves,
+        scratch_shapes=[
+            pltpu.VMEM((chunks, tokens, rows), BF16),
+            pltpu.VMEM((tokens, width), F32),
+        ],
+        compiler_params=pltpu.CompilerParams(
+            dimension_semantics=("arbitrary", "arbitrary"), vmem_limit_bytes=38 * MIB
+        ),
+        cost_estimate=cost(
+            2 * chunks * rows * tokens * size, 2 * chunks * rows * (size + tokens)
+        ),
+        name="grad_hidden_rest",
+    )(flag, *grads, head_t)
 
 
 def head_body(count, after, *refs):
     hidden_ref, *refs = refs[after:]
     grads = jnp.concatenate([ref[...] for ref in refs[:count]], axis=1)
-    out_ref, flag_ref = refs[-2:]
+    out_ref, *flag_refs = refs[-3:]
 
     @pl.when(pl.program_id(0) == 0)
     def _():
-        flag_ref[...] = jnp.zeros(flag_ref.shape, F32)
+        for ref in flag_refs:
+            ref[...] = jnp.zeros(ref.shape, F32)
 
     for at in range(0, out_ref.shape[1], COLUMNS):
         lanes = slice(at, min(at + COLUMNS, out_ref.shape[1]))
@@ -397,7 +456,7 @@
         ).astype(BF16)
 
 
-def head_chunk(hidden, grads, first, skip, rows, total, before, after):
+def head_chunk(hidden, grads, first, skip, rows, total, before, after, widths):
     tokens, depth = hidden.shape
     tile = tile_of(rows, TILE)
     base = (first + skip) // tile
@@ -410,11 +469,10 @@
         functools.partial(head_body, len(grads), len(after)),
         grid=(rows // tile,),
         in_specs=specs,
-        out_specs=[pl.BlockSpec((tile, depth), lambda i: (i + base, 0)), whole((8, 128))],
-        out_shape=[
-            jax.ShapeDtypeStruct((total, depth), BF16),
-            jax.ShapeDtypeStruct((8, 128), F32),
-        ],
+        out_specs=[pl.BlockSpec((tile, depth), lambda i: (i + base, 0))]
+        + [whole((1, n)) for n in widths],
+        out_shape=[jax.ShapeDtypeStruct((total, depth), BF16)]
+        + [jax.ShapeDtypeStruct((1, n), F32) for n in widths],
         input_output_aliases=aliases,
         compiler_params=params(24),
         cost_estimate=cost(
@@ -434,7 +492,7 @@
     width = totals.shape[1] // waves
     step = 1
     while step < n:
-        span = min(4, n // step)
+        span = min(2, n // step)
         values = [totals] + [swap(totals, axis, k * step) for k in range(1, span)]
         shifts = tuple(k * step % waves if axis == "dp" else 0 for k in range(span))
         step *= span
@@ -467,20 +525,37 @@
         self.total = total
         return total
 
-    def over_vocab(self, step, flag):
-        n = lax.axis_size("vocab")
-        if n > 4:
-            if step == 1:
-                self.total = lax.psum(self.total, "vocab")
-        elif step < n:
+
+    def halve_vocab(self, flag):
+        if lax.axis_size("vocab") != 4:
+            self.total = lax.psum(self.total, "vocab")
+            return self.total
+        self.bit = lax.axis_index("vocab") % 2
+        half = self.shard // 2
+        sent = rows_at(self.total, 1 - self.bit, half).astype(BF16)
+        self.total = rows_at(self.total, self.bit, half) + late(swap(sent, "vocab", 1), flag)
+        return self.total
+
+    def cross_vocab(self, flag):
+        if lax.axis_size("vocab") == 4:
             sent = self.total.astype(BF16)
-            self.total = sent.astype(F32) + late(swap(sent, "vocab", step), flag)
+            self.total = sent.astype(F32) + late(swap(sent, "vocab", 2), flag)
+        return self.total
+
+    def join_vocab(self, flag):
+        if lax.axis_size("vocab") == 4:
+            sent = self.total.astype(BF16)
+            got, kept = late(swap(sent, "vocab", 1), flag), sent.astype(F32)
+            upper = self.bit == 1
+            self.total = jnp.concatenate(
+                [jnp.where(upper, got, kept), jnp.where(upper, kept, got)], axis=0
+            )
         return self.total
 
 
 def late(x, flag):
     x = x.astype(F32)
-    return x if flag is None else x + flag[0, 0]
+    return x if flag is None else x + flag
 
 
 def per_device(hidden, head_weight, teacher_logits, response_start):
@@ -552,41 +627,39 @@
     for c in range(len(chunks)):
         all_grads.append(exchanged([grads_chunk(parts[c], teachers[c], coef)] * n_mp))
 
-    tiles = depth // (COLUMNS if depth % COLUMNS == 0 else 128)
+    width = hidden_width(depth)
+    tiles = depth // width
     split = (tiles + 1) // 2
-    reductions = []
-    outs = []
-    for at, count in ((0, split), (split, tiles - split)):
-        acc, after = None, outs
-        for c, (first, rows) in enumerate(chunks):
-            last = c == len(chunks) - 1
-            outs = hidden_chunk(
-                all_grads[c], head_t, first, waves, at, count, acc, last, after
-            )
-            acc, after = outs[0], []
-        reductions.append(Reduction(outs, shard, own))
-
-    one, two = reductions
+    acc = None
+    for c, (first, rows) in enumerate(chunks):
+        last = c == len(chunks) - 1
+        outs = hidden_chunk(all_grads[c], head_t, first, waves, split, acc, last)
+        acc = outs[0]
+    *outs, flag = outs
+    one = Reduction(outs, shard, own)
+    two = Reduction(hidden_rest(all_grads, head_t, waves, split, tiles - split, flag), shard, own)
+
     results = [one.over_inner(None)]
     plan = [
-        lambda flag: [one.over_outer(flag), two.over_inner(flag)],
-        lambda flag: [one.over_vocab(1, flag), two.over_outer(flag)],
-        lambda flag: [one.over_vocab(2, flag), two.over_vocab(1, flag)],
-        lambda flag: [one.total, two.over_vocab(2, flag)],
+        lambda f, g: [one.over_outer(f), two.over_inner(g)],
+        lambda f, g: [one.halve_vocab(f), two.over_outer(g)],
+        lambda f, g: [one.cross_vocab(f), two.halve_vocab(g)],
+        lambda f, g: [one.join_vocab(f), two.cross_vocab(g)],
     ]
+    widths = (split * width, depth - split * width)
     calls = [(c, 0, rows) for c, (_, rows) in enumerate(chunks)]
     if calls[-1][2] % (2 * TILE) == 0:
         c, _, rows = calls.pop()
         calls += [(c, 0, rows // 2), (c, rows // 2, rows // 2)]
     grad_head = None
     for c, skip, rows in calls:
-        grad_head, flag = head_chunk(
-            ordered, all_grads[c], chunks[c][0], skip, rows, columns, grad_head, results
+        grad_head, *flags = head_chunk(
+            ordered, all_grads[c], chunks[c][0], skip, rows, columns, grad_head, results, widths
         )
-        results = plan.pop(0)(flag)
+        results = plan.pop(0)(*flags)
     while plan:
-        results = plan.pop(0)(flag)
-    grad_hidden = jnp.concatenate(results, axis=1)
+        results = plan.pop(0)(*flags)
+    grad_hidden = jnp.concatenate([one.total, two.join_vocab(None)], axis=1)
     return (token_kl.reshape(own_rows), grad_hidden, grad_head.T)
 
 

time: 213 us -> 218 us (1.023)
  Pallas kernels: 135 us -> 125 us
  local copies, waits for them, and re-layouts: 17 us -> 23.1 us
  other arithmetic: 7.35 us -> 13 us
  waiting for transfers between devices: 25.9 us -> 29.1 us
    pallas_call x3, Pallas kernels: 18.4 us -> 12.8 us  [totals_chunk(): pl.pallas_call(functools.partial(totals_body, len(parts), len(teachers),...]
    unnamed x56 -> x84, local copies, waits for them, and re-layouts: 9.89 us -> 15.1 us
    ppermute x24, waiting for transfers between devices: 25.9 us -> 29.1 us  [swap(): return lax.ppermute(x, axis, [(i, i ^ k) for i in range(n)])]
    pallas_call x3, Pallas kernels: 11.9 us -> 8.73 us  [grads_chunk(): pl.pallas_call(functools.partial(grads_body, len(parts)), grid=(rows // t...]
    convert_element_type x4, other arithmetic: 2.87 us -> 5.93 us  [the longest x2 3.35 us: cross_vocab(): sent = self.total.astype(BF16)]
    pallas_call x6 -> x4, Pallas kernels: 41.2 us -> 39.8 us  [the longest x3 23.8 us: hidden_chunk(): pl.pallas_call(functools.partial(hidden_body, len(grads), has_acc, last),...]
  transfers between devices with their start and end apart: 24 -> 24, of which waited for: 7 -> 8; matrix products, arithmetic and copies ran while one was open for 6% -> 8% of each run, Pallas kernels for 49% -> 39%
where the time goes in v2:
time: 218 us; the launch traced here: 217 us
  Pallas kernels  125 us (57%)
  waiting for transfers between devices  29.1 us (13%)
  starting transfers between devices  26.1 us (12%)
  local copies, waits for them, and re-layouts  23.1 us (11%)
  other arithmetic  13 us (6%)
    pallas_call x3, Pallas kernels, student_chunk(): pl.pallas_call(functools.partial(student_body, owners, places, len(after)...  36.4 us
    ppermute x24, waiting for transfers between devices, swap(): return lax.ppermute(x, axis, [(i, i ^ k) for i in range(n)])  29.1 us
    pallas_call x4, Pallas kernels, head_chunk(): pl.pallas_call(functools.partial(head_body, len(grads), len(after)), grid...  26.7 us
    ppermute x24, starting transfers between devices, swap(): return lax.ppermute(x, axis, [(i, i ^ k) for i in range(n)])  26.1 us
    pallas_call x3, Pallas kernels, hidden_chunk(): pl.pallas_call(functools.partial(hidden_body, len(grads), has_acc, last),...  23.8 us
    pallas_call x1, Pallas kernels, hidden_rest(): pl.pallas_call(functools.partial(hidden_rest_body, chunks, owners), grid=...  16 us
    unnamed x84, local copies, waits for them, and re-layouts  15.1 us
    pallas_call x3, Pallas kernels, totals_chunk(): pl.pallas_call(functools.partial(totals_body, len(parts), len(teachers),...  12.8 us
  transfers between devices with their start and end apart: 24, of which 8 were waited for; matrix products, arithmetic and copies ran while one was open for 8% of the time, Pallas kernels for 39%

profile of v2, /device:TPU:0, one launch (start us, length us, event | category | flops | bytes accessed | tf_op | source)
XLA Modules:
  0.0 217.0 jit_solution(150380934345510272)
XLA Ops:
  0.6 3.0 %collective-permute-start.1 = (bf16[128,1792]{1,0:T(8,128)(2,1)}, bf16[128,1792]{1,0:T(8,128)(2,1)S(1)}, u32[]{:S(2)}, u32[]{:S(2)}) collective-permute-start(bf16[128,1792]{1,0:T(8,128)(2,1)} %refs_7_.1), channel_id=1, source_target_pairs={{0,16},{8,24},{16,0},{24,8},{1,17},{9,25},{17,1},{25,9},{2,18},{10... | collective-permute-start | bytes 1376264 | tf_op jit(solution)/shard_map/ppermute | solution.py:487
  5.2 9.2 %collective-permute-done.1.refs_9_ = bf16[128,1792]{1,0:T(8,128)(2,1)S(1)} collective-permute-done((bf16[128,1792]{1,0:T(8,128)(2,1)}, bf16[128,1792]{1,0:T(8,128)(2,1)S(1)}, u32[]{:S(2)}, u32[]{:S(2)}) %collective-permute-start.1) | collective-permute-done | bytes 458784 | tf_op jit(solution)/shard_map/ppermute | solution.py:487
  17.8 4.7 %dynamic-slice_bitcast_fusion = (bf16[3168,128]{1,0:T(8,128)(2,1)}, bf16[3168,128]{1,0:T(8,128)(2,1)}, bf16[3168,128]{1,0:T(8,128)(2,1)}, bf16[3168,128]{1,0:T(8...) fusion(bf16[256,9504]{0,1:T(8,128)(2,1)} %param.6, s32[]{:T(128)S(6)} %select_n.97, s32[]{:T(128)S(6)} %select_n.96), kind=kLoop, calls=%fused_computation.2 | loop fusion | bytes 9732104 | tf_op jit(solution)/shard_map/dynamic_slice | solution.py:585
  23.9 12.9 %student_chunk.3 = (f32[3168,256]{1,0:T(8,128)}, f32[3168,256]{1,0:T(8,128)}, bf16[512,1792]{1,0:T(8,128)(2,1)}, bf16[1792,512]{1,0:T(8,128)(2,1)}) custom-call(bf16[3168,128]{1,0:T(8,128)(2,1)} %get-tuple-element.67.refs_0_.refs_2_, bf16[3168,128]{1,0:T(8,128)(2,1)} %get-tuple-element.66.refs_1_.refs_3_, bf16[3168,128]{1,0:T(8,128)(2,1)} %get-tuple-element.65.refs_2_, ...), custom_call_target="tpu_custom_call" | custom-call | flops 363331584 | bytes 1229824 | tf_op jit(solution)/shard_map/student_chunk/pallas_call | solution.py:209
  36.8 11.8 %student_chunk.5 = (f32[3168,256]{1,0:T(8,128)}, f32[3168,256]{1,0:T(8,128)}) custom-call(bf16[1792,512]{1,0:T(8,128)(2,1)} %get-tuple-element.30.refs_0_, bf16[9504,1792]{1,0:T(8,128)(2,1)} %bitcast.33), custom_call_target="tpu_custom_call" | custom-call | flops 363331584 | bytes 1229824 | tf_op jit(solution)/shard_map/student_chunk/pallas_call | solution.py:209
  49.1 11.8 %student_chunk.4 = (f32[3168,256]{1,0:T(8,128)}, f32[3168,256]{1,0:T(8,128)}) custom-call(bf16[1792,512]{1,0:T(8,128)(2,1)} %get-tuple-element.30.refs_0_, bf16[9504,1792]{1,0:T(8,128)(2,1)} %bitcast.34), custom_call_target="tpu_custom_call" | custom-call | flops 363331584 | bytes 1229824 | tf_op jit(solution)/shard_map/student_chunk/pallas_call | solution.py:209
  65.1 5.2 %totals_chunk.3.refs_4_ = f32[40,256]{1,0:T(8,128)S(1)} custom-call(f32[3168,256]{1,0:T(8,128)S(1)} %copy-done.14, f32[3168,256]{1,0:T(8,128)} %collective-permute-done.6.refs_1_, bf16[3168,128]{1,0:T(8,128)(2,1)S(1)} %copy-done.26, bf16[3168,128]{1,0:T(8,128)(2,1)S(1)} %copy-done.24, f32[40,256]{1,0:T(8,128)S(1)} %copy-done.35), custom_call_target="tpu_custom_call" | custom-call | flops 608256 | bytes 506880 | tf_op jit(solution)/shard_map/totals_chunk/pallas_call | solution.py:147
  70.4 5.1 %totals_chunk.4.refs_4_ = f32[40,256]{1,0:T(8,128)S(1)} custom-call(f32[3168,256]{1,0:T(8,128)S(1)} %copy-done.16, f32[3168,256]{1,0:T(8,128)} %collective-permute-done.5.refs_1_, bf16[3168,128]{1,0:T(8,128)(2,1)S(1)} %copy-done.23, bf16[3168,128]{1,0:T(8,128)(2,1)S(1)} %copy-done.22, f32[40,256]{1,0:T(8,128)S(1)} %totals_chunk.3.refs_4_), custom_call_target="tpu_custom_call" | custom-call | flops 608256 | bytes 506880 | tf_op jit(solution)/shard_map/totals_chunk/pallas_call | solution.py:147
  78.8 3.1 %collective-permute-done.7.refs_1_ = f32[8,256]{1,0:T(8,128)S(1)} collective-permute-done((f32[8,256]{1,0:T(8,128)S(1)}, f32[8,256]{1,0:T(8,128)S(1)}, u32[]{:S(2)}, u32[]{:S(2)}) %collective-permute-start.7) | collective-permute-done | bytes 8224 | tf_op jit(solution)/shard_map/ppermute | solution.py:487
  82.8 2.8 %collective-permute-done.8.refs_1_ = f32[8,256]{1,0:T(8,128)S(1)} collective-permute-done((f32[8,256]{1,0:T(8,128)S(1)}, f32[8,256]{1,0:T(8,128)S(1)}, u32[]{:S(2)}, u32[]{:S(2)}) %collective-permute-start.8) | collective-permute-done | bytes 8224 | tf_op jit(solution)/shard_map/ppermute | solution.py:487
  89.3 2.7 %collective-permute-start.10 = (f32[8,256]{1,0:T(8,128)S(1)}, f32[8,256]{1,0:T(8,128)S(1)}, u32[]{:S(2)}, u32[]{:S(2)}) collective-permute-start(f32[8,256]{1,0:T(8,128)S(1)} %merge_totals.5.refs_0_), channel_id=1, source_target_pairs={{0,4},{2,6},{4,0},{6,2},{1,5},{3,7},{5,1},{7,3},{8,12},{10,14},{12... | collective-permute-start | bytes 24584 | tf_op jit(solution)/shard_map/ppermute | solution.py:487
  94.0 3.4 %logit_grads_chunk.5.refs_0_.refs_2_.refs_1_ = bf16[3168,256]{1,0:T(8,128)(2,1)S(1)} custom-call(f32[3168,256]{1,0:T(8,128)S(1)} %copy-done.15, f32[3168,256]{1,0:T(8,128)} %collective-permute-done.6.refs_1_, bf16[3168,128]{1,0:T(8,128)(2,1)S(1)} %copy-done.27, bf16[3168,128]{1,0:T(8,128)(2,1)S(1)} %copy-done.25, f32[8,256]{1,0:T(8,128)S(1)} %get-tuple-element.38.refs_4_), custom_call_target="tpu_custom_call" | custom-call | flops 405504 | bytes 608256 | tf_op jit(solution)/shard_map/logit_grads_chunk/pallas_call | solution.py:308
  97.5 4.0 %logit_grads_chunk.4.refs_0_.refs_3_ = bf16[3168,256]{1,0:T(8,128)(2,1)S(1)} custom-call(f32[3168,256]{1,0:T(8,128)S(1)} %copy-done.16, f32[3168,256]{1,0:T(8,128)} %collective-permute-done.5.refs_1_, bf16[3168,128]{1,0:T(8,128)(2,1)S(1)} %copy-done.23, bf16[3168,128]{1,0:T(8,128)(2,1)S(1)} %copy-done.22, f32[8,256]{1,0:T(8,128)S(1)} %get-tuple-element.38.refs_4_), custom_call_target="tpu_custom_call" | custom-call | flops 405504 | bytes 608256 | tf_op jit(solution)/shard_map/logit_grads_chunk/pallas_call | solution.py:308
  103.5 7.7 %grad_hidden_chunk.3.refs_3_ = f32[512,1024]{1,0:T(8,128)S(1)} custom-call(bf16[3168,256]{1,0:T(8,128)(2,1)S(1)} %logit_grads_chunk.5.refs_0_.refs_2_.refs_1_, bf16[3168,256]{1,0:T(8,128)(2,1)S(1)} %collective-permute-done.13.refs_1_.refs_3_.refs_2_, bf16[9504,1792]{1,0:T(8,128)(2,1)} %bitcast.35), custom_call_target="tpu_custom_call" | custom-call | flops 207618048 | bytes 608256 | tf_op jit(solution)/shard_map/grad_hidden_chunk/pallas_call | solution.py:371
  111.2 7.7 %grad_hidden_chunk.4.refs_3_ = f32[512,1024]{1,0:T(8,128)S(1)} custom-call(bf16[3168,256]{1,0:T(8,128)(2,1)S(1)} %logit_grads_chunk.4.refs_0_.refs_3_, bf16[3168,256]{1,0:T(8,128)(2,1)S(1)} %collective-permute-done.12.refs_1_.refs_4_, bf16[9504,1792]{1,0:T(8,128)(2,1)} %bitcast.36, f32[512,1024]{1,0:T(8,128)S(1)} %grad_hidden_chunk.3.refs_3_), custom_call_target="tpu_custom_call" | custom-call | flops 207618048 | bytes 608256 | tf_op jit(solution)/shard_map/grad_hidden_chunk/pallas_call | solution.py:371
  119.0 8.4 %grad_hidden_chunk.5 = (bf16[256,1024]{1,0:T(8,128)(2,1)S(1)}, bf16[256,1024]{1,0:T(8,128)(2,1)}, f32[8,128]{1,0:T(8,128)S(1)}) custom-call(bf16[3168,256]{1,0:T(8,128)(2,1)S(1)} %logit_grads_chunk.3.refs_0_.refs_5_.refs_3_, bf16[3168,256]{1,0:T(8,128)(2,1)S(1)} %collective-permute-done.11.refs_1_.refs_6_.refs_4_, bf16[9504,1792]{1,0:T(8,128)(2,1)} %bitcast.37, ...), custom_call_target="tpu_custom_call" | custom-call | flops 207618048 | bytes 608256 | tf_op jit(solution)/shard_map/grad_hidden_chunk/pallas_call | solution.py:371
  134.7 16.0 %grad_hidden_rest.1 = (bf16[256,768]{1,0:T(8,128)(2,1)S(1)}, bf16[256,768]{1,0:T(8,128)(2,1)}) custom-call(f32[8,128]{1,0:T(8,128)S(1)} %get-tuple-element.43.refs_0_, bf16[3168,256]{1,0:T(8,128)(2,1)S(1)} %copy-done.8, bf16[3168,256]{1,0:T(8,128)(2,1)S(1)} %copy-done.13, bf16[3168,256]{1,0:T(8,128)(2,1)S(1)} %copy-done.5, bf16[3168,256]{1,0:T(8,128)(2,1)S(1)} %copy-done.10, ...), custom_call_target="tpu_custom_call" | custom-call | flops 467140608 | bytes 1520640 | tf_op jit(solution)/shard_map/grad_hidden_rest/pallas_call | solution.py:420
  155.0 8.5 %grad_head_chunk.4 = (bf16[9504,1792]{1,0:T(8,128)(2,1)}, f32[1,1024]{1,0:T(1,128)S(1)}, f32[1,768]{1,0:T(1,128)S(1)}) custom-call(f32[256,1024]{1,0:T(8,128)S(1)} %convert_add_fusion.refs_0_, bf16[512,1792]{1,0:T(8,128)(2,1)S(1)} %copy-done, bf16[3168,256]{1,0:T(8,128)(2,1)S(1)} %copy-done.8, bf16[3168,256]{1,0:T(8,128)(2,1)S(1)} %copy-done.13), custom_call_target="tpu_custom_call" | custom-call | flops 363331584 | bytes 1027072 | tf_op jit(solution)/shard_map/grad_head_chunk/pallas_call | solution.py:468
  170.5 8.5 %grad_head_chunk.5 = (bf16[9504,1792]{1,0:T(8,128)(2,1)}, f32[1,1024]{1,0:T(1,128)S(1)}, f32[1,768]{1,0:T(1,128)S(1)}) custom-call(f32[128,1024]{1,0:T(8,128)S(1)} %add_add_fusion.1.refs_0_, f32[256,768]{1,0:T(8,128)S(1)} %add_add_fusion.refs_1_, bf16[512,1792]{1,0:T(8,128)(2,1)S(1)} %copy-done, ...), custom_call_target="tpu_custom_call", output_to_operand_aliasing={{0}: (5, {})} | custom-call | flops 363331584 | bytes 1027072 | tf_op jit(solution)/shard_map/grad_head_chunk/pallas_call | solution.py:468
  184.5 4.9 %grad_head_chunk.6 = (bf16[9504,1792]{1,0:T(8,128)(2,1)}, f32[1,1024]{1,0:T(1,128)S(1)}, f32[1,768]{1,0:T(1,128)S(1)}) custom-call(f32[64,1024]{1,0:T(8,128)S(1)} %get-tuple-element.60.refs_0_, f32[128,768]{1,0:T(8,128)S(1)} %add_add_fusion.2.refs_1_, bf16[512,1792]{1,0:T(8,128)(2,1)S(1)} %copy-done, ...), custom_call_target="tpu_custom_call", output_to_operand_aliasing={{0}: (5, {})} | custom-call | flops 181665792 | bytes 570880 | tf_op jit(solution)/shard_map/grad_head_chunk/pallas_call | solution.py:468
  189.4 2.7 %collective-permute-start.18 = (bf16[64,1024]{1,0:T(8,128)(2,1)}, bf16[64,1024]{1,0:T(8,128)(2,1)S(1)}, u32[]{:S(2)}, u32[]{:S(2)}) collective-permute-start(bf16[64,1024]{1,0:T(8,128)(2,1)} %get-tuple-element.59), channel_id=1, source_target_pairs={{0,4},{2,6},{4,0},{6,2},{1,5},{3,7},{5,1},{7,3},{8,12},{10,14},{12... | collective-permute-start | bytes 393224 | tf_op jit(solution)/shard_map/ppermute | solution.py:487
  194.0 4.6 %collective-permute-done.18 = bf16[64,1024]{1,0:T(8,128)(2,1)S(1)} collective-permute-done((bf16[64,1024]{1,0:T(8,128)(2,1)}, bf16[64,1024]{1,0:T(8,128)(2,1)S(1)}, u32[]{:S(2)}, u32[]{:S(2)}) %collective-permute-start.18) | collective-permute-done | bytes 131104 | tf_op jit(solution)/shard_map/ppermute | solution.py:487
  201.7 4.9 %grad_head_chunk.7 = (bf16[9504,1792]{1,0:T(8,128)(2,1)}, f32[1,1024]{1,0:T(1,128)S(1)}, f32[1,768]{1,0:T(1,128)S(1)}) custom-call(f32[64,1024]{1,0:T(8,128)S(1)} %get-tuple-element.58.refs_0_, f32[64,768]{1,0:T(8,128)S(1)} %get-tuple-element.62.refs_1_, bf16[512,1792]{1,0:T(8,128)(2,1)S(1)} %copy-done, ...), custom_call_target="tpu_custom_call", output_to_operand_aliasing={{0}: (5, {})} | custom-call | flops 181665792 | bytes 570880 | tf_op jit(solution)/shard_map/grad_head_chunk/pallas_call | solution.py:468
  209.7 3.3 %collective-permute-done.23 = bf16[64,768]{1,0:T(8,128)(2,1)S(1)} collective-permute-done((bf16[64,768]{1,0:T(8,128)(2,1)S(1)}, bf16[64,768]{1,0:T(8,128)(2,1)S(1)}, u32[]{:S(2)}, u32[]{:S(2)}) %collective-permute-start.23) | collective-permute-done | bytes 98336 | tf_op jit(solution)/shard_map/ppermute | solution.py:487
  (159 shorter events, 59.2 us)
Async XLA Ops:
  0.6 13.8 %collective-permute-start.1 = (bf16[128,1792]{1,0:T(8,128)(2,1)}, bf16[128,1792]{1,0:T(8,128)(2,1)S(1)}, u32[]{:S(2)}, u32[]{:S(2)}) collective-permute-start(bf16[128,1792]{1,0:T(8,128)(2,1)} %refs_7_.1), channel_id=1, source_target_pairs={{0,16},{8,24},{16,0},{24,8},{1,17},{9,25},{17,1},{25,9},{2,18},{10... | collective-permute-start | bytes 1376264 | tf_op jit(solution)/shard_map/ppermute | solution.py:487
  3.7 12.5 %collective-permute-start = (bf16[128,1792]{1,0:T(8,128)(2,1)}, bf16[128,1792]{1,0:T(8,128)(2,1)S(1)}, u32[]{:S(2)}, u32[]{:S(2)}) collective-permute-start(bf16[128,1792]{1,0:T(8,128)(2,1)} %refs_7_.1), channel_id=1, source_target_pairs={{0,8},{8,0},{16,24},{24,16},{1,9},{9,1},{17,25},{25,17},{2,10},{10... | collective-permute-start | bytes 1376264 | tf_op jit(solution)/shard_map/ppermute | solution.py:487
  14.4 8.1 %collective-permute-start.2 = (bf16[64,1792]{1,0:T(8,128)(2,1)S(1)}, bf16[64,1792]{1,0:T(8,128)(2,1)S(1)}, u32[]{:S(2)}, u32[]{:S(2)}) collective-permute-start(bf16[64,1792]{1,0:T(8,128)(2,1)S(1)} %slice.16), channel_id=1, source_target_pairs={{0,8},{8,0},{16,24},{24,16},{1,9},{9,1},{17,25},{25,17},{2,10},{10... | collective-permute-start | bytes 688136 | tf_op jit(solution)/shard_map/ppermute | solution.py:487
  16.2 6.3 %collective-permute-start.3 = (bf16[64,1792]{1,0:T(8,128)(2,1)S(1)}, bf16[64,1792]{1,0:T(8,128)(2,1)S(1)}, u32[]{:S(2)}, u32[]{:S(2)}) collective-permute-start(bf16[64,1792]{1,0:T(8,128)(2,1)S(1)} %slice.17), channel_id=1, source_target_pairs={{0,16},{8,24},{16,0},{24,8},{1,17},{9,25},{17,1},{25,9},{2,18},{10... | collective-permute-start | bytes 688136 | tf_op jit(solution)/shard_map/ppermute | solution.py:487
  48.6 21.7 %collective-permute-start.5 = (f32[3168,256]{1,0:T(8,128)}, f32[3168,256]{1,0:T(8,128)}, u32[]{:S(2)}, u32[]{:S(2)}) collective-permute-start(f32[3168,256]{1,0:T(8,128)} %get-tuple-element.34), channel_id=1, source_target_pairs={{0,1},{1,0},{2,3},{3,2},{4,5},{5,4},{6,7},{7,6},{8,9},{9,8},{10,11... | collective-permute-start | bytes 9732104 | tf_op jit(solution)/shard_map/ppermute | solution.py:487
  48.6 12.3 %collective-permute-start.6 = (f32[3168,256]{1,0:T(8,128)}, f32[3168,256]{1,0:T(8,128)}, u32[]{:S(2)}, u32[]{:S(2)}) collective-permute-start(f32[3168,256]{1,0:T(8,128)} %get-tuple-element.36), channel_id=1, source_target_pairs={{0,1},{1,0},{2,3},{3,2},{4,5},{5,4},{6,7},{7,6},{8,9},{9,8},{10,11... | collective-permute-start | bytes 9732104 | tf_op jit(solution)/shard_map/ppermute | solution.py:487
  60.8 14.7 %collective-permute-start.4 = (f32[3168,256]{1,0:T(8,128)}, f32[3168,256]{1,0:T(8,128)S(1)}, u32[]{:S(2)}, u32[]{:S(2)}) collective-permute-start(f32[3168,256]{1,0:T(8,128)} %get-tuple-element.32), channel_id=1, source_target_pairs={{0,1},{1,0},{2,3},{3,2},{4,5},{5,4},{6,7},{7,6},{8,9},{9,8},{10,11... | collective-permute-start | bytes 9732104 | tf_op jit(solution)/shard_map/ppermute | solution.py:487
  78.1 3.7 %collective-permute-start.7 = (f32[8,256]{1,0:T(8,128)S(1)}, f32[8,256]{1,0:T(8,128)S(1)}, u32[]{:S(2)}, u32[]{:S(2)}) collective-permute-start(f32[8,256]{1,0:T(8,128)S(1)} %totals_chunk.5.refs_0_), channel_id=1, source_target_pairs={{0,8},{8,0},{16,24},{24,16},{1,9},{9,1},{17,25},{25,17},{2,10},{10... | collective-permute-start | bytes 24584 | tf_op jit(solution)/shard_map/ppermute | solution.py:487
  81.9 3.7 %collective-permute-start.8 = (f32[8,256]{1,0:T(8,128)S(1)}, f32[8,256]{1,0:T(8,128)S(1)}, u32[]{:S(2)}, u32[]{:S(2)}) collective-permute-start(f32[8,256]{1,0:T(8,128)S(1)} %merge_totals.3.refs_0_), channel_id=1, source_target_pairs={{0,16},{8,24},{16,0},{24,8},{1,17},{9,25},{17,1},{25,9},{2,18},{10... | collective-permute-start | bytes 24584 | tf_op jit(solution)/shard_map/ppermute | solution.py:487
  85.6 3.7 %collective-permute-start.9 = (f32[8,256]{1,0:T(8,128)S(1)}, f32[8,256]{1,0:T(8,128)S(1)}, u32[]{:S(2)}, u32[]{:S(2)}) collective-permute-start(f32[8,256]{1,0:T(8,128)S(1)} %merge_totals.4.refs_0_), channel_id=1, source_target_pairs={{0,2},{2,0},{4,6},{6,4},{1,3},{3,1},{5,7},{7,5},{8,10},{10,8},{12,... | collective-permute-start | bytes 24584 | tf_op jit(solution)/shard_map/ppermute | solution.py:487
  89.3 4.6 %collective-permute-start.10 = (f32[8,256]{1,0:T(8,128)S(1)}, f32[8,256]{1,0:T(8,128)S(1)}, u32[]{:S(2)}, u32[]{:S(2)}) collective-permute-start(f32[8,256]{1,0:T(8,128)S(1)} %merge_totals.5.refs_0_), channel_id=1, source_target_pairs={{0,4},{2,6},{4,0},{6,2},{1,5},{3,7},{5,1},{7,3},{8,12},{10,14},{12... | collective-permute-start | bytes 24584 | tf_op jit(solution)/shard_map/ppermute | solution.py:487
  97.4 6.1 %collective-permute-start.13 = (bf16[3168,256]{1,0:T(8,128)(2,1)S(1)}, bf16[3168,256]{1,0:T(8,128)(2,1)S(1)}, u32[]{:S(2)}, u32[]{:S(2)}) collective-permute-start(bf16[3168,256]{1,0:T(8,128)(2,1)S(1)} %logit_grads_chunk.5.refs_0_.refs_2_.refs_1_), channel_id=1, source_target_pairs={{0,1},{1,0},{2,3},{3,2},{4,5},{5,4},{6,7},{7,6},{8,9},{9,8},{10,11... | collective-permute-start | bytes 4866056 | tf_op jit(solution)/shard_map/ppermute | solution.py:487
  101.5 9.7 %collective-permute-start.12 = (bf16[3168,256]{1,0:T(8,128)(2,1)S(1)}, bf16[3168,256]{1,0:T(8,128)(2,1)S(1)}, u32[]{:S(2)}, u32[]{:S(2)}) collective-permute-start(bf16[3168,256]{1,0:T(8,128)(2,1)S(1)} %logit_grads_chunk.4.refs_0_.refs_3_), channel_id=1, source_target_pairs={{0,1},{1,0},{2,3},{3,2},{4,5},{5,4},{6,7},{7,6},{8,9},{9,8},{10,11... | collective-permute-start | bytes 4866056 | tf_op jit(solution)/shard_map/ppermute | solution.py:487
  103.0 16.0 %collective-permute-start.11 = (bf16[3168,256]{1,0:T(8,128)(2,1)S(1)}, bf16[3168,256]{1,0:T(8,128)(2,1)S(1)}, u32[]{:S(2)}, u32[]{:S(2)}) collective-permute-start(bf16[3168,256]{1,0:T(8,128)(2,1)S(1)} %logit_grads_chunk.3.refs_0_.refs_5_.refs_3_), channel_id=1, source_target_pairs={{0,1},{1,0},{2,3},{3,2},{4,5},{5,4},{6,7},{7,6},{8,9},{9,8},{10,11... | collective-permute-start | bytes 4866056 | tf_op jit(solution)/shard_map/ppermute | solution.py:487
  128.2 23.9 %collective-permute-start.14 = (bf16[256,1024]{1,0:T(8,128)(2,1)}, bf16[256,1024]{1,0:T(8,128)(2,1)}, u32[]{:S(2)}, u32[]{:S(2)}) collective-permute-start(bf16[256,1024]{1,0:T(8,128)(2,1)} %get-tuple-element.40), channel_id=1, source_target_pairs={{0,8},{8,0},{16,24},{24,16},{1,9},{9,1},{17,25},{25,17},{2,10},{10... | collective-permute-start | bytes 1572872 | tf_op jit(solution)/shard_map/ppermute | solution.py:487
  150.7 12.8 %collective-permute-start.17 = (bf16[256,768]{1,0:T(8,128)(2,1)}, bf16[256,768]{1,0:T(8,128)(2,1)}, u32[]{:S(2)}, u32[]{:S(2)}) collective-permute-start(bf16[256,768]{1,0:T(8,128)(2,1)} %get-tuple-element.45), channel_id=1, source_target_pairs={{0,8},{8,0},{16,24},{24,16},{1,9},{9,1},{17,25},{25,17},{2,10},{10... | collective-permute-start | bytes 1179656 | tf_op jit(solution)/shard_map/ppermute | solution.py:487
  154.2 12.7 %collective-permute-start.15 = (bf16[128,1024]{1,0:T(8,128)(2,1)}, bf16[128,1024]{1,0:T(8,128)(2,1)}, u32[]{:S(2)}, u32[]{:S(2)}) collective-permute-start(bf16[128,1024]{1,0:T(8,128)(2,1)} %dynamic-slice_convert_fusion), channel_id=1, source_target_pairs={{0,16},{8,24},{16,0},{24,8},{1,17},{9,25},{17,1},{25,9},{2,18},{10... | collective-permute-start | bytes 786440 | tf_op jit(solution)/shard_map/ppermute | solution.py:487
  165.7 13.3 %collective-permute-start.19 = (bf16[128,768]{1,0:T(8,128)(2,1)}, bf16[128,768]{1,0:T(8,128)(2,1)}, u32[]{:S(2)}, u32[]{:S(2)}) collective-permute-start(bf16[128,768]{1,0:T(8,128)(2,1)} %dynamic-slice_convert_fusion.1), channel_id=1, source_target_pairs={{0,16},{8,24},{16,0},{24,8},{1,17},{9,25},{17,1},{25,9},{2,18},{10... | collective-permute-start | bytes 589832 | tf_op jit(solution)/shard_map/ppermute | solution.py:487
  168.9 12.5 %collective-permute-start.16 = (bf16[64,1024]{1,0:T(8,128)(2,1)}, bf16[64,1024]{1,0:T(8,128)(2,1)}, u32[]{:S(2)}, u32[]{:S(2)}) collective-permute-start(bf16[64,1024]{1,0:T(8,128)(2,1)} %dynamic-slice_convert_fusion.2), channel_id=1, source_target_pairs={{0,2},{2,0},{4,6},{6,4},{1,3},{3,1},{5,7},{7,5},{8,10},{10,8},{12,... | collective-permute-start | bytes 393224 | tf_op jit(solution)/shard_map/ppermute | solution.py:487
  180.9 11.1 %collective-permute-start.21 = (bf16[64,768]{1,0:T(8,128)(2,1)}, bf16[64,768]{1,0:T(8,128)(2,1)}, u32[]{:S(2)}, u32[]{:S(2)}) collective-permute-start(bf16[64,768]{1,0:T(8,128)(2,1)} %dynamic-slice_convert_fusion.3), channel_id=1, source_target_pairs={{0,2},{2,0},{4,6},{6,4},{1,3},{3,1},{5,7},{7,5},{8,10},{10,8},{12,... | collective-permute-start | bytes 294920 | tf_op jit(solution)/shard_map/ppermute | solution.py:487
  189.4 9.2 %collective-permute-start.18 = (bf16[64,1024]{1,0:T(8,128)(2,1)}, bf16[64,1024]{1,0:T(8,128)(2,1)S(1)}, u32[]{:S(2)}, u32[]{:S(2)}) collective-permute-start(bf16[64,1024]{1,0:T(8,128)(2,1)} %get-tuple-element.59), channel_id=1, source_target_pairs={{0,4},{2,6},{4,0},{6,2},{1,5},{3,7},{5,1},{7,3},{8,12},{10,14},{12... | collective-permute-start | bytes 393224 | tf_op jit(solution)/shard_map/ppermute | solution.py:487
  193.7 12.9 %collective-permute-start.22 = (bf16[64,768]{1,0:T(8,128)(2,1)}, bf16[64,768]{1,0:T(8,128)(2,1)}, u32[]{:S(2)}, u32[]{:S(2)}) collective-permute-start(bf16[64,768]{1,0:T(8,128)(2,1)} %get-tuple-element.61), channel_id=1, source_target_pairs={{0,4},{2,6},{4,0},{6,2},{1,5},{3,7},{5,1},{7,3},{8,12},{10,14},{12... | collective-permute-start | bytes 294920 | tf_op jit(solution)/shard_map/ppermute | solution.py:487
  207.5 5.5 %collective-permute-start.23 = (bf16[64,768]{1,0:T(8,128)(2,1)S(1)}, bf16[64,768]{1,0:T(8,128)(2,1)S(1)}, u32[]{:S(2)}, u32[]{:S(2)}) collective-permute-start(bf16[64,768]{1,0:T(8,128)(2,1)S(1)} %add_convert_fusion), channel_id=1, source_target_pairs={{0,2},{2,0},{4,6},{6,4},{1,3},{3,1},{5,7},{7,5},{8,10},{10,8},{12,... | collective-permute-start | bytes 294920 | tf_op jit(solution)/shard_map/ppermute | solution.py:487
  209.4 5.7 %collective-permute-start.20 = (bf16[64,1024]{1,0:T(8,128)(2,1)}, bf16[64,1024]{1,0:T(8,128)(2,1)S(1)}, u32[]{:S(2)}, u32[]{:S(2)}) collective-permute-start(bf16[64,1024]{1,0:T(8,128)(2,1)} %get-tuple-element.57), channel_id=1, source_target_pairs={{0,2},{2,0},{4,6},{6,4},{1,3},{3,1},{5,7},{7,5},{8,10},{10,8},{12,... | collective-permute-start | bytes 393224 | tf_op jit(solution)/shard_map/ppermute | solution.py:487
  (42 other events, 283.7 us)

commit v3 on v2

--- a/solution.py
+++ b/solution.py
@@ -325,19 +325,19 @@
         turned_ref[k * width : (k + 1) * width] = ref[...].T
 
 
-def put_waves(total, owners, out_refs):
-    waves = len(out_refs)
-    shard = total.shape[0] // (owners * waves)
-    for k in range(owners):
-        for w, out_ref in enumerate(out_refs):
-            at = (k * waves + w) * shard
-            out_ref[k * shard : (k + 1) * shard] = total[at : at + shard].astype(BF16)
+def put_rows(total, places_ref, out_ref):
+    count = places_ref.shape[0]
+    shard = total.shape[0] // count
+    for n in range(count):
+        place = pl.ds(pl.multiple_of(places_ref[n] * shard, shard), shard)
+        out_ref[place] = total[n * shard : (n + 1) * shard].astype(BF16)
 
 
 def hidden_body(count, has_acc, last, *refs):
+    places_ref, *refs = refs
     grads_refs, head_ref, *rest = (refs[:count], *refs[count:])
     before_ref = rest.pop(0) if has_acc else None
-    *out_refs, turned_ref = rest
+    out_ref, *flag_refs, turned_ref = rest
 
     @pl.when(pl.program_id(0) == 0)
     def _():
@@ -347,46 +347,45 @@
     if has_acc:
         total = total + before_ref[...]
     if last:
-        *out_refs, flag_ref = out_refs
-        flag_ref[...] = jnp.zeros(flag_ref.shape, F32)
-        put_waves(total, count, out_refs)
+        flag_refs[0][...] = jnp.zeros(flag_refs[0].shape, F32)
+        put_rows(total, places_ref, out_ref)
     else:
-        out_refs[0][...] = total
+        out_ref[...] = total
 
 
 def hidden_width(depth):
     return COLUMNS if depth % COLUMNS == 0 else 128
 
 
-def hidden_chunk(grads, head_t, first, waves, tiles, before, last):
+def hidden_chunk(places, grads, head_t, first, tiles, before, last):
     rows = grads[0].shape[0]
     width = hidden_width(head_t.shape[1])
     base = first // rows
     tokens = sum(g.shape[1] for g in grads)
     size = tiles * width
-    pieces = waves if last else 1
-    block = lambda count: pl.BlockSpec((count, width), lambda i: (0, i))
+    block = pl.BlockSpec((tokens, width), lambda i: (0, i))
     has_acc = before is not None
     flag = jax.ShapeDtypeStruct((8, 128), F32)
     return pl.pallas_call(
         functools.partial(hidden_body, len(grads), has_acc, last),
         grid=(tiles,),
-        in_specs=[whole(g.shape) for g in grads]
+        in_specs=[pl.BlockSpec(memory_space=pltpu.SMEM)]
+        + [whole(g.shape) for g in grads]
         + [pl.BlockSpec((rows, width), lambda i: (base, i))]
-        + [block(tokens)] * has_acc,
-        out_specs=[block(tokens // pieces)] * pieces + [whole(flag.shape)] * last,
-        out_shape=[jax.ShapeDtypeStruct((tokens // pieces, size), BF16 if last else F32)] * pieces
-        + [flag] * last,
+        + [block] * has_acc,
+        out_specs=[block] + [whole(flag.shape)] * last,
+        out_shape=[jax.ShapeDtypeStruct((tokens, size), BF16 if last else F32)] + [flag] * last,
         scratch_shapes=[pltpu.VMEM((tokens, rows), BF16)],
         compiler_params=params(30),
         cost_estimate=cost(2 * rows * tokens * size, 2 * rows * (size + tokens)),
         name="grad_hidden_chunk",
-    )(*grads, head_t, *([before] if has_acc else []))
+    )(places, *grads, head_t, *([before] if has_acc else []))
 
 
 def hidden_rest_body(chunks, owners, *refs):
-    grads_refs, head_ref, *out_refs = refs[1 : 1 + chunks * owners], *refs[1 + chunks * owners :]
-    *out_refs, turned_ref, acc_ref = out_refs
+    places_ref, *refs = refs[1:]
+    grads_refs = refs[: chunks * owners]
+    head_ref, out_ref, turned_ref, acc_ref = refs[chunks * owners :]
     tile, chunk = pl.program_id(0), pl.program_id(1)
     for c in range(chunks):
 
@@ -406,10 +405,10 @@
 
     @pl.when(chunk == chunks - 1)
     def _():
-        put_waves(acc_ref[...], owners, out_refs)
-
-
-def hidden_rest(all_grads, head_t, waves, tile, tiles, flag):
+        put_rows(acc_ref[...], places_ref, out_ref)
+
+
+def hidden_rest(places, all_grads, head_t, tile, tiles, flag):
     chunks, owners = len(all_grads), len(all_grads[0])
     grads = [g for chunk in all_grads for g in chunk]
     rows, per_owner = grads[0].shape
@@ -420,11 +419,11 @@
     return pl.pallas_call(
         functools.partial(hidden_rest_body, chunks, owners),
         grid=(tiles, chunks),
-        in_specs=[UNREAD]
+        in_specs=[UNREAD, pl.BlockSpec(memory_space=pltpu.SMEM)]
         + [full(g.shape) for g in grads]
         + [pl.BlockSpec((rows, width), lambda i, c: (c, i + tile))],
-        out_specs=[pl.BlockSpec((tokens // waves, width), lambda i, c: (0, i))] * waves,
-        out_shape=[jax.ShapeDtypeStruct((tokens // waves, size), BF16)] * waves,
+        out_specs=pl.BlockSpec((tokens, width), lambda i, c: (0, i)),
+        out_shape=jax.ShapeDtypeStruct((tokens, size), BF16),
         scratch_shapes=[
             pltpu.VMEM((chunks, tokens, rows), BF16),
             pltpu.VMEM((tokens, width), F32),
@@ -436,18 +435,17 @@
             2 * chunks * rows * tokens * size, 2 * chunks * rows * (size + tokens)
         ),
         name="grad_hidden_rest",
-    )(flag, *grads, head_t)
+    )(flag, places, *grads, head_t)
 
 
 def head_body(count, after, *refs):
     hidden_ref, *refs = refs[after:]
     grads = jnp.concatenate([ref[...] for ref in refs[:count]], axis=1)
-    out_ref, *flag_refs = refs[-3:]
+    out_ref, flag_ref = refs[-2:]
 
     @pl.when(pl.program_id(0) == 0)
     def _():
-        for ref in flag_refs:
-            ref[...] = jnp.zeros(ref.shape, F32)
+        flag_ref[...] = jnp.zeros(flag_ref.shape, F32)
 
     for at in range(0, out_ref.shape[1], COLUMNS):
         lanes = slice(at, min(at + COLUMNS, out_ref.shape[1]))
@@ -456,7 +454,7 @@
         ).astype(BF16)
 
 
-def head_chunk(hidden, grads, first, skip, rows, total, before, after, widths):
+def head_chunk(hidden, grads, first, skip, rows, total, before, after):
     tokens, depth = hidden.shape
     tile = tile_of(rows, TILE)
     base = (first + skip) // tile
@@ -469,10 +467,11 @@
         functools.partial(head_body, len(grads), len(after)),
         grid=(rows // tile,),
         in_specs=specs,
-        out_specs=[pl.BlockSpec((tile, depth), lambda i: (i + base, 0))]
-        + [whole((1, n)) for n in widths],
-        out_shape=[jax.ShapeDtypeStruct((total, depth), BF16)]
-        + [jax.ShapeDtypeStruct((1, n), F32) for n in widths],
+        out_specs=[pl.BlockSpec((tile, depth), lambda i: (i + base, 0)), whole((1, depth))],
+        out_shape=[
+            jax.ShapeDtypeStruct((total, depth), BF16),
+            jax.ShapeDtypeStruct((1, depth), F32),
+        ],
         input_output_aliases=aliases,
         compiler_params=params(24),
         cost_estimate=cost(
@@ -500,62 +499,17 @@
     return totals
 
 
-def rows_at(x, index, size):
-    return lax.dynamic_slice_in_dim(x, index * size, size)
-
-
-class Reduction:
-    def __init__(self, partial, shard, own):
-        self.partial, self.shard, self.own = partial, shard, own
-        self.owners = lax.axis_size("mp")
-        self.waves = lax.axis_size("dp") // self.owners
-
-    def over_inner(self, flag):
-        total = self.partial[0].astype(F32)
-        for w in range(1, self.waves):
-            total += late(swap(self.partial[w], "dp", w), flag)
-        self.total = total
-        return total
-
-    def over_outer(self, flag):
-        total = rows_at(self.total, self.own, self.shard)
-        for a in range(1, self.owners):
-            sent = rows_at(self.total, self.own ^ a, self.shard).astype(BF16)
-            total += late(swap(sent, "dp", a * self.waves), flag)
-        self.total = total
-        return total
-
-
-    def halve_vocab(self, flag):
-        if lax.axis_size("vocab") != 4:
-            self.total = lax.psum(self.total, "vocab")
-            return self.total
-        self.bit = lax.axis_index("vocab") % 2
-        half = self.shard // 2
-        sent = rows_at(self.total, 1 - self.bit, half).astype(BF16)
-        self.total = rows_at(self.total, self.bit, half) + late(swap(sent, "vocab", 1), flag)
-        return self.total
-
-    def cross_vocab(self, flag):
-        if lax.axis_size("vocab") == 4:
-            sent = self.total.astype(BF16)
-            self.total = sent.astype(F32) + late(swap(sent, "vocab", 2), flag)
-        return self.total
-
-    def join_vocab(self, flag):
-        if lax.axis_size("vocab") == 4:
-            sent = self.total.astype(BF16)
-            got, kept = late(swap(sent, "vocab", 1), flag), sent.astype(F32)
-            upper = self.bit == 1
-            self.total = jnp.concatenate(
-                [jnp.where(upper, got, kept), jnp.where(upper, kept, got)], axis=0
-            )
-        return self.total
-
-
-def late(x, flag):
-    x = x.astype(F32)
-    return x if flag is None else x + flag
+def once_there(x, *others):
+    return pl.pallas_call(
+        lambda *refs: None,
+        in_specs=[UNREAD] * (1 + len(others)),
+        out_specs=UNREAD,
+        out_shape=jax.ShapeDtypeStruct(x.shape, x.dtype),
+        input_output_aliases={0: 0},
+        compiler_params=pltpu.CompilerParams(vmem_limit_bytes=MIB),
+        cost_estimate=cost(0, 0),
+        name="once_there",
+    )(x, *others)
 
 
 def per_device(hidden, head_weight, teacher_logits, response_start):
@@ -630,36 +584,28 @@
     width = hidden_width(depth)
     tiles = depth // width
     split = (tiles + 1) // 2
+    places = jnp.stack(
+        [(mp ^ k) * waves + (inner ^ w) for k in range(n_mp) for w in range(waves)]
+    ).astype(jnp.int32)
     acc = None
     for c, (first, rows) in enumerate(chunks):
         last = c == len(chunks) - 1
-        outs = hidden_chunk(all_grads[c], head_t, first, waves, split, acc, last)
-        acc = outs[0]
-    *outs, flag = outs
-    one = Reduction(outs, shard, own)
-    two = Reduction(hidden_rest(all_grads, head_t, waves, split, tiles - split, flag), shard, own)
-
-    results = [one.over_inner(None)]
-    plan = [
-        lambda f, g: [one.over_outer(f), two.over_inner(g)],
-        lambda f, g: [one.halve_vocab(f), two.over_outer(g)],
-        lambda f, g: [one.cross_vocab(f), two.halve_vocab(g)],
-        lambda f, g: [one.join_vocab(f), two.cross_vocab(g)],
-    ]
-    widths = (split * width, depth - split * width)
-    calls = [(c, 0, rows) for c, (_, rows) in enumerate(chunks)]
-    if calls[-1][2] % (2 * TILE) == 0:
-        c, _, rows = calls.pop()
-        calls += [(c, 0, rows // 2), (c, rows // 2, rows // 2)]
-    grad_head = None
-    for c, skip, rows in calls:
-        grad_head, *flags = head_chunk(
-            ordered, all_grads[c], chunks[c][0], skip, rows, columns, grad_head, results, widths
+        acc, *flags = hidden_chunk(places, all_grads[c], head_t, first, split, acc, last)
+    scattered = lax.psum_scatter(acc, "dp", scatter_dimension=0, tiled=True)
+    rest = hidden_rest(places, all_grads, head_t, split, tiles - split, flags[0])
+    two = lax.psum_scatter(rest, "dp", scatter_dimension=0, tiled=True)
+    one = lax.psum(scattered, "vocab")
+
+    grad_head, flag = None, scattered
+    for c, (first, rows) in enumerate(chunks):
+        if c == len(chunks) - 1:
+            two = once_there(two, one, flag)
+        after = [scattered] if c == 0 else [two] if c == len(chunks) - 1 else []
+        grad_head, flag = head_chunk(
+            ordered, all_grads[c], first, 0, rows, columns, grad_head, after
         )
-        results = plan.pop(0)(*flags)
-    while plan:
-        results = plan.pop(0)(*flags)
-    grad_hidden = jnp.concatenate([one.total, two.join_vocab(None)], axis=1)
+    two = lax.psum(two, "vocab")
+    grad_hidden = jnp.concatenate([one, two], axis=1).astype(F32) + flag
     return (token_kl.reshape(own_rows), grad_hidden, grad_head.T)
 
 

time: 218 us -> 290 us (1.33)
  waiting for transfers between devices: 29.1 us -> 110 us
  between operations: 1.22 us -> 14.1 us
  starting transfers between devices: 26.1 us -> 15.1 us
  other arithmetic: 13 us -> 2.13 us
  local copies, waits for them, and re-layouts: 23.1 us -> 18.8 us
  Pallas kernels: 125 us -> 129 us
    psum x0 -> x2, waiting for transfers between devices: none -> 74.5 us  [the longest x1 37.8 us: per_device(): one = lax.psum(scattered, 'vocab')]
    reduce_scatter x0 -> x2, waiting for transfers between devices: none -> 14.7 us  [the longest x1 9.11 us: per_device(): scattered = lax.psum_scatter(acc, 'dp', scatter_dimension=0, tiled=True)]
    ppermute x24 -> x14, starting transfers between devices: 26.1 us -> 14.8 us  [swap(): return lax.ppermute(x, axis, [(i, i ^ k) for i in range(n)])]
    ppermute x24 -> x14, waiting for transfers between devices: 29.1 us -> 19.2 us  [swap(): return lax.ppermute(x, axis, [(i, i ^ k) for i in range(n)])]
    convert_element_type x4 -> x0, other arithmetic: 5.93 us -> none  [the longest x2 3.35 us: cross_vocab(): sent = self.total.astype(BF16)]
    convert_element_type x4 -> x0, local copies, waits for them, and re-layouts: 3.07 us -> none  [the longest x2 1.58 us: over_outer(): sent = rows_at(self.total, self.own ^ a, self.shard).astype(BF16)]
    add x4 -> x1, other arithmetic: 4.93 us -> 1.91 us  [per_device(): grad_hidden = jnp.concatenate([one, two], axis=1).astype(F32) + flag]
    pallas_call x4 -> x3, Pallas kernels: 26.7 us -> 29 us  [head_chunk(): pl.pallas_call(functools.partial(head_body, len(grads), len(after)), grid...]
  transfers between devices with their start and end apart: 24 -> 18, of which waited for: 8 -> 9; matrix products, arithmetic and copies ran while one was open for 8% -> 2% of each run, Pallas kernels for 39% -> 32%
where the time goes in v3:
time: 290 us; the launch traced here: 288 us
  Pallas kernels  129 us (44%)
  waiting for transfers between devices  110 us (38%)
  local copies, waits for them, and re-layouts  18.8 us (6%)
  starting transfers between devices  15.1 us (5%)
  between operations  14.1 us (5%)
    psum x1, waiting for transfers between devices, per_device(): one = lax.psum(scattered, 'vocab')  37.8 us
    psum x1, waiting for transfers between devices, per_device(): two = lax.psum(two, 'vocab')  36.7 us
    pallas_call x3, Pallas kernels, student_chunk(): pl.pallas_call(functools.partial(student_body, owners, places, len(after)...  36.4 us
    pallas_call x3, Pallas kernels, head_chunk(): pl.pallas_call(functools.partial(head_body, len(grads), len(after)), grid...  29 us
    pallas_call x3, Pallas kernels, hidden_chunk(): pl.pallas_call(functools.partial(hidden_body, len(grads), has_acc, last),...  23.5 us
    ppermute x14, waiting for transfers between devices, swap(): return lax.ppermute(x, axis, [(i, i ^ k) for i in range(n)])  19.2 us
    pallas_call x1, Pallas kernels, hidden_rest(): pl.pallas_call(functools.partial(hidden_rest_body, chunks, owners), grid=...  17.6 us
    ppermute x14, starting transfers between devices, swap(): return lax.ppermute(x, axis, [(i, i ^ k) for i in range(n)])  14.8 us
  transfers between devices with their start and end apart: 18, of which 9 were waited for; matrix products, arithmetic and copies ran while one was open for 2% of the time, Pallas kernels for 32%

profile of v3, /device:TPU:0, one launch (start us, length us, event | category | flops | bytes accessed | tf_op | source)
XLA Modules:
  0.0 288.5 jit_solution(6973573580602735517)
XLA Ops:
  7.2 3.0 %collective-permute-start = (bf16[128,1792]{1,0:T(8,128)(2,1)}, bf16[128,1792]{1,0:T(8,128)(2,1)S(1)}, u32[]{:S(2)}, u32[]{:S(2)}) collective-permute-start(bf16[128,1792]{1,0:T(8,128)(2,1)} %refs_7_.1), channel_id=1, source_target_pairs={{0,8},{8,0},{16,24},{24,16},{1,9},{9,1},{17,25},{25,17},{2,10},{10... | collective-permute-start | bytes 1376264 | tf_op jit(solution)/shard_map/ppermute | solution.py:486
  11.7 9.2 %collective-permute-done.refs_8_ = bf16[128,1792]{1,0:T(8,128)(2,1)S(1)} collective-permute-done((bf16[128,1792]{1,0:T(8,128)(2,1)}, bf16[128,1792]{1,0:T(8,128)(2,1)S(1)}, u32[]{:S(2)}, u32[]{:S(2)}) %collective-permute-start) | collective-permute-done | bytes 458784 | tf_op jit(solution)/shard_map/ppermute | solution.py:486
  24.4 4.7 %dynamic-slice_bitcast_fusion = (bf16[3168,128]{1,0:T(8,128)(2,1)}, bf16[3168,128]{1,0:T(8,128)(2,1)}, bf16[3168,128]{1,0:T(8,128)(2,1)}, bf16[3168,128]{1,0:T(8...) fusion(bf16[256,9504]{0,1:T(8,128)(2,1)} %param.6, s32[]{:T(128)S(6)} %select_n.51, s32[]{:T(128)S(6)} %select_n.50), kind=kLoop, calls=%fused_computation.1 | loop fusion | bytes 9732104 | tf_op jit(solution)/shard_map/dynamic_slice | solution.py:539
  30.5 12.8 %student_chunk.3 = (f32[3168,256]{1,0:T(8,128)}, f32[3168,256]{1,0:T(8,128)}, bf16[512,1792]{1,0:T(8,128)(2,1)}, bf16[1792,512]{1,0:T(8,128)(2,1)}) custom-call(bf16[3168,128]{1,0:T(8,128)(2,1)} %get-tuple-element.41.refs_0_.refs_2_, bf16[3168,128]{1,0:T(8,128)(2,1)} %get-tuple-element.40.refs_1_.refs_3_, bf16[3168,128]{1,0:T(8,128)(2,1)} %get-tuple-element.39.refs_2_, ...), custom_call_target="tpu_custom_call" | custom-call | flops 363331584 | bytes 1229824 | tf_op jit(solution)/shard_map/student_chunk/pallas_call | solution.py:209
  43.3 11.8 %student_chunk.5 = (f32[3168,256]{1,0:T(8,128)}, f32[3168,256]{1,0:T(8,128)}) custom-call(bf16[1792,512]{1,0:T(8,128)(2,1)} %get-tuple-element.20.refs_0_, bf16[9504,1792]{1,0:T(8,128)(2,1)} %bitcast.29), custom_call_target="tpu_custom_call" | custom-call | flops 363331584 | bytes 1229824 | tf_op jit(solution)/shard_map/student_chunk/pallas_call | solution.py:209
  55.6 11.8 %student_chunk.4 = (f32[3168,256]{1,0:T(8,128)}, f32[3168,256]{1,0:T(8,128)}) custom-call(bf16[1792,512]{1,0:T(8,128)(2,1)} %get-tuple-element.20.refs_0_, bf16[9504,1792]{1,0:T(8,128)(2,1)} %bitcast.30), custom_call_target="tpu_custom_call" | custom-call | flops 363331584 | bytes 1229824 | tf_op jit(solution)/shard_map/student_chunk/pallas_call | solution.py:209
  71.6 5.2 %totals_chunk.3.refs_4_ = f32[40,256]{1,0:T(8,128)S(1)} custom-call(f32[3168,256]{1,0:T(8,128)S(1)} %copy-done.3, f32[3168,256]{1,0:T(8,128)} %collective-permute-done.6.refs_1_, bf16[3168,128]{1,0:T(8,128)(2,1)S(1)} %copy-done.15, bf16[3168,128]{1,0:T(8,128)(2,1)S(1)} %copy-done.13, f32[40,256]{1,0:T(8,128)S(1)} %copy-done.22), custom_call_target="tpu_custom_call" | custom-call | flops 608256 | bytes 506880 | tf_op jit(solution)/shard_map/totals_chunk/pallas_call | solution.py:147
  76.9 5.1 %totals_chunk.4.refs_4_ = f32[40,256]{1,0:T(8,128)S(1)} custom-call(f32[3168,256]{1,0:T(8,128)S(1)} %copy-done.6, f32[3168,256]{1,0:T(8,128)} %collective-permute-done.5.refs_1_, bf16[3168,128]{1,0:T(8,128)(2,1)S(1)} %copy-done.12, bf16[3168,128]{1,0:T(8,128)(2,1)S(1)} %copy-done.11, f32[40,256]{1,0:T(8,128)S(1)} %totals_chunk.3.refs_4_), custom_call_target="tpu_custom_call" | custom-call | flops 608256 | bytes 506880 | tf_op jit(solution)/shard_map/totals_chunk/pallas_call | solution.py:147
  85.5 2.8 collective-permute-done.7.refs_1_
  89.0 3.1 %collective-permute-done.8.refs_1_ = f32[8,256]{1,0:T(8,128)S(1)} collective-permute-done((f32[8,256]{1,0:T(8,128)S(1)}, f32[8,256]{1,0:T(8,128)S(1)}, u32[]{:S(2)}, u32[]{:S(2)}) %collective-permute-start.8) | collective-permute-done | bytes 8224 | tf_op jit(solution)/shard_map/ppermute | solution.py:486
  95.8 2.6 collective-permute-start.10
  100.5 4.5 %logit_grads_chunk.5.refs_1_.refs_2_ = bf16[3168,256]{1,0:T(8,128)(2,1)} custom-call(f32[3168,256]{1,0:T(8,128)S(1)} %copy-done.4, f32[3168,256]{1,0:T(8,128)} %collective-permute-done.6.refs_1_, bf16[3168,128]{1,0:T(8,128)(2,1)S(1)} %copy-done.16, bf16[3168,128]{1,0:T(8,128)(2,1)S(1)} %copy-done.14, f32[8,256]{1,0:T(8,128)S(1)} %get-tuple-element.28.refs_4_), custom_call_target="tpu_custom_call" | custom-call | flops 405504 | bytes 608256 | tf_op jit(solution)/shard_map/logit_grads_chunk/pallas_call | solution.py:308
  105.0 3.5 %logit_grads_chunk.4.refs_1_.refs_4_ = bf16[3168,256]{1,0:T(8,128)(2,1)S(1)} custom-call(f32[3168,256]{1,0:T(8,128)S(1)} %copy-done.6, f32[3168,256]{1,0:T(8,128)} %collective-permute-done.5.refs_1_, bf16[3168,128]{1,0:T(8,128)(2,1)S(1)} %copy-done.12, bf16[3168,128]{1,0:T(8,128)(2,1)S(1)} %copy-done.11, f32[8,256]{1,0:T(8,128)S(1)} %get-tuple-element.28.refs_4_), custom_call_target="tpu_custom_call" | custom-call | flops 405504 | bytes 608256 | tf_op jit(solution)/shard_map/logit_grads_chunk/pallas_call | solution.py:308
  110.6 8.1 %grad_hidden_chunk.3.refs_4_ = f32[512,1024]{1,0:T(8,128)S(1)} custom-call(s32[4]{0:T(128)S(1)} %pad_add_fusion.refs_0_.refs_1_, bf16[3168,256]{1,0:T(8,128)(2,1)} %logit_grads_chunk.5.refs_1_.refs_2_, bf16[3168,256]{1,0:T(8,128)(2,1)} %collective-permute-done.13.refs_2_.refs_3_, bf16[9504,1792]{1,0:T(8,128)(2,1)} %bitcast.31), custom_call_target="tpu_custom_call" | custom-call | flops 207618048 | bytes 608256 | tf_op jit(solution)/shard_map/grad_hidden_chunk/pallas_call | solution.py:369
  118.7 7.7 %grad_hidden_chunk.4.refs_4_ = f32[512,1024]{1,0:T(8,128)S(1)} custom-call(s32[4]{0:T(128)S(1)} %pad_add_fusion.refs_0_.refs_1_, bf16[3168,256]{1,0:T(8,128)(2,1)S(1)} %logit_grads_chunk.4.refs_1_.refs_4_, bf16[3168,256]{1,0:T(8,128)(2,1)} %collective-permute-done.12.refs_2_.refs_5_, bf16[9504,1792]{1,0:T(8,128)(2,1)} %bitcast.32, ...), custom_call_target="tpu_custom_call" | custom-call | flops 207618048 | bytes 608256 | tf_op jit(solution)/shard_map/grad_hidden_chunk/pallas_call | solution.py:369
  126.4 7.7 %grad_hidden_chunk.5 = (bf16[512,1024]{1,0:T(8,128)(2,1)S(1)}, f32[8,128]{1,0:T(8,128)S(1)}) custom-call(s32[4]{0:T(128)S(1)} %pad_add_fusion.refs_0_.refs_1_, bf16[3168,256]{1,0:T(8,128)(2,1)S(1)} %logit_grads_chunk.3.refs_1_.refs_6_.refs_2_, bf16[3168,256]{1,0:T(8,128)(2,1)} %collective-permute-done.11.refs_2_.refs_7_.refs_3_, ...), custom_call_target="tpu_custom_call" | custom-call | flops 207618048 | bytes 608256 | tf_op jit(solution)/shard_map/grad_hidden_chunk/pallas_call | solution.py:369
  135.4 17.6 %grad_hidden_rest.1 = bf16[512,768]{1,0:T(8,128)(2,1)S(1)} custom-call(f32[8,128]{1,0:T(8,128)S(1)} %get-tuple-element.30.refs_0_, s32[4]{0:T(128)S(1)} %pad_add_fusion.refs_0_.refs_1_, bf16[3168,256]{1,0:T(8,128)(2,1)} %logit_grads_chunk.5.refs_1_.refs_2_, bf16[3168,256]{1,0:T(8,128)(2,1)} %collective-permute-done.13.refs_2_.refs_3_, ...), custom_call_target="tpu_custom_call" | custom-call | flops 467140608 | bytes 1520640 | tf_op jit(solution)/shard_map/grad_hidden_rest/pallas_call | solution.py:419
  153.9 9.1 %reduce-scatter.3.cloned.1.call-done.refs_0_ = bf16[128,1024]{1,0:T(8,128)(2,1)} async-done(((bf16[512,1024]{1,0:T(8,128)(2,1)}), bf16[128,1024]{1,0:T(8,128)(2,1)}) %reduce-scatter.3.cloned.1.call-update) | async-done | bytes 262160 | tf_op jit(solution)/shard_map/reduce_scatter | solution.py:594
  165.4 10.0 %grad_head_chunk.3 = (bf16[9504,1792]{1,0:T(8,128)(2,1)}, f32[1,1792]{1,0:T(1,128)}) custom-call(bf16[128,1024]{1,0:T(8,128)(2,1)S(1)} %copy-done.21, bf16[512,1792]{1,0:T(8,128)(2,1)S(1)} %copy-done, bf16[3168,256]{1,0:T(8,128)(2,1)} %logit_grads_chunk.5.refs_1_.refs_2_, bf16[3168,256]{1,0:T(8,128)(2,1)} %collective-permute-done.13.refs_2_.refs_3_), custom_call_target="tpu_custom_call" | custom-call | flops 363331584 | bytes 1027072 | tf_op jit(solution)/shard_map/grad_head_chunk/pallas_call | solution.py:466
  177.8 9.5 %grad_head_chunk.4 = (bf16[9504,1792]{1,0:T(8,128)(2,1)}, f32[1,1792]{1,0:T(1,128)S(1)}) custom-call(bf16[512,1792]{1,0:T(8,128)(2,1)S(1)} %copy-done.1, bf16[3168,256]{1,0:T(8,128)(2,1)S(1)} %logit_grads_chunk.4.refs_1_.refs_4_, bf16[3168,256]{1,0:T(8,128)(2,1)} %collective-permute-done.12.refs_2_.refs_5_, ...), custom_call_target="tpu_custom_call", output_to_operand_aliasing={{0}: (3, {})} | custom-call | flops 363331584 | bytes 1027072 | tf_op jit(solution)/shard_map/grad_head_chunk/pallas_call | solution.py:466
  187.3 5.6 %reduce-scatter.5.cloned.1.call-done.refs_0_ = bf16[128,768]{1,0:T(8,128)(2,1)} async-done(((bf16[512,768]{1,0:T(8,128)(2,1)}), bf16[128,768]{1,0:T(8,128)(2,1)}) %reduce-scatter.5.cloned.1.call-update) | async-done | bytes 196624 | tf_op jit(solution)/shard_map/reduce_scatter | solution.py:596
  192.9 37.8 %all-reduce.3.cloned.1.call-done.refs_1_ = bf16[128,1024]{1,0:T(8,128)(2,1)} async-done(((bf16[128,1024]{1,0:T(8,128)(2,1)}), bf16[128,1024]{1,0:T(8,128)(2,1)}) %all-reduce.3.cloned.1.call-update) | async-done | bytes 262160 | tf_op jit(solution)/shard_map/psum | solution.py:597
  233.1 9.5 %grad_head_chunk.5 = (bf16[9504,1792]{1,0:T(8,128)(2,1)}, f32[1,1792]{1,0:T(1,128)S(1)}) custom-call(bf16[128,768]{1,0:T(8,128)(2,1)} %once_there.1.refs_0_, bf16[512,1792]{1,0:T(8,128)(2,1)S(1)} %copy-done.2, bf16[3168,256]{1,0:T(8,128)(2,1)S(1)} %logit_grads_chunk.3.refs_1_.refs_6_.refs_2_, ...), custom_call_target="tpu_custom_call", output_to_operand_aliasing={{0}: (4, {})} | custom-call | flops 363331584 | bytes 1027072 | tf_op jit(solution)/shard_map/grad_head_chunk/pallas_call | solution.py:466
  243.3 36.7 %all-reduce.5.cloned.1.call-done = bf16[128,768]{1,0:T(8,128)(2,1)} async-done(((bf16[128,768]{1,0:T(8,128)(2,1)}), bf16[128,768]{1,0:T(8,128)(2,1)}) %all-reduce.5.cloned.1.call-update) | async-done | bytes 196624 | tf_op jit(solution)/shard_map/psum | solution.py:607
  (109 shorter events, 34.9 us)
Async XLA Ops:
  7.2 155.8 %reduce-scatter.3.cloned.1.call-start = ((), (), s32[]{:S(2)}) async-start(), calls=%async_computation.2 | async-start | bytes 1310720 | tf_op jit(solution)/shard_map/reduce_scatter | solution.py:594
  7.2 13.7 %collective-permute-start = (bf16[128,1792]{1,0:T(8,128)(2,1)}, bf16[128,1792]{1,0:T(8,128)(2,1)S(1)}, u32[]{:S(2)}, u32[]{:S(2)}) collective-permute-start(bf16[128,1792]{1,0:T(8,128)(2,1)} %refs_7_.1), channel_id=1, source_target_pairs={{0,8},{8,0},{16,24},{24,16},{1,9},{9,1},{17,25},{25,17},{2,10},{10... | collective-permute-start | bytes 1376264 | tf_op jit(solution)/shard_map/ppermute | solution.py:486
  10.2 12.6 %collective-permute-start.1 = (bf16[128,1792]{1,0:T(8,128)(2,1)}, bf16[128,1792]{1,0:T(8,128)(2,1)S(1)}, u32[]{:S(2)}, u32[]{:S(2)}) collective-permute-start(bf16[128,1792]{1,0:T(8,128)(2,1)} %refs_7_.1), channel_id=1, source_target_pairs={{0,16},{8,24},{16,0},{24,8},{1,17},{9,25},{17,1},{25,9},{2,18},{10... | collective-permute-start | bytes 1376264 | tf_op jit(solution)/shard_map/ppermute | solution.py:486
  21.0 8.1 %collective-permute-start.3 = (bf16[64,1792]{1,0:T(8,128)(2,1)S(1)}, bf16[64,1792]{1,0:T(8,128)(2,1)S(1)}, u32[]{:S(2)}, u32[]{:S(2)}) collective-permute-start(bf16[64,1792]{1,0:T(8,128)(2,1)S(1)} %slice.17), channel_id=1, source_target_pairs={{0,16},{8,24},{16,0},{24,8},{1,17},{9,25},{17,1},{25,9},{2,18},{10... | collective-permute-start | bytes 688136 | tf_op jit(solution)/shard_map/ppermute | solution.py:486
  22.8 6.3 %collective-permute-start.2 = (bf16[64,1792]{1,0:T(8,128)(2,1)S(1)}, bf16[64,1792]{1,0:T(8,128)(2,1)S(1)}, u32[]{:S(2)}, u32[]{:S(2)}) collective-permute-start(bf16[64,1792]{1,0:T(8,128)(2,1)S(1)} %slice.16), channel_id=1, source_target_pairs={{0,8},{8,0},{16,24},{24,16},{1,9},{9,1},{17,25},{25,17},{2,10},{10... | collective-permute-start | bytes 688136 | tf_op jit(solution)/shard_map/ppermute | solution.py:486
  43.3 24.1 %collective-permute-start.6 = (f32[3168,256]{1,0:T(8,128)}, f32[3168,256]{1,0:T(8,128)}, u32[]{:S(2)}, u32[]{:S(2)}) collective-permute-start(f32[3168,256]{1,0:T(8,128)} %get-tuple-element.26), channel_id=1, source_target_pairs={{0,1},{1,0},{2,3},{3,2},{4,5},{5,4},{6,7},{7,6},{8,9},{9,8},{10,11... | collective-permute-start | bytes 9732104 | tf_op jit(solution)/shard_map/ppermute | solution.py:486
  55.1 12.3 %copy-start.22 = (f32[40,256]{1,0:T(8,128)S(1)}, f32[40,256]{1,0:T(8,128)}, u32[]{:S(2)}) copy-start(f32[40,256]{1,0:T(8,128)} %constant.69.clone.1.refs_4_) | copy-start | bytes 122884
  55.1 21.7 %collective-permute-start.5 = (f32[3168,256]{1,0:T(8,128)}, f32[3168,256]{1,0:T(8,128)}, u32[]{:S(2)}, u32[]{:S(2)}) collective-permute-start(f32[3168,256]{1,0:T(8,128)} %get-tuple-element.24), channel_id=1, source_target_pairs={{0,1},{1,0},{2,3},{3,2},{4,5},{5,4},{6,7},{7,6},{8,9},{9,8},{10,11... | collective-permute-start | bytes 9732104 | tf_op jit(solution)/shard_map/ppermute | solution.py:486
  67.4 14.6 %collective-permute-start.4 = (f32[3168,256]{1,0:T(8,128)}, f32[3168,256]{1,0:T(8,128)S(1)}, u32[]{:S(2)}, u32[]{:S(2)}) collective-permute-start(f32[3168,256]{1,0:T(8,128)} %get-tuple-element.22), channel_id=1, source_target_pairs={{0,1},{1,0},{2,3},{3,2},{4,5},{5,4},{6,7},{7,6},{8,9},{9,8},{10,11... | collective-permute-start | bytes 9732104 | tf_op jit(solution)/shard_map/ppermute | solution.py:486
  82.1 18.4 %copy-start.4 = (f32[3168,256]{1,0:T(8,128)S(1)}, f32[3168,256]{1,0:T(8,128)}, u32[]{:S(2)}) copy-start(f32[3168,256]{1,0:T(8,128)} %get-tuple-element.25.refs_0_) | copy-start | bytes 9732100
  82.1 18.4 %copy-start.14 = (bf16[3168,128]{1,0:T(8,128)(2,1)S(1)}, bf16[3168,128]{1,0:T(8,128)(2,1)}, u32[]{:S(2)}) copy-start(bf16[3168,128]{1,0:T(8,128)(2,1)} %get-tuple-element.40.refs_1_.refs_3_) | copy-start | bytes 2433028
  82.1 18.4 %copy-start.16 = (bf16[3168,128]{1,0:T(8,128)(2,1)S(1)}, bf16[3168,128]{1,0:T(8,128)(2,1)}, u32[]{:S(2)}) copy-start(bf16[3168,128]{1,0:T(8,128)(2,1)} %get-tuple-element.41.refs_0_.refs_2_) | copy-start | bytes 2433028
  84.6 3.7 %collective-permute-start.7 = (f32[8,256]{1,0:T(8,128)S(1)}, f32[8,256]{1,0:T(8,128)S(1)}, u32[]{:S(2)}, u32[]{:S(2)}) collective-permute-start(f32[8,256]{1,0:T(8,128)S(1)} %totals_chunk.5.refs_0_), channel_id=1, source_target_pairs={{0,8},{8,0},{16,24},{24,16},{1,9},{9,1},{17,25},{25,17},{2,10},{10... | collective-permute-start | bytes 24584 | tf_op jit(solution)/shard_map/ppermute | solution.py:486
  88.4 3.7 %collective-permute-start.8 = (f32[8,256]{1,0:T(8,128)S(1)}, f32[8,256]{1,0:T(8,128)S(1)}, u32[]{:S(2)}, u32[]{:S(2)}) collective-permute-start(f32[8,256]{1,0:T(8,128)S(1)} %merge_totals.3.refs_0_), channel_id=1, source_target_pairs={{0,16},{8,24},{16,0},{24,8},{1,17},{9,25},{17,1},{25,9},{2,18},{10... | collective-permute-start | bytes 24584 | tf_op jit(solution)/shard_map/ppermute | solution.py:486
  92.1 3.7 %collective-permute-start.9 = (f32[8,256]{1,0:T(8,128)S(1)}, f32[8,256]{1,0:T(8,128)S(1)}, u32[]{:S(2)}, u32[]{:S(2)}) collective-permute-start(f32[8,256]{1,0:T(8,128)S(1)} %merge_totals.4.refs_0_), channel_id=1, source_target_pairs={{0,2},{2,0},{4,6},{6,4},{1,3},{3,1},{5,7},{7,5},{8,10},{10,8},{12,... | collective-permute-start | bytes 24584 | tf_op jit(solution)/shard_map/ppermute | solution.py:486
  95.8 4.6 %collective-permute-start.10 = (f32[8,256]{1,0:T(8,128)S(1)}, f32[8,256]{1,0:T(8,128)S(1)}, u32[]{:S(2)}, u32[]{:S(2)}) collective-permute-start(f32[8,256]{1,0:T(8,128)S(1)} %merge_totals.5.refs_0_), channel_id=1, source_target_pairs={{0,4},{2,6},{4,0},{6,2},{1,5},{3,7},{5,1},{7,3},{8,12},{10,14},{12... | collective-permute-start | bytes 24584 | tf_op jit(solution)/shard_map/ppermute | solution.py:486
  105.0 5.6 %collective-permute-start.13 = (bf16[3168,256]{1,0:T(8,128)(2,1)}, bf16[3168,256]{1,0:T(8,128)(2,1)}, u32[]{:S(2)}, u32[]{:S(2)}) collective-permute-start(bf16[3168,256]{1,0:T(8,128)(2,1)} %logit_grads_chunk.5.refs_1_.refs_2_), channel_id=1, source_target_pairs={{0,1},{1,0},{2,3},{3,2},{4,5},{5,4},{6,7},{7,6},{8,9},{9,8},{10,11... | collective-permute-start | bytes 4866056 | tf_op jit(solution)/shard_map/ppermute | solution.py:486
  108.5 10.2 %collective-permute-start.12 = (bf16[3168,256]{1,0:T(8,128)(2,1)S(1)}, bf16[3168,256]{1,0:T(8,128)(2,1)}, u32[]{:S(2)}, u32[]{:S(2)}) collective-permute-start(bf16[3168,256]{1,0:T(8,128)(2,1)S(1)} %logit_grads_chunk.4.refs_1_.refs_4_), channel_id=1, source_target_pairs={{0,1},{1,0},{2,3},{3,2},{4,5},{5,4},{6,7},{7,6},{8,9},{9,8},{10,11... | collective-permute-start | bytes 4866056 | tf_op jit(solution)/shard_map/ppermute | solution.py:486
  110.3 16.1 %collective-permute-start.11 = (bf16[3168,256]{1,0:T(8,128)(2,1)S(1)}, bf16[3168,256]{1,0:T(8,128)(2,1)}, u32[]{:S(2)}, u32[]{:S(2)}) collective-permute-start(bf16[3168,256]{1,0:T(8,128)(2,1)S(1)} %logit_grads_chunk.3.refs_1_.refs_6_.refs_2_), channel_id=1, source_target_pairs={{0,1},{1,0},{2,3},{3,2},{4,5},{5,4},{6,7},{7,6},{8,9},{9,8},{10,11... | collective-permute-start | bytes 4866056 | tf_op jit(solution)/shard_map/ppermute | solution.py:486
  135.1 57.7 %reduce-scatter.5.cloned.1.call-start = ((), (), s32[]{:S(2)}) async-start(), calls=%async_computation.4 | async-start | bytes 983040 | tf_op jit(solution)/shard_map/reduce_scatter | solution.py:596
  175.4 55.2 %all-reduce.3.cloned.1.call-start = ((), (), s32[]{:S(2)}) async-start(), calls=%async_computation.3 | async-start | bytes 524288 | tf_op jit(solution)/shard_map/psum | solution.py:597
  233.1 46.9 %copy-start.20 = (bf16[128,1024]{1,0:T(8,128)(2,1)S(1)}, bf16[128,1024]{1,0:T(8,128)(2,1)}, u32[]{:S(2)}) copy-start(bf16[128,1024]{1,0:T(8,128)(2,1)} %all-reduce.3.cloned.1.call-done.refs_1_) | copy-start | bytes 786436
  242.6 37.4 %all-reduce.5.cloned.1.call-start = ((), (), s32[]{:S(2)}) async-start(), calls=%async_computation.5 | async-start | bytes 393216 | tf_op jit(solution)/shard_map/psum | solution.py:607
  243.3 38.7 %copy-start.28 = (f32[256]{0:T(256)}, f32[256]{0:T(256)S(1)}, u32[]{:S(2)}) copy-start(f32[256]{0:T(256)S(1)} %bitcast_dynamic-update-slice_fusion) | copy-start | bytes 3076
  (23 other events, 72.8 us)
Sparse Core Ops, SparseCore 0:
  135.3 27.6 reduce-scatter.2
  166.7 26.1 reduce-scatter.4
  195.3 35.2 all-reduce.2
  245.4 34.5 all-reduce.4

commit v4 on v2

--- a/solution.py
+++ b/solution.py
@@ -135,8 +135,8 @@
             out_ref[...] = state_ref[...]
 
 
-def row_blocks(arrays, tile, skip=0):
-    return [pl.BlockSpec((tile, x.shape[1]), lambda i: (i + skip, 0)) for x in arrays]
+def row_blocks(arrays, tile):
+    return [pl.BlockSpec((tile, x.shape[1]), lambda i: (i, 0)) for x in arrays]
 
 
 def totals_chunk(parts, teachers, before, last):
@@ -430,7 +430,7 @@
             pltpu.VMEM((tokens, width), F32),
         ],
         compiler_params=pltpu.CompilerParams(
-            dimension_semantics=("arbitrary", "arbitrary"), vmem_limit_bytes=38 * MIB
+            dimension_semantics=("arbitrary", "arbitrary"), vmem_limit_bytes=58 * MIB
         ),
         cost_estimate=cost(
             2 * chunks * rows * tokens * size, 2 * chunks * rows * (size + tokens)
@@ -456,11 +456,11 @@
         ).astype(BF16)
 
 
-def head_chunk(hidden, grads, first, skip, rows, total, before, after, widths):
+def head_chunk(hidden, grads, first, rows, total, before, after, widths):
     tokens, depth = hidden.shape
     tile = tile_of(rows, TILE)
-    base = (first + skip) // tile
-    specs = [UNREAD] * len(after) + [whole(hidden.shape)] + row_blocks(grads, tile, skip // tile)
+    base = first // tile
+    specs = [UNREAD] * len(after) + [whole(hidden.shape)] + row_blocks(grads, tile)
     extra, aliases = [], {}
     if before is not None:
         specs.append(UNREAD)
@@ -526,31 +526,33 @@
         return total
 
 
-    def halve_vocab(self, flag):
-        if lax.axis_size("vocab") != 4:
-            self.total = lax.psum(self.total, "vocab")
-            return self.total
-        self.bit = lax.axis_index("vocab") % 2
-        half = self.shard // 2
-        sent = rows_at(self.total, 1 - self.bit, half).astype(BF16)
-        self.total = rows_at(self.total, self.bit, half) + late(swap(sent, "vocab", 1), flag)
-        return self.total
-
-    def cross_vocab(self, flag):
-        if lax.axis_size("vocab") == 4:
-            sent = self.total.astype(BF16)
-            self.total = sent.astype(F32) + late(swap(sent, "vocab", 2), flag)
-        return self.total
-
-    def join_vocab(self, flag):
-        if lax.axis_size("vocab") == 4:
-            sent = self.total.astype(BF16)
-            got, kept = late(swap(sent, "vocab", 1), flag), sent.astype(F32)
-            upper = self.bit == 1
-            self.total = jnp.concatenate(
-                [jnp.where(upper, got, kept), jnp.where(upper, kept, got)], axis=0
-            )
-        return self.total
+    def scatter_vocab(self, flag):
+        n = lax.axis_size("vocab")
+        if n > 4 or self.shard % (8 * n):
+            self.block = lax.psum(self.total, "vocab")
+            return self.block
+        mine, size = lax.axis_index("vocab"), self.shard // n
+        block = rows_at(self.total, mine, size)
+        for c in range(1, n):
+            sent = rows_at(self.total, mine ^ c, size).astype(BF16)
+            block += late(swap(sent, "vocab", c), flag)
+        self.block = block.astype(BF16)
+        return self.block
+
+
+def gather_vocab(blocks, shard):
+    block = jnp.concatenate(blocks, axis=1)
+    size = block.shape[0]
+    if size == shard:
+        return block
+    mine = lax.axis_index("vocab")
+    result = jnp.zeros((shard, block.shape[1]), F32)
+    for c in range(lax.axis_size("vocab")):
+        piece = swap(block, "vocab", c) if c else block
+        result = lax.dynamic_update_slice_in_dim(
+            result, piece.astype(F32), (mine ^ c) * size, 0
+        )
+    return result
 
 
 def late(x, flag):
@@ -642,24 +644,19 @@
     results = [one.over_inner(None)]
     plan = [
         lambda f, g: [one.over_outer(f), two.over_inner(g)],
-        lambda f, g: [one.halve_vocab(f), two.over_outer(g)],
-        lambda f, g: [one.cross_vocab(f), two.halve_vocab(g)],
-        lambda f, g: [one.join_vocab(f), two.cross_vocab(g)],
+        lambda f, g: [one.scatter_vocab(f), two.over_outer(g)],
+        lambda f, g: [one.block, two.scatter_vocab(g)],
     ]
     widths = (split * width, depth - split * width)
-    calls = [(c, 0, rows) for c, (_, rows) in enumerate(chunks)]
-    if calls[-1][2] % (2 * TILE) == 0:
-        c, _, rows = calls.pop()
-        calls += [(c, 0, rows // 2), (c, rows // 2, rows // 2)]
     grad_head = None
-    for c, skip, rows in calls:
+    for c, (first, rows) in enumerate(chunks):
         grad_head, *flags = head_chunk(
-            ordered, all_grads[c], chunks[c][0], skip, rows, columns, grad_head, results, widths
+            ordered, all_grads[c], first, rows, columns, grad_head, results, widths
         )
         results = plan.pop(0)(*flags)
     while plan:
         results = plan.pop(0)(*flags)
-    grad_hidden = jnp.concatenate([one.total, two.join_vocab(None)], axis=1)
+    grad_hidden = gather_vocab([one.block, two.block], shard)
     return (token_kl.reshape(own_rows), grad_hidden, grad_head.T)
 
 

time: 218 us -> 211 us (0.968)
  other arithmetic: 13 us -> 4.82 us
  starting transfers between devices: 26.1 us -> 32.3 us
  local copies, waits for them, and re-layouts: 23.1 us -> 19.7 us
  waiting for transfers between devices: 29.1 us -> 26 us
    ppermute x24 -> x27, starting transfers between devices: 26.1 us -> 32.3 us  [swap(): return lax.ppermute(x, axis, [(i, i ^ k) for i in range(n)])]
    convert_element_type x4 -> x2, other arithmetic: 5.93 us -> 0.99 us  [scatter_vocab(): self.block = block.astype(BF16)]
    pallas_call x1, Pallas kernels: 16 us -> 19.2 us  [hidden_rest(): pl.pallas_call(functools.partial(hidden_rest_body, chunks, owners), grid=...]
    ppermute x24 -> x27, waiting for transfers between devices: 29.1 us -> 26 us  [swap(): return lax.ppermute(x, axis, [(i, i ^ k) for i in range(n)])]
    pallas_call x4 -> x3, Pallas kernels: 26.7 us -> 25.5 us  [head_chunk(): pl.pallas_call(functools.partial(head_body, len(grads), len(after)), grid...]
  transfers between devices with their start and end apart: 24 -> 27, of which waited for: 8 -> 9; matrix products, arithmetic and copies ran while one was open for 8% -> 5% of each run, Pallas kernels for 39% -> 47%
where the time goes in v4:
time: 211 us; the launch traced here: 210 us
  Pallas kernels  126 us (60%)
  starting transfers between devices  32.3 us (15%)
  waiting for transfers between devices  26 us (12%)
  local copies, waits for them, and re-layouts  19.7 us (9%)
  other arithmetic  4.82 us (2%)
    pallas_call x3, Pallas kernels, student_chunk(): pl.pallas_call(functools.partial(student_body, owners, places, len(after)...  36.4 us
    ppermute x27, starting transfers between devices, swap(): return lax.ppermute(x, axis, [(i, i ^ k) for i in range(n)])  32.3 us
    ppermute x27, waiting for transfers between devices, swap(): return lax.ppermute(x, axis, [(i, i ^ k) for i in range(n)])  26 us
    pallas_call x3, Pallas kernels, head_chunk(): pl.pallas_call(functools.partial(head_body, len(grads), len(after)), grid...  25.5 us
    pallas_call x3, Pallas kernels, hidden_chunk(): pl.pallas_call(functools.partial(hidden_body, len(grads), has_acc, last),...  23.1 us
    pallas_call x1, Pallas kernels, hidden_rest(): pl.pallas_call(functools.partial(hidden_rest_body, chunks, owners), grid=...  19.2 us
    unnamed x84, local copies, waits for them, and re-layouts  13 us
    pallas_call x3, Pallas kernels, totals_chunk(): pl.pallas_call(functools.partial(totals_body, len(parts), len(teachers),...  12.8 us
  transfers between devices with their start and end apart: 27, of which 9 were waited for; matrix products, arithmetic and copies ran while one was open for 5% of the time, Pallas kernels for 47%

profile of v4, /device:TPU:0, one launch (start us, length us, event | category | flops | bytes accessed | tf_op | source)
XLA Modules:
  0.0 209.9 jit_solution(14319852035374314107)
XLA Ops:
  0.6 3.0 %collective-permute-start.1 = (bf16[128,1792]{1,0:T(8,128)(2,1)}, bf16[128,1792]{1,0:T(8,128)(2,1)S(1)}, u32[]{:S(2)}, u32[]{:S(2)}) collective-permute-start(bf16[128,1792]{1,0:T(8,128)(2,1)} %refs_7_.1), channel_id=1, source_target_pairs={{0,16},{8,24},{16,0},{24,8},{1,17},{9,25},{17,1},{25,9},{2,18},{10... | collective-permute-start | bytes 1376264 | tf_op jit(solution)/shard_map/ppermute | solution.py:487
  5.2 9.2 %collective-permute-done.1.refs_9_ = bf16[128,1792]{1,0:T(8,128)(2,1)S(1)} collective-permute-done((bf16[128,1792]{1,0:T(8,128)(2,1)}, bf16[128,1792]{1,0:T(8,128)(2,1)S(1)}, u32[]{:S(2)}, u32[]{:S(2)}) %collective-permute-start.1) | collective-permute-done | bytes 458784 | tf_op jit(solution)/shard_map/ppermute | solution.py:487
  17.8 4.7 %dynamic-slice_bitcast_fusion = (bf16[3168,128]{1,0:T(8,128)(2,1)}, bf16[3168,128]{1,0:T(8,128)(2,1)}, bf16[3168,128]{1,0:T(8,128)(2,1)}, bf16[3168,128]{1,0:T(8...) fusion(bf16[256,9504]{0,1:T(8,128)(2,1)} %param.6, s32[]{:T(128)S(6)} %select_n.79, s32[]{:T(128)S(6)} %select_n.78), kind=kLoop, calls=%fused_computation.1 | loop fusion | bytes 9732104 | tf_op jit(solution)/shard_map/dynamic_slice | solution.py:587
  23.9 12.8 %student_chunk.3 = (f32[3168,256]{1,0:T(8,128)}, f32[3168,256]{1,0:T(8,128)}, bf16[512,1792]{1,0:T(8,128)(2,1)}, bf16[1792,512]{1,0:T(8,128)(2,1)}) custom-call(bf16[3168,128]{1,0:T(8,128)(2,1)} %get-tuple-element.53.refs_0_.refs_2_, bf16[3168,128]{1,0:T(8,128)(2,1)} %get-tuple-element.52.refs_1_.refs_3_, bf16[3168,128]{1,0:T(8,128)(2,1)} %get-tuple-element.51.refs_2_, ...), custom_call_target="tpu_custom_call" | custom-call | flops 363331584 | bytes 1229824 | tf_op jit(solution)/shard_map/student_chunk/pallas_call | solution.py:209
  36.8 11.8 %student_chunk.5 = (f32[3168,256]{1,0:T(8,128)}, f32[3168,256]{1,0:T(8,128)}) custom-call(bf16[1792,512]{1,0:T(8,128)(2,1)} %get-tuple-element.26.refs_0_, bf16[9504,1792]{1,0:T(8,128)(2,1)} %bitcast.29), custom_call_target="tpu_custom_call" | custom-call | flops 363331584 | bytes 1229824 | tf_op jit(solution)/shard_map/student_chunk/pallas_call | solution.py:209
  49.1 11.8 %student_chunk.4 = (f32[3168,256]{1,0:T(8,128)}, f32[3168,256]{1,0:T(8,128)}) custom-call(bf16[1792,512]{1,0:T(8,128)(2,1)} %get-tuple-element.26.refs_0_, bf16[9504,1792]{1,0:T(8,128)(2,1)} %bitcast.30), custom_call_target="tpu_custom_call" | custom-call | flops 363331584 | bytes 1229824 | tf_op jit(solution)/shard_map/student_chunk/pallas_call | solution.py:209
  65.1 5.2 %totals_chunk.3.refs_4_ = f32[40,256]{1,0:T(8,128)S(1)} custom-call(f32[3168,256]{1,0:T(8,128)S(1)} %copy-done.15, f32[3168,256]{1,0:T(8,128)} %collective-permute-done.6.refs_1_, bf16[3168,128]{1,0:T(8,128)(2,1)S(1)} %copy-done.27, bf16[3168,128]{1,0:T(8,128)(2,1)S(1)} %copy-done.25, f32[40,256]{1,0:T(8,128)S(1)} %copy-done.32), custom_call_target="tpu_custom_call" | custom-call | flops 608256 | bytes 506880 | tf_op jit(solution)/shard_map/totals_chunk/pallas_call | solution.py:147
  70.3 5.1 %totals_chunk.4.refs_4_ = f32[40,256]{1,0:T(8,128)S(1)} custom-call(f32[3168,256]{1,0:T(8,128)S(1)} %copy-done.18, f32[3168,256]{1,0:T(8,128)} %collective-permute-done.5.refs_1_, bf16[3168,128]{1,0:T(8,128)(2,1)S(1)} %copy-done.24, bf16[3168,128]{1,0:T(8,128)(2,1)S(1)} %copy-done.23, f32[40,256]{1,0:T(8,128)S(1)} %totals_chunk.3.refs_4_), custom_call_target="tpu_custom_call" | custom-call | flops 608256 | bytes 506880 | tf_op jit(solution)/shard_map/totals_chunk/pallas_call | solution.py:147
  78.7 3.1 %collective-permute-done.7.refs_1_ = f32[8,256]{1,0:T(8,128)S(1)} collective-permute-done((f32[8,256]{1,0:T(8,128)S(1)}, f32[8,256]{1,0:T(8,128)S(1)}, u32[]{:S(2)}, u32[]{:S(2)}) %collective-permute-start.7) | collective-permute-done | bytes 8224 | tf_op jit(solution)/shard_map/ppermute | solution.py:487
  82.7 2.8 %collective-permute-done.8.refs_1_ = f32[8,256]{1,0:T(8,128)S(1)} collective-permute-done((f32[8,256]{1,0:T(8,128)S(1)}, f32[8,256]{1,0:T(8,128)S(1)}, u32[]{:S(2)}, u32[]{:S(2)}) %collective-permute-start.8) | collective-permute-done | bytes 8224 | tf_op jit(solution)/shard_map/ppermute | solution.py:487
  89.3 2.7 %collective-permute-start.10 = (f32[8,256]{1,0:T(8,128)S(1)}, f32[8,256]{1,0:T(8,128)S(1)}, u32[]{:S(2)}, u32[]{:S(2)}) collective-permute-start(f32[8,256]{1,0:T(8,128)S(1)} %merge_totals.5.refs_0_), channel_id=1, source_target_pairs={{0,4},{2,6},{4,0},{6,2},{1,5},{3,7},{5,1},{7,3},{8,12},{10,14},{12... | collective-permute-start | bytes 24584 | tf_op jit(solution)/shard_map/ppermute | solution.py:487
  94.0 3.4 %logit_grads_chunk.5.refs_0_.refs_2_.refs_1_ = bf16[3168,256]{1,0:T(8,128)(2,1)S(1)} custom-call(f32[3168,256]{1,0:T(8,128)S(1)} %copy-done.16, f32[3168,256]{1,0:T(8,128)} %collective-permute-done.6.refs_1_, bf16[3168,128]{1,0:T(8,128)(2,1)S(1)} %copy-done.28, bf16[3168,128]{1,0:T(8,128)(2,1)S(1)} %copy-done.26, f32[8,256]{1,0:T(8,128)S(1)} %get-tuple-element.34.refs_4_), custom_call_target="tpu_custom_call" | custom-call | flops 405504 | bytes 608256 | tf_op jit(solution)/shard_map/logit_grads_chunk/pallas_call | solution.py:308
  97.5 4.0 %logit_grads_chunk.4.refs_0_.refs_3_ = bf16[3168,256]{1,0:T(8,128)(2,1)S(1)} custom-call(f32[3168,256]{1,0:T(8,128)S(1)} %copy-done.18, f32[3168,256]{1,0:T(8,128)} %collective-permute-done.5.refs_1_, bf16[3168,128]{1,0:T(8,128)(2,1)S(1)} %copy-done.24, bf16[3168,128]{1,0:T(8,128)(2,1)S(1)} %copy-done.23, f32[8,256]{1,0:T(8,128)S(1)} %get-tuple-element.34.refs_4_), custom_call_target="tpu_custom_call" | custom-call | flops 405504 | bytes 608256 | tf_op jit(solution)/shard_map/logit_grads_chunk/pallas_call | solution.py:308
  103.5 7.7 %grad_hidden_chunk.3.refs_3_ = f32[512,1024]{1,0:T(8,128)S(1)} custom-call(bf16[3168,256]{1,0:T(8,128)(2,1)S(1)} %logit_grads_chunk.5.refs_0_.refs_2_.refs_1_, bf16[3168,256]{1,0:T(8,128)(2,1)S(1)} %collective-permute-done.13.refs_1_.refs_3_.refs_2_, bf16[9504,1792]{1,0:T(8,128)(2,1)} %bitcast.31), custom_call_target="tpu_custom_call" | custom-call | flops 207618048 | bytes 608256 | tf_op jit(solution)/shard_map/grad_hidden_chunk/pallas_call | solution.py:371
  111.2 7.7 %grad_hidden_chunk.4.refs_3_ = f32[512,1024]{1,0:T(8,128)S(1)} custom-call(bf16[3168,256]{1,0:T(8,128)(2,1)S(1)} %logit_grads_chunk.4.refs_0_.refs_3_, bf16[3168,256]{1,0:T(8,128)(2,1)S(1)} %collective-permute-done.12.refs_1_.refs_4_, bf16[9504,1792]{1,0:T(8,128)(2,1)} %bitcast.32, f32[512,1024]{1,0:T(8,128)S(1)} %grad_hidden_chunk.3.refs_3_), custom_call_target="tpu_custom_call" | custom-call | flops 207618048 | bytes 608256 | tf_op jit(solution)/shard_map/grad_hidden_chunk/pallas_call | solution.py:371
  119.0 7.7 %grad_hidden_chunk.5 = (bf16[256,1024]{1,0:T(8,128)(2,1)S(1)}, bf16[256,1024]{1,0:T(8,128)(2,1)S(1)}, f32[8,128]{1,0:T(8,128)S(1)}) custom-call(bf16[3168,256]{1,0:T(8,128)(2,1)S(1)} %logit_grads_chunk.3.refs_0_.refs_5_.refs_3_, bf16[3168,256]{1,0:T(8,128)(2,1)S(1)} %collective-permute-done.11.refs_1_.refs_6_.refs_4_, bf16[9504,1792]{1,0:T(8,128)(2,1)} %bitcast.33, ...), custom_call_target="tpu_custom_call" | custom-call | flops 207618048 | bytes 608256 | tf_op jit(solution)/shard_map/grad_hidden_chunk/pallas_call | solution.py:371
  128.1 19.2 %grad_hidden_rest.1 = (bf16[256,768]{1,0:T(8,128)(2,1)}, bf16[256,768]{1,0:T(8,128)(2,1)}) custom-call(f32[8,128]{1,0:T(8,128)} %copy-done.33, bf16[3168,256]{1,0:T(8,128)(2,1)} %copy-done.4, bf16[3168,256]{1,0:T(8,128)(2,1)} %copy-done.13, bf16[3168,256]{1,0:T(8,128)(2,1)} %copy-done.2, bf16[3168,256]{1,0:T(8,128)(2,1)} %copy-done.11, ...), custom_call_target="tpu_custom_call" | custom-call | flops 467140608 | bytes 1520640 | tf_op jit(solution)/shard_map/grad_hidden_rest/pallas_call | solution.py:420
  150.0 8.5 %grad_head_chunk.3 = (bf16[9504,1792]{1,0:T(8,128)(2,1)}, f32[1,1024]{1,0:T(1,128)S(1)}, f32[1,768]{1,0:T(1,128)S(1)}) custom-call(f32[256,1024]{1,0:T(8,128)S(1)} %convert_add_fusion.refs_0_, bf16[512,1792]{1,0:T(8,128)(2,1)S(1)} %copy-done.6, bf16[3168,256]{1,0:T(8,128)(2,1)S(1)} %copy-done.5, bf16[3168,256]{1,0:T(8,128)(2,1)S(1)} %copy-done.14), custom_call_target="tpu_custom_call" | custom-call | flops 363331584 | bytes 1027072 | tf_op jit(solution)/shard_map/grad_head_chunk/pallas_call | solution.py:468
  165.6 2.6 %collective-permute-start.18 = (bf16[32,1024]{1,0:T(8,128)(2,1)}, bf16[32,1024]{1,0:T(8,128)(2,1)S(1)}, u32[]{:S(2)}, u32[]{:S(2)}) collective-permute-start(bf16[32,1024]{1,0:T(8,128)(2,1)} %get-tuple-element.57), channel_id=1, source_target_pairs={{0,4},{2,6},{4,0},{6,2},{1,5},{3,7},{5,1},{7,3},{8,12},{10,14},{12... | collective-permute-start | bytes 196616 | tf_op jit(solution)/shard_map/ppermute | solution.py:487
  171.3 8.5 %grad_head_chunk.4 = (bf16[9504,1792]{1,0:T(8,128)(2,1)}, f32[1,1024]{1,0:T(1,128)S(1)}, f32[1,768]{1,0:T(1,128)S(1)}) custom-call(f32[128,1024]{1,0:T(8,128)S(1)} %add_add_fusion.1.refs_0_, f32[256,768]{1,0:T(8,128)S(1)} %add_add_fusion.refs_1_, bf16[512,1792]{1,0:T(8,128)(2,1)S(1)} %copy-done.7, ...), custom_call_target="tpu_custom_call", output_to_operand_aliasing={{0}: (5, {})} | custom-call | flops 363331584 | bytes 1027072 | tf_op jit(solution)/shard_map/grad_head_chunk/pallas_call | solution.py:468
  181.8 3.5 %collective-permute-start.22 = (bf16[32,768]{1,0:T(8,128)(2,1)S(1)}, bf16[32,768]{1,0:T(8,128)(2,1)S(1)}, u32[]{:S(2)}, u32[]{:S(2)}) collective-permute-start(bf16[32,768]{1,0:T(8,128)(2,1)S(1)} %get-tuple-element.60), channel_id=1, source_target_pairs={{0,4},{2,6},{4,0},{6,2},{1,5},{3,7},{5,1},{7,3},{8,12},{10,14},{12... | collective-permute-start | bytes 147464 | tf_op jit(solution)/shard_map/ppermute | solution.py:487
  189.4 8.5 %grad_head_chunk.5 = (bf16[9504,1792]{1,0:T(8,128)(2,1)}, f32[1,1024]{1,0:T(1,128)}, f32[1,768]{1,0:T(1,128)S(1)}) custom-call(bf16[32,1024]{1,0:T(8,128)(2,1)S(1)} %add_convert_fusion.refs_0_, f32[128,768]{1,0:T(8,128)S(1)} %add_add_fusion.2.refs_1_, bf16[512,1792]{1,0:T(8,128)(2,1)S(1)} %copy-done.8, ...), custom_call_target="tpu_custom_call", output_to_operand_aliasing={{0}: (5, {})} | custom-call | flops 363331584 | bytes 1027072 | tf_op jit(solution)/shard_map/grad_head_chunk/pallas_call | solution.py:468
  198.4 3.8 %collective-permute-start.25 = (bf16[32,1792]{1,0:T(8,128)(2,1)S(1)}, bf16[32,1792]{1,0:T(8,128)(2,1)S(1)}, u32[]{:S(2)}, u32[]{:S(2)}) collective-permute-start(bf16[32,1792]{1,0:T(8,128)(2,1)S(1)} %pad_maximum_fusion), channel_id=1, source_target_pairs={{0,4},{2,6},{4,0},{6,2},{1,5},{3,7},{5,1},{7,3},{8,12},{10,14},{12... | collective-permute-start | bytes 344072 | tf_op jit(solution)/shard_map/ppermute | solution.py:487
  203.1 4.5 %collective-permute-done.25 = bf16[32,1792]{1,0:T(8,128)(2,1)S(1)} collective-permute-done((bf16[32,1792]{1,0:T(8,128)(2,1)S(1)}, bf16[32,1792]{1,0:T(8,128)(2,1)S(1)}, u32[]{:S(2)}, u32[]{:S(2)}) %collective-permute-start.25) | collective-permute-done | bytes 114720 | tf_op jit(solution)/shard_map/ppermute | solution.py:487
  (164 shorter events, 46.7 us)
Async XLA Ops:
  0.6 13.8 %collective-permute-start.1 = (bf16[128,1792]{1,0:T(8,128)(2,1)}, bf16[128,1792]{1,0:T(8,128)(2,1)S(1)}, u32[]{:S(2)}, u32[]{:S(2)}) collective-permute-start(bf16[128,1792]{1,0:T(8,128)(2,1)} %refs_7_.1), channel_id=1, source_target_pairs={{0,16},{8,24},{16,0},{24,8},{1,17},{9,25},{17,1},{25,9},{2,18},{10... | collective-permute-start | bytes 1376264 | tf_op jit(solution)/shard_map/ppermute | solution.py:487
  3.7 12.5 %collective-permute-start = (bf16[128,1792]{1,0:T(8,128)(2,1)}, bf16[128,1792]{1,0:T(8,128)(2,1)S(1)}, u32[]{:S(2)}, u32[]{:S(2)}) collective-permute-start(bf16[128,1792]{1,0:T(8,128)(2,1)} %refs_7_.1), channel_id=1, source_target_pairs={{0,8},{8,0},{16,24},{24,16},{1,9},{9,1},{17,25},{25,17},{2,10},{10... | collective-permute-start | bytes 1376264 | tf_op jit(solution)/shard_map/ppermute | solution.py:487
  14.4 8.1 %collective-permute-start.2 = (bf16[64,1792]{1,0:T(8,128)(2,1)S(1)}, bf16[64,1792]{1,0:T(8,128)(2,1)S(1)}, u32[]{:S(2)}, u32[]{:S(2)}) collective-permute-start(bf16[64,1792]{1,0:T(8,128)(2,1)S(1)} %slice.16), channel_id=1, source_target_pairs={{0,8},{8,0},{16,24},{24,16},{1,9},{9,1},{17,25},{25,17},{2,10},{10... | collective-permute-start | bytes 688136 | tf_op jit(solution)/shard_map/ppermute | solution.py:487
  16.2 6.3 %collective-permute-start.3 = (bf16[64,1792]{1,0:T(8,128)(2,1)S(1)}, bf16[64,1792]{1,0:T(8,128)(2,1)S(1)}, u32[]{:S(2)}, u32[]{:S(2)}) collective-permute-start(bf16[64,1792]{1,0:T(8,128)(2,1)S(1)} %slice.17), channel_id=1, source_target_pairs={{0,16},{8,24},{16,0},{24,8},{1,17},{9,25},{17,1},{25,9},{2,18},{10... | collective-permute-start | bytes 688136 | tf_op jit(solution)/shard_map/ppermute | solution.py:487
  36.8 24.1 %collective-permute-start.6 = (f32[3168,256]{1,0:T(8,128)}, f32[3168,256]{1,0:T(8,128)}, u32[]{:S(2)}, u32[]{:S(2)}) collective-permute-start(f32[3168,256]{1,0:T(8,128)} %get-tuple-element.32), channel_id=1, source_target_pairs={{0,1},{1,0},{2,3},{3,2},{4,5},{5,4},{6,7},{7,6},{8,9},{9,8},{10,11... | collective-permute-start | bytes 9732104 | tf_op jit(solution)/shard_map/ppermute | solution.py:487
  48.6 21.7 %collective-permute-start.5 = (f32[3168,256]{1,0:T(8,128)}, f32[3168,256]{1,0:T(8,128)}, u32[]{:S(2)}, u32[]{:S(2)}) collective-permute-start(f32[3168,256]{1,0:T(8,128)} %get-tuple-element.30), channel_id=1, source_target_pairs={{0,1},{1,0},{2,3},{3,2},{4,5},{5,4},{6,7},{7,6},{8,9},{9,8},{10,11... | collective-permute-start | bytes 9732104 | tf_op jit(solution)/shard_map/ppermute | solution.py:487
  60.8 14.6 %collective-permute-start.4 = (f32[3168,256]{1,0:T(8,128)}, f32[3168,256]{1,0:T(8,128)S(1)}, u32[]{:S(2)}, u32[]{:S(2)}) collective-permute-start(f32[3168,256]{1,0:T(8,128)} %get-tuple-element.28), channel_id=1, source_target_pairs={{0,1},{1,0},{2,3},{3,2},{4,5},{5,4},{6,7},{7,6},{8,9},{9,8},{10,11... | collective-permute-start | bytes 9732104 | tf_op jit(solution)/shard_map/ppermute | solution.py:487
  89.3 4.6 %collective-permute-start.10 = (f32[8,256]{1,0:T(8,128)S(1)}, f32[8,256]{1,0:T(8,128)S(1)}, u32[]{:S(2)}, u32[]{:S(2)}) collective-permute-start(f32[8,256]{1,0:T(8,128)S(1)} %merge_totals.5.refs_0_), channel_id=1, source_target_pairs={{0,4},{2,6},{4,0},{6,2},{1,5},{3,7},{5,1},{7,3},{8,12},{10,14},{12... | collective-permute-start | bytes 24584 | tf_op jit(solution)/shard_map/ppermute | solution.py:487
  97.4 6.1 %collective-permute-start.13 = (bf16[3168,256]{1,0:T(8,128)(2,1)S(1)}, bf16[3168,256]{1,0:T(8,128)(2,1)S(1)}, u32[]{:S(2)}, u32[]{:S(2)}) collective-permute-start(bf16[3168,256]{1,0:T(8,128)(2,1)S(1)} %logit_grads_chunk.5.refs_0_.refs_2_.refs_1_), channel_id=1, source_target_pairs={{0,1},{1,0},{2,3},{3,2},{4,5},{5,4},{6,7},{7,6},{8,9},{9,8},{10,11... | collective-permute-start | bytes 4866056 | tf_op jit(solution)/shard_map/ppermute | solution.py:487
  101.5 9.7 %collective-permute-start.12 = (bf16[3168,256]{1,0:T(8,128)(2,1)S(1)}, bf16[3168,256]{1,0:T(8,128)(2,1)S(1)}, u32[]{:S(2)}, u32[]{:S(2)}) collective-permute-start(bf16[3168,256]{1,0:T(8,128)(2,1)S(1)} %logit_grads_chunk.4.refs_0_.refs_3_), channel_id=1, source_target_pairs={{0,1},{1,0},{2,3},{3,2},{4,5},{5,4},{6,7},{7,6},{8,9},{9,8},{10,11... | collective-permute-start | bytes 4866056 | tf_op jit(solution)/shard_map/ppermute | solution.py:487
  102.9 16.0 %collective-permute-start.11 = (bf16[3168,256]{1,0:T(8,128)(2,1)S(1)}, bf16[3168,256]{1,0:T(8,128)(2,1)S(1)}, u32[]{:S(2)}, u32[]{:S(2)}) collective-permute-start(bf16[3168,256]{1,0:T(8,128)(2,1)S(1)} %logit_grads_chunk.3.refs_0_.refs_5_.refs_3_), channel_id=1, source_target_pairs={{0,1},{1,0},{2,3},{3,2},{4,5},{5,4},{6,7},{7,6},{8,9},{9,8},{10,11... | collective-permute-start | bytes 4866056 | tf_op jit(solution)/shard_map/ppermute | solution.py:487
  127.3 21.6 %collective-permute-start.14 = (bf16[256,1024]{1,0:T(8,128)(2,1)S(1)}, bf16[256,1024]{1,0:T(8,128)(2,1)S(1)}, u32[]{:S(2)}, u32[]{:S(2)}) collective-permute-start(bf16[256,1024]{1,0:T(8,128)(2,1)S(1)} %get-tuple-element.36), channel_id=1, source_target_pairs={{0,8},{8,0},{16,24},{24,16},{1,9},{9,1},{17,25},{25,17},{2,10},{10... | collective-permute-start | bytes 1572872 | tf_op jit(solution)/shard_map/ppermute | solution.py:487
  147.3 11.6 %collective-permute-start.17 = (bf16[256,768]{1,0:T(8,128)(2,1)}, bf16[256,768]{1,0:T(8,128)(2,1)}, u32[]{:S(2)}, u32[]{:S(2)}) collective-permute-start(bf16[256,768]{1,0:T(8,128)(2,1)} %get-tuple-element.41), channel_id=1, source_target_pairs={{0,8},{8,0},{16,24},{24,16},{1,9},{9,1},{17,25},{25,17},{2,10},{10... | collective-permute-start | bytes 1179656 | tf_op jit(solution)/shard_map/ppermute | solution.py:487
  149.1 13.0 %collective-permute-start.15 = (bf16[128,1024]{1,0:T(8,128)(2,1)S(1)}, bf16[128,1024]{1,0:T(8,128)(2,1)S(1)}, u32[]{:S(2)}, u32[]{:S(2)}) collective-permute-start(bf16[128,1024]{1,0:T(8,128)(2,1)S(1)} %dynamic-slice_convert_fusion), channel_id=1, source_target_pairs={{0,16},{8,24},{16,0},{24,8},{1,17},{9,25},{17,1},{25,9},{2,18},{10... | collective-permute-start | bytes 786440 | tf_op jit(solution)/shard_map/ppermute | solution.py:487
  160.9 19.0 %collective-permute-start.20 = (bf16[128,768]{1,0:T(8,128)(2,1)}, bf16[128,768]{1,0:T(8,128)(2,1)}, u32[]{:S(2)}, u32[]{:S(2)}) collective-permute-start(bf16[128,768]{1,0:T(8,128)(2,1)} %dynamic-slice_convert_fusion.1), channel_id=1, source_target_pairs={{0,16},{8,24},{16,0},{24,8},{1,17},{9,25},{17,1},{25,9},{2,18},{10... | collective-permute-start | bytes 589832 | tf_op jit(solution)/shard_map/ppermute | solution.py:487
  164.0 21.3 %collective-permute-start.16 = (bf16[32,1024]{1,0:T(8,128)(2,1)}, bf16[32,1024]{1,0:T(8,128)(2,1)S(1)}, u32[]{:S(2)}, u32[]{:S(2)}) collective-permute-start(bf16[32,1024]{1,0:T(8,128)(2,1)} %get-tuple-element.55), channel_id=1, source_target_pairs={{0,2},{2,0},{4,6},{6,4},{1,3},{3,1},{5,7},{7,5},{8,10},{10,8},{12,... | collective-permute-start | bytes 196616 | tf_op jit(solution)/shard_map/ppermute | solution.py:487
  165.6 19.9 %collective-permute-start.18 = (bf16[32,1024]{1,0:T(8,128)(2,1)}, bf16[32,1024]{1,0:T(8,128)(2,1)S(1)}, u32[]{:S(2)}, u32[]{:S(2)}) collective-permute-start(bf16[32,1024]{1,0:T(8,128)(2,1)} %get-tuple-element.57), channel_id=1, source_target_pairs={{0,4},{2,6},{4,0},{6,2},{1,5},{3,7},{5,1},{7,3},{8,12},{10,14},{12... | collective-permute-start | bytes 196616 | tf_op jit(solution)/shard_map/ppermute | solution.py:487
  168.2 17.3 %collective-permute-start.19 = (bf16[32,1024]{1,0:T(8,128)(2,1)S(1)}, bf16[32,1024]{1,0:T(8,128)(2,1)S(1)}, u32[]{:S(2)}, u32[]{:S(2)}) collective-permute-start(bf16[32,1024]{1,0:T(8,128)(2,1)S(1)} %get-tuple-element.56), channel_id=1, source_target_pairs={{0,6},{2,4},{4,2},{6,0},{1,7},{3,5},{5,3},{7,1},{8,14},{10,12},{12... | collective-permute-start | bytes 196616 | tf_op jit(solution)/shard_map/ppermute | solution.py:487
  181.0 16.9 %collective-permute-start.21 = (bf16[32,768]{1,0:T(8,128)(2,1)S(1)}, bf16[32,768]{1,0:T(8,128)(2,1)S(1)}, u32[]{:S(2)}, u32[]{:S(2)}) collective-permute-start(bf16[32,768]{1,0:T(8,128)(2,1)S(1)} %get-tuple-element.58), channel_id=1, source_target_pairs={{0,2},{2,0},{4,6},{6,4},{1,3},{3,1},{5,7},{7,5},{8,10},{10,8},{12,... | collective-permute-start | bytes 147464 | tf_op jit(solution)/shard_map/ppermute | solution.py:487
  181.8 16.1 %collective-permute-start.22 = (bf16[32,768]{1,0:T(8,128)(2,1)S(1)}, bf16[32,768]{1,0:T(8,128)(2,1)S(1)}, u32[]{:S(2)}, u32[]{:S(2)}) collective-permute-start(bf16[32,768]{1,0:T(8,128)(2,1)S(1)} %get-tuple-element.60), channel_id=1, source_target_pairs={{0,4},{2,6},{4,0},{6,2},{1,5},{3,7},{5,1},{7,3},{8,12},{10,14},{12... | collective-permute-start | bytes 147464 | tf_op jit(solution)/shard_map/ppermute | solution.py:487
  185.3 12.7 %collective-permute-start.23 = (bf16[32,768]{1,0:T(8,128)(2,1)S(1)}, bf16[32,768]{1,0:T(8,128)(2,1)S(1)}, u32[]{:S(2)}, u32[]{:S(2)}) collective-permute-start(bf16[32,768]{1,0:T(8,128)(2,1)S(1)} %get-tuple-element.59), channel_id=1, source_target_pairs={{0,6},{2,4},{4,2},{6,0},{1,7},{3,5},{5,3},{7,1},{8,14},{10,12},{12... | collective-permute-start | bytes 147464 | tf_op jit(solution)/shard_map/ppermute | solution.py:487
  198.0 5.0 %collective-permute-start.24 = (bf16[32,1792]{1,0:T(8,128)(2,1)S(1)}, bf16[32,1792]{1,0:T(8,128)(2,1)S(1)}, u32[]{:S(2)}, u32[]{:S(2)}) collective-permute-start(bf16[32,1792]{1,0:T(8,128)(2,1)S(1)} %pad_maximum_fusion), channel_id=1, source_target_pairs={{0,2},{2,0},{4,6},{6,4},{1,3},{3,1},{5,7},{7,5},{8,10},{10,8},{12,... | collective-permute-start | bytes 344072 | tf_op jit(solution)/shard_map/ppermute | solution.py:487
  198.4 9.2 %collective-permute-start.25 = (bf16[32,1792]{1,0:T(8,128)(2,1)S(1)}, bf16[32,1792]{1,0:T(8,128)(2,1)S(1)}, u32[]{:S(2)}, u32[]{:S(2)}) collective-permute-start(bf16[32,1792]{1,0:T(8,128)(2,1)S(1)} %pad_maximum_fusion), channel_id=1, source_target_pairs={{0,4},{2,6},{4,0},{6,2},{1,5},{3,7},{5,1},{7,3},{8,12},{10,14},{12... | collective-permute-start | bytes 344072 | tf_op jit(solution)/shard_map/ppermute | solution.py:487
  202.2 6.7 %collective-permute-start.26 = (bf16[32,1792]{1,0:T(8,128)(2,1)S(1)}, bf16[32,1792]{1,0:T(8,128)(2,1)S(1)}, u32[]{:S(2)}, u32[]{:S(2)}) collective-permute-start(bf16[32,1792]{1,0:T(8,128)(2,1)S(1)} %pad_maximum_fusion), channel_id=1, source_target_pairs={{0,6},{2,4},{4,2},{6,0},{1,7},{3,5},{5,3},{7,1},{8,14},{10,12},{12... | collective-permute-start | bytes 344072 | tf_op jit(solution)/shard_map/ppermute | solution.py:487
  (45 other events, 352.3 us)
